TPU v7x, 32 devices: a whole 2x2x4 slice. The times are simulated.
32 devices in a mesh: blk: 8 (over z, x), mp: 4 (over y, core).
Axes of the slice: x: 2, y: 2, z: 4, core: 2. Of those that a mesh axis runs over, the one named last changes fastest.
Arguments:
- hidden_in: bfloat16 [1024, 2048], P('blk'), may hold values from -6 to 6
- norm_gain: float32 [2048], replicated, may hold values from 0.25 to 1.75
- norm_bias: float32 [2048], replicated, may hold values from -3 to 3
- w_query: bfloat16 [2048, 2048], P(None, 'mp'), may hold values from -2 to 2
- w_key: bfloat16 [2048, 2048], P(None, 'mp'), may hold values from -0.125 to 0.125
- w_value: bfloat16 [2048, 2048], P(None, 'mp'), may hold values from -0.125 to 0.125
- w_out: bfloat16 [2048, 2048], P('mp'), may hold values from -0.125 to 0.125
- prefix_keys: bfloat16 [8, 128, 2048], P('blk', None, 'mp'), may hold values from -6 to 6
- prefix_values: bfloat16 [8, 128, 2048], P('blk', None, 'mp'), may hold values from -6 to 6
- segment: int32 [8, 128], P('blk'), may hold values from 0 to 3, never falling along the last dimension, each value on 1 to 64 neighbouring positions
- request_group: int32 [8, 4], P('blk'), may hold values from 0 to 3
- block_slot: int32 [8], P('blk'), may hold values from 0 to 7, each once
- block_live: int32 [8], P('blk'), may hold values 0 or 1
Outputs:
- hidden_out: bfloat16 [1024, 2048], P('blk')
Inputs may be any that keep to these rules, and one draw needn't show every extreme that they name: Each row of segment counts requests 0 to 3 without falling; each request has 1 to 64 tokens. `block_slot`: each slot once.
All inputs are finite; a program needn't handle non-finite values. No bound on the sum of `block_live` on one device may be relied on, other than what follows from the above.
Results may differ from a plain program's by a relative error of at most 0.009.
Values may be sent and summed in bfloat16 or wider, within the bound.
No kernel may reach another device: no remote copies, remote signals or barrier semaphores. Data moves between devices by JAX's collectives and lax.ppermute only.
A program may use at most 128 MiB of HBM per device.

v0:
```python
import jax
import jax.numpy as jnp
from jax import lax
from jax.sharding import PartitionSpec as P

HD = 128
GROUPS = 4


big = 1e30


def layer_norm(values, gain, bias):
    mean = jnp.mean(values, axis=-1, keepdims=True)
    centred = values - mean
    var = jnp.mean(centred * centred, axis=-1, keepdims=True)
    return centred * lax.rsqrt(var + 1e-05) * gain + bias


def absorb(carry, scores, mask, values):
    top, total, summed = carry
    masked = jnp.where(mask[None], scores, -big)
    new_top = jnp.maximum(top, jnp.max(masked, axis=2))
    weights = jnp.where(mask[None], jnp.exp(scores - new_top[..., None]), 0.0)
    factor = jnp.exp(top - new_top)
    total = total * factor + jnp.sum(weights, axis=2)
    part = jnp.einsum(
        "hqk,khd->hqd", weights.astype(jnp.bfloat16), values, preferred_element_type=jnp.float32
    )
    summed = summed * factor[..., None] + part
    return (new_top, total, summed)


def local(
    hidden_in,
    norm_gain,
    norm_bias,
    w_query,
    w_key,
    w_value,
    w_out,
    prefix_keys,
    prefix_values,
    segment,
    request_group,
    block_slot,
    block_live,
):
    rows = hidden_in.shape[0]
    local_width = w_query.shape[1]
    local_heads = local_width // HD
    cycle_size = lax.axis_size("blk")
    inputs = hidden_in.astype(jnp.float32)
    normed = layer_norm(inputs, norm_gain, norm_bias).astype(jnp.bfloat16)
    query = (
        jnp.dot(normed, w_query, preferred_element_type=jnp.float32) / jnp.sqrt(jnp.float32(HD))
    ).astype(jnp.bfloat16)
    key = jnp.dot(normed, w_key, preferred_element_type=jnp.float32).astype(jnp.bfloat16)
    value = jnp.dot(normed, w_value, preferred_element_type=jnp.float32).astype(jnp.bfloat16)
    q_heads = query.reshape(rows, local_heads, HD)
    seg_row = segment[0]
    groups_row = request_group[0]
    token_group = jnp.sum(
        jnp.where(
            seg_row[:, None] == jnp.arange(groups_row.shape[0])[None, :], groups_row[None, :], 0
        ),
        axis=1,
    )
    places = jnp.arange(rows)
    start_carry = (
        jnp.full((local_heads, rows), -big, jnp.float32),
        jnp.zeros((local_heads, rows), jnp.float32),
        jnp.zeros((local_heads, rows, HD), jnp.float32),
    )
    scores = jnp.einsum(
        "qhd,khd->hqk",
        q_heads,
        key.reshape(rows, local_heads, HD),
        preferred_element_type=jnp.float32,
    )
    mask = (seg_row[:, None] == seg_row[None, :]) & (places[None, :] <= places[:, None])
    first_carry = absorb(start_carry, scores, mask, value.reshape(rows, local_heads, HD))
    keys = lax.all_gather(prefix_keys, "blk", axis=0, tiled=True)
    values = lax.all_gather(prefix_values, "blk", axis=0, tiled=True)
    slots = lax.all_gather(block_slot, "blk", axis=0, tiled=True)
    lives = lax.all_gather(block_live, "blk", axis=0, tiled=True)
    blocks_here = keys.shape[0]
    block_width = keys.shape[1]
    merged = 4
    turns = blocks_here // merged
    tags = jnp.repeat(jnp.where(lives == 1, slots * GROUPS // cycle_size, -1), block_width)
    key_steps = keys.reshape(turns, merged * block_width, local_heads, HD)
    value_steps = values.reshape(turns, merged * block_width, local_heads, HD)
    tag_steps = tags.reshape(turns, merged * block_width)

    def one_turn(state, item):
        turn_keys, turn_values, turn_tags = item
        scores = jnp.einsum("qhd,khd->hqk", q_heads, turn_keys, preferred_element_type=jnp.float32)
        mask = token_group[:, None] == turn_tags[None, :]
        return (absorb(state, scores, mask, turn_values), None)

    result, _ = lax.scan(one_turn, first_carry, (key_steps, value_steps, tag_steps))
    top, total, summed = result
    attended = (summed / total[..., None]).astype(jnp.bfloat16)
    attended = jnp.transpose(attended, (1, 0, 2)).reshape(rows, local_width)
    branch = jnp.dot(attended, w_out, preferred_element_type=jnp.float32)
    summed_branch = lax.psum(branch.astype(jnp.bfloat16), "mp").astype(jnp.float32)
    return (inputs + summed_branch).astype(jnp.bfloat16)


def solution(mesh):
    return jax.shard_map(
        local,
        mesh=mesh,
        in_specs=(
            P("blk", None),
            P(),
            P(),
            P(None, "mp"),
            P(None, "mp"),
            P(None, "mp"),
            P("mp", None),
            P("blk", None, "mp"),
            P("blk", None, "mp"),
            P("blk", None),
            P("blk", None),
            P("blk"),
            P("blk"),
        ),
        out_specs=P("blk", None),
        check_vma=False,
    )
```

profile of v0, /device:TPU:0, one launch (start us, length us, event | category | flops | bytes accessed | tf_op | source)
XLA Modules:
  0.0 143.2 jit_solution(4447402115552608499)
XLA Ops:
  6.5 0.0 copy-start
  6.5 0.0 all-gather.3.cloned.1.call-start
  6.5 0.7 all-gather.3.cloned.1.call-update
  7.3 0.0 all-gather.5.cloned.1.call-start
  7.3 0.7 all-gather.5.cloned.1.call-update
  8.0 0.0 all-reduce.5.cloned.1.call-start
  9.4 1.2 convert_reduce_fusion
  10.5 0.0 copy-start.3
  10.6 0.0 copy-start.8
  10.6 0.0 copy-start.1
  10.6 0.0 copy-start.6
  10.6 0.0 copy-start.7
  10.6 1.4 fusion.13
  12.0 1.3 dynamic-slice
  13.3 0.7 dynamic-update-slice
  14.0 0.7 dynamic-update-slice.1
  14.7 13.2 %all-reduce.2 = (s32[8]{0:T(128)S(1)}, s32[8]{0:T(128)S(1)}) all-reduce(s32[8]{0:T(128)S(1)} %dynamic-update-slice, s32[8]{0:T(128)S(1)} %dynamic-update-slice.1), channel_id=1, replica_groups=mesh['blk'=8,'mp'=4] {'blk'}, use_global_device_ids=true, to_apply=%add | all-reduce | flops 16 | bytes 128
  28.0 0.1 broadcast_in_dim.92
  28.0 0.0 copy-start.4
  28.0 0.1 broadcast_bitcast_fusion
  28.1 2.4 %fusion.12 = bf16[16,4,8,128]{3,2,1,0:T(8,128)(2,1)S(1)} fusion(bf16[2048,512]{1,0:T(8,128)(2,1)} %param.18, bf16[128,2048]{1,0:T(8,128)(2,1)} %param.15, f32[2048]{0:T(1024)} %param.17, f32[2048]{0:T(1024)} %param.16, f32[128]{0:T(128)S(1)} %add_rsqrt_fusion, f32[128]{0:T(128)S(1)} %broadcast_multiply_fusion), kind=kOutput, calls=%fused_computation.31 | convolution fusion | flops 270139392 | bytes 2769920 | tf_op jit(solution)/shard_map/dot_general | solution.py:56
  30.5 0.0 copy-done.3
  30.6 0.0 copy-done.8
  30.6 0.1 select_reduce_fusion.2
  30.7 0.0 copy-start.5
  30.7 0.1 fusion.29
  30.8 0.0 copy-done.1
  30.8 0.0 copy-done.6
  30.8 0.0 copy-done.7
  30.8 0.0 copy-done.4
  30.8 0.5 fusion.10
  31.3 0.2 select_reduce_fusion.1
  31.6 0.1 fusion.19
  31.6 0.6 copy-done.5
  32.3 0.5 fusion.11
  32.8 0.2 convolution_add_fusion.1
  33.0 19.5 %all-gather.3.cloned.1.call-done = bf16[8,128,512]{2,1,0:T(8,128)(2,1)} async-done(((bf16[1,128,512]{2,1,0:T(8,128)(2,1)}), bf16[8,128,512]{2,1,0:T(8,128)(2,1)}) %all-gather.3.cloned.1.call-update) | async-done | bytes 1048592 | tf_op jit(solution)/shard_map/all_gather | solution.py:83
  52.5 1.3 reshape.118
  53.8 39.7 %all-gather.5.cloned.1.call-done = bf16[8,128,512]{2,1,0:T(8,128)(2,1)} async-done(((bf16[1,128,512]{2,1,0:T(8,128)(2,1)}), bf16[8,128,512]{2,1,0:T(8,128)(2,1)}) %all-gather.5.cloned.1.call-update) | async-done | bytes 1048592 | tf_op jit(solution)/shard_map/all_gather | solution.py:84
  93.6 2.2 %reshape.119 = bf16[2,512,4,128]{3,2,1,0:T(4,128)(2,1)} reshape(bf16[8,128,512]{2,1,0:T(8,128)(2,1)} %all-gather.5.cloned.1.call-done) | data formatting | bytes 2097152 | tf_op jit(solution)/shard_map/reshape | solution.py:93
  95.8 5.3 %while.14 = (s32[]{:T(128)}, f32[4,128]{1,0:T(4,128)S(1)}, f32[4,128]{1,0:T(4,128)S(1)}, f32[4,128,128]{2,1,0:T(8,128)S(1)}, s32[128]{0:T(128)S(1)}, /*index=5*/...) while((s32[]{:T(128)}, f32[4,128]{1,0:T(4,128)S(1)}, ...), condition=%wide.region_8.9_spmd, body=%wide.region_5.8_spmd.sunk | while | flops 136512512 | bytes 7248501 | solution.py:102
  95.8 0.1 broadcast_compare_fusion.2
  95.9 1.4 constant_dynamic-slice_fusion.6
  97.3 0.3 select_reduce_fusion.4
  97.7 0.2 fusion.46
  97.9 0.5 convolution_add_fusion.3
  98.4 0.1 broadcast_compare_fusion.2
  98.6 1.4 constant_dynamic-slice_fusion.6
  100.0 0.3 select_reduce_fusion.4
  100.3 0.2 fusion.46
  100.6 0.5 convolution_add_fusion.3
  101.1 0.0 copy-start.2
  101.1 0.1 copy.46
  101.3 0.0 copy-done
  101.3 1.3 convolution_convert_fusion
  102.5 0.0 all-reduce.5.cloned.1.call-update
  102.6 32.1 %all-reduce.5.cloned.1.call-done = bf16[128,2048]{1,0:T(8,128)(2,1)} async-done(((bf16[128,2048]{1,0:T(8,128)(2,1)}), bf16[128,2048]{1,0:T(8,128)(2,1)}) %all-reduce.5.cloned.1.call-update) | async-done | bytes 524304 | tf_op jit(solution)/shard_map/psum | solution.py:107
  134.7 0.0 copy-done.2
  134.7 2.0 %fusion.17 = bf16[128,2048]{1,0:T(8,128)(2,1)} fusion(bf16[128,2048]{1,0:T(8,128)(2,1)S(1)} %copy-done.2, bf16[128,2048]{1,0:T(8,128)(2,1)} %all-reduce.5.cloned.1.call-done), kind=kLoop, calls=%fused_computation.36 | loop fusion | flops 1048576 | bytes 1572864 | tf_op jit(solution)/shard_map/convert_element_type | solution.py:108
  (18 shorter events, 0.2 us)
Async XLA Ops:
  6.5 94.7 %copy-start = (bf16[512,2048]{1,0:T(8,128)(2,1)S(1)}, bf16[512,2048]{1,0:T(8,128)(2,1)}, u32[]{:S(2)}) copy-start(bf16[512,2048]{1,0:T(8,128)(2,1)} %param.21) | copy-start | bytes 6291460
  6.5 46.0 %all-gather.3.cloned.1.call-start = ((), (), s32[]{:S(2)}) async-start(), calls=%async_computation | async-start | bytes 1179648 | tf_op jit(solution)/shard_map/all_gather | solution.py:83
  7.3 86.3 %all-gather.5.cloned.1.call-start = ((), (), s32[]{:S(2)}) async-start(), calls=%async_computation.1 | async-start | bytes 1179648 | tf_op jit(solution)/shard_map/all_gather | solution.py:84
  8.0 126.7 %all-reduce.5.cloned.1.call-start = ((), (), s32[]{:S(2)}) async-start(), calls=%async_computation.2 | async-start | bytes 1048576 | tf_op jit(solution)/shard_map/psum | solution.py:107
  10.5 20.0 %copy-start.3 = (s32[1,128]{1,0:T(1,128)S(1)}, s32[1,128]{1,0:T(1,128)}, u32[]{:S(2)}) copy-start(s32[1,128]{1,0:T(1,128)} %param.24) | copy-start | bytes 1540
  10.6 20.0 %copy-start.8 = (s32[1,4]{1,0:T(1,128)S(1)}, s32[1,4]{1,0:T(1,128)}, u32[]{:S(2)}) copy-start(s32[1,4]{1,0:T(1,128)} %param.25) | copy-start | bytes 52
  10.6 20.2 %copy-start.1 = (bf16[128,2048]{1,0:T(8,128)(2,1)S(1)}, bf16[128,2048]{1,0:T(8,128)(2,1)}, u32[]{:S(2)}) copy-start(bf16[128,2048]{1,0:T(8,128)(2,1)} %param.15) | copy-start | bytes 1572868
  10.6 20.2 %copy-start.6 = (f32[2048]{0:T(1024)S(1)}, f32[2048]{0:T(1024)}, u32[]{:S(2)}) copy-start(f32[2048]{0:T(1024)} %param.17) | copy-start | bytes 24580
  10.6 20.2 %copy-start.7 = (f32[2048]{0:T(1024)S(1)}, f32[2048]{0:T(1024)}, u32[]{:S(2)}) copy-start(f32[2048]{0:T(1024)} %param.16) | copy-start | bytes 24580
  28.0 2.8 %copy-start.4 = (bf16[2048,512]{1,0:T(8,128)(2,1)S(1)}, bf16[2048,512]{1,0:T(8,128)(2,1)}, u32[]{:S(2)}) copy-start(bf16[2048,512]{1,0:T(8,128)(2,1)} %param.19) | copy-start | bytes 6291460
  30.7 1.6 %copy-start.5 = (bf16[2048,512]{1,0:T(8,128)(2,1)S(1)}, bf16[2048,512]{1,0:T(8,128)(2,1)}, u32[]{:S(2)}) copy-start(bf16[2048,512]{1,0:T(8,128)(2,1)} %param.20) | copy-start | bytes 6291460
  101.1 33.6 %copy-start.2 = (bf16[128,2048]{1,0:T(8,128)(2,1)S(1)}, bf16[128,2048]{1,0:T(8,128)(2,1)}, u32[]{:S(2)}) copy-start(bf16[128,2048]{1,0:T(8,128)(2,1)} %param.15) | copy-start | bytes 1572868
Sparse Core Ops, SparseCore 0:
  9.5 42.9 all-gather.2
  54.6 38.9 all-gather.4
  102.7 31.9 all-reduce.4
where the time goes:
time: 144 us; the launch traced here: 143 us
  waiting for transfers between devices  92.7 us (64%)
  between operations  14.6 us (10%)
  blocking collectives  13.2 us (9%)
  local copies, waits for them, and re-layouts  10.1 us (7%)
  matrix products  6.81 us (5%)
  other arithmetic  5.58 us (4%)
    all_gather x1, waiting for transfers between devices, local(): values = lax.all_gather(prefix_values, 'blk', axis=0, tiled=True)  39.7 us
    psum x1, waiting for transfers between devices, local(): lax.psum(branch.astype(jnp.bfloat16), 'mp').astype(jnp.float32)  32.1 us
    all_gather x1, waiting for transfers between devices, local(): keys = lax.all_gather(prefix_keys, 'blk', axis=0, tiled=True)  19.5 us
    unnamed x1, blocking collectives  13.2 us
    unnamed x25, local copies, waits for them, and re-layouts  3.45 us
  transfers between devices with their start and end apart: 3, of which 3 were waited for; matrix products, arithmetic and copies ran while one was open for 8% of the time, Pallas kernels for 0%

commit v1 on v0

v1 whole, which is shorter than its diff:
```python
import functools

import jax
import jax.numpy as jnp
from jax import lax
from jax.experimental import pallas as pl
from jax.experimental.pallas import tpu as pltpu
from jax.sharding import PartitionSpec as P

HD = 128
GROUPS = 4
TAG_ROWS = 16

big = 1e30

VMEM = pl.BlockSpec(memory_space=pltpu.VMEM)
SMEM = pl.BlockSpec(memory_space=pltpu.SMEM)
NT = (((1,), (1,)), ((), ()))
TN = (((0,), (0,)), ((), ()))


def dot(a, b, dims=(((1,), (0,)), ((), ()))):
    return lax.dot_general(a, b, dims, preferred_element_type=jnp.float32)


def head_at(part, shift, heads):
    return lax.rem(part + shift, heads) * HD


def pack_kernel(blocks, heads, part_ref, slot_ref, live_ref, keys_ref, values_ref, *outs):
    rows = keys_ref.shape[1]
    group = lax.div(slot_ref[0] * GROUPS, blocks)
    tag = jnp.where(live_ref[0] == 1, group, -1).astype(jnp.float32)
    tag_rows = jnp.full((TAG_ROWS, HD), tag, jnp.float32).astype(jnp.bfloat16)
    for k in range(heads):
        at = pl.ds(pl.multiple_of(head_at(part_ref[0], k, heads), HD), HD)
        outs[k][0:rows, :] = keys_ref[0, :, at]
        outs[k][rows : 2 * rows, :] = values_ref[0, :, at]
        outs[k][2 * rows : 2 * rows + TAG_ROWS, :] = tag_rows


def query_kernel(
    heads,
    part_ref,
    request_group_ref,
    hidden_ref,
    gain_ref,
    bias_ref,
    w_query_ref,
    segment_ref,
    normed_ref,
    query_ref,
    *outs,
):
    rows = hidden_ref.shape[0]
    inputs = hidden_ref[...].astype(jnp.float32)
    mean = jnp.mean(inputs, axis=-1, keepdims=True)
    centred = inputs - mean
    var = jnp.mean(centred * centred, axis=-1, keepdims=True)
    normed = centred * lax.rsqrt(var + 1e-05) * gain_ref[...] + bias_ref[...]
    normed = normed.astype(jnp.bfloat16)
    normed_ref[...] = normed
    query = dot(normed, w_query_ref[...]) * (HD**-0.5)
    query_ref[...] = query.astype(jnp.bfloat16)
    segment = segment_ref[...]
    group = jnp.zeros_like(segment)
    for r in range(request_group_ref.shape[1]):
        group = jnp.where(segment == r, request_group_ref[0, r], group)
    group_rows = jnp.broadcast_to(group.astype(jnp.float32), (TAG_ROWS, rows))
    for k in range(heads):
        at = pl.ds(pl.multiple_of(head_at(part_ref[0], k, heads), HD), HD)
        outs[k][0:rows, :] = query_ref[:, at]
        outs[k][rows : rows + TAG_ROWS, :] = group_rows.astype(jnp.bfloat16)


def suffix_kernel(
    heads, normed_ref, query_ref, w_key_ref, w_value_ref, segment_ref, sum_ref, log_ref
):
    rows = normed_ref.shape[0]
    key = dot(normed_ref[...], w_key_ref[...]).astype(jnp.bfloat16)
    value = dot(normed_ref[...], w_value_ref[...]).astype(jnp.bfloat16)
    by_token = jnp.broadcast_to(segment_ref[...], (rows, rows))
    key_place = lax.broadcasted_iota(jnp.int32, (rows, rows), 0)
    token_place = lax.broadcasted_iota(jnp.int32, (rows, rows), 1)
    by_key = jnp.sum(
        jnp.where(key_place == token_place, by_token, 0).astype(jnp.float32), axis=1, keepdims=True
    )
    mask = (by_key == by_token.astype(jnp.float32)) & (key_place <= token_place)
    for h in range(heads):
        cols = slice(h * HD, (h + 1) * HD)
        scores = jnp.where(mask, dot(key[:, cols], query_ref[:, cols], NT), -big)
        top = jnp.max(scores, axis=0, keepdims=True)
        weights = jnp.exp(scores - top)
        total = jnp.sum(weights, axis=0, keepdims=True)
        summed = dot(value[:, cols], weights.astype(jnp.bfloat16), TN)
        sum_ref[cols, :] = summed / total
        log_ref[h : h + 1, :] = top + jnp.log(total)


def prefix_kernel(n_queries, n_blocks, rows, *refs):
    queries = refs[:n_queries]
    blocks = refs[n_queries : n_queries + n_blocks]
    outs = refs[n_queries + n_blocks : 2 * n_queries + n_blocks]
    query = jnp.concatenate([ref[0:rows, :] for ref in queries], axis=0)
    group = jnp.concatenate(
        [ref[rows : rows + TAG_ROWS, :].astype(jnp.float32)[0:1, :] for ref in queries], axis=1
    )
    tokens = query.shape[0]
    key_rows = (HD, 2 * HD + TAG_ROWS)
    step = key_rows[1]

    def score(ref, at):
        keys = ref[pl.ds(at, HD), :]
        tag = ref[pl.ds(at + 2 * HD, TAG_ROWS), :].astype(jnp.float32)[0:1, 0:1]
        scores = dot(keys, query, NT)
        return scores, group == tag

    def absorb(carry, found):
        top, total, summed = carry
        new_top = top
        for scores, mask, _ in found:
            best = jnp.max(scores, axis=0, keepdims=True)
            new_top = jnp.maximum(new_top, jnp.where(mask, best, -big))
        factor = jnp.exp(top - new_top)
        total, summed = total * factor, summed * factor
        for scores, mask, values in found:
            weights = jnp.exp(scores - jnp.where(mask, new_top, big))
            total = total + jnp.sum(weights, axis=0, keepdims=True)
            summed = summed + dot(values, weights.astype(jnp.bfloat16), TN)
        return new_top, total, summed

    def one(ref, at):
        scores, mask = score(ref, at)
        return scores, mask, ref[pl.ds(at + HD, HD), :]

    carry = (
        jnp.full((1, tokens), -big, jnp.float32),
        jnp.zeros((1, tokens), jnp.float32),
        jnp.zeros((HD, tokens), jnp.float32),
    )
    carry = absorb(carry, [one(ref, 0) for ref in blocks if ref.shape[0] == step])
    for ref in blocks:
        held = ref.shape[0] // step
        if held > 1:

            def body(i, state, ref=ref):
                return absorb(state, [one(ref, pl.multiple_of(i * step, TAG_ROWS))])

            carry = lax.fori_loop(0, held, body, carry)
    top, total, summed = carry
    found = total > 0.0
    summed = summed * jnp.where(found, 1.0 / jnp.where(found, total, 1.0), 0.0)
    log = jnp.where(found, top + jnp.log(jnp.where(found, total, 1.0)), -big)
    first = log.astype(jnp.bfloat16).astype(jnp.float32)
    second = (log - first).astype(jnp.bfloat16).astype(jnp.float32)
    third = log - first - second
    place = lax.broadcasted_iota(jnp.int32, (TAG_ROWS, tokens), 0)
    logs = jnp.where(place == 0, first, jnp.where(place == 1, second, jnp.where(place == 2, third, 0.0)))
    for k in range(n_queries):
        cols = slice(k * rows, (k + 1) * rows)
        outs[k][0:HD, :] = summed[:, cols].astype(jnp.bfloat16)
        outs[k][HD : HD + TAG_ROWS, :] = logs[:, cols].astype(jnp.bfloat16)


def project_kernel(heads, part_ref, half_ref, sum_ref, log_ref, w_out_ref, *refs):
    backs = refs[:heads]
    keep_ref, send_ref, attended, branch = refs[heads:]
    for k in range(heads):
        at = pl.multiple_of(head_at(part_ref[0], k, heads), HD)
        logs = backs[k][HD : HD + TAG_ROWS, :].astype(jnp.float32)
        prefix_log = logs[0:1, :] + logs[1:2, :] + logs[2:3, :]
        suffix_log = log_ref[pl.ds(lax.rem(part_ref[0] + k, heads), 1), :]
        top = jnp.maximum(prefix_log, suffix_log)
        prefix_part = jnp.exp(prefix_log - top)
        suffix_part = jnp.exp(suffix_log - top)
        whole = prefix_part + suffix_part
        joined = (
            backs[k][0:HD, :].astype(jnp.float32) * (prefix_part / whole)
            + sum_ref[pl.ds(at, HD), :] * (suffix_part / whole)
        )
        attended[pl.ds(at, HD), :] = joined.astype(jnp.bfloat16)
    branch[...] = dot(attended[...], w_out_ref[...], TN)
    half = keep_ref.shape[0]
    mine = pl.multiple_of(half_ref[0] * half, half)
    other = pl.multiple_of((1 - half_ref[0]) * half, half)
    keep_ref[...] = branch[pl.ds(mine, half), :]
    send_ref[...] = branch[pl.ds(other, half), :].astype(jnp.bfloat16)


def call(kernel, outs, specs, scratch=()):
    return pl.pallas_call(
        kernel,
        out_shape=tuple(jax.ShapeDtypeStruct(s, t) for s, t in outs),
        in_specs=specs,
        out_specs=(VMEM,) * len(outs),
        scratch_shapes=scratch,
        compiler_params=pltpu.CompilerParams(vmem_limit_bytes=40 * 1024 * 1024),
    )


def local(
    hidden_in,
    norm_gain,
    norm_bias,
    w_query,
    w_key,
    w_value,
    w_out,
    prefix_keys,
    prefix_values,
    segment,
    request_group,
    block_slot,
    block_live,
):
    bf16, f32 = jnp.bfloat16, jnp.float32
    rows, width = hidden_in.shape
    local_width = w_query.shape[1]
    heads = local_width // HD
    n_blk = lax.axis_size("blk")
    n_mp = lax.axis_size("mp")
    rest = n_blk // heads
    me = lax.axis_index("blk")
    part = (me // rest).astype(jnp.int32).reshape(1)
    half = lax.rem(lax.axis_index("mp"), 2).astype(jnp.int32).reshape(1)

    def along_part(x, shift):
        if shift % heads == 0:
            return x
        pairs = [(i, (i // rest + shift) % heads * rest + i % rest) for i in range(n_blk)]
        return lax.ppermute(x, "blk", pairs)

    def across(x, bit):
        return lax.ppermute(x, "blk", [(i, i ^ bit) for i in range(n_blk)])

    def across_mp(x, bit):
        return lax.ppermute(x, "mp", [(i, i ^ bit) for i in range(n_mp)])

    block = 2 * HD + TAG_ROWS
    packs = call(
        functools.partial(pack_kernel, n_blk, heads),
        [((block, HD), bf16)] * heads,
        (SMEM,) * 3 + (VMEM,) * 2,
    )(part, block_slot, block_live, prefix_keys, prefix_values)
    blocks = [along_part(packs[k], k) for k in range(heads)]

    normed, query, *asks = call(
        functools.partial(query_kernel, heads),
        [((rows, width), bf16), ((rows, local_width), bf16)] + [((rows + TAG_ROWS, HD), bf16)] * heads,
        (SMEM,) * 2 + (VMEM,) * 5,
    )(
        part,
        request_group,
        hidden_in,
        norm_gain.reshape(1, width),
        norm_bias.reshape(1, width),
        w_query,
        segment,
    )
    asks = [along_part(asks[k], k) for k in range(heads)]

    bit = 1
    while bit < rest:
        sends = blocks if bit == 1 else [jnp.concatenate(blocks, axis=0)]
        blocks = blocks + [across(x, bit) for x in sends]
        bit *= 2

    suffix_sum, suffix_log = call(
        functools.partial(suffix_kernel, heads),
        [((local_width, rows), f32), ((max(heads, 8), rows), f32)],
        (VMEM,) * 5,
    )(normed, query, w_key, w_value, segment)

    backs = call(
        functools.partial(prefix_kernel, heads, len(blocks), rows),
        [((HD + TAG_ROWS, rows), bf16)] * heads,
        (VMEM,) * (heads + len(blocks)),
    )(*asks, *blocks)
    backs = [along_part(backs[k], -k) for k in range(heads)]

    keep, send = call(
        functools.partial(project_kernel, heads),
        [((rows // 2, width), f32), ((rows // 2, width), bf16)],
        (SMEM,) * 2 + (VMEM,) * (3 + heads),
        scratch=[pltpu.VMEM((local_width, rows), bf16), pltpu.VMEM((rows, width), f32)],
    )(part, half, suffix_sum, suffix_log, w_out, *backs)

    mine = (keep + across_mp(send, 1).astype(f32)).astype(bf16)
    bit = 2
    while bit < n_mp:
        mine = (mine.astype(f32) + across_mp(mine, bit).astype(f32)).astype(bf16 if 2 * bit < n_mp else f32)
        bit *= 2
    inputs = lax.dynamic_slice_in_dim(hidden_in, half[0] * (rows // 2), rows // 2, 0)
    done = (inputs.astype(f32) + mine.astype(f32)).astype(bf16)
    other = across_mp(done, 1)
    first = half[0] == 0
    return jnp.concatenate([jnp.where(first, done, other), jnp.where(first, other, done)], axis=0)


def solution(mesh):
    return jax.shard_map(
        local,
        mesh=mesh,
        in_specs=(
            P("blk", None),
            P(),
            P(),
            P(None, "mp"),
            P(None, "mp"),
            P(None, "mp"),
            P("mp", None),
            P("blk", None, "mp"),
            P("blk", None, "mp"),
            P("blk", None),
            P("blk", None),
            P("blk"),
            P("blk"),
        ),
        out_specs=P("blk", None),
        check_vma=False,
    )
```

time: 144 us -> 53.5 us (0.37)
  waiting for transfers between devices: 92.7 us -> 20.9 us
  starting transfers between devices: 0.08 us -> 16.3 us
  blocking collectives: 13.2 us -> 0 us
  between operations: 14.6 us -> 1.58 us
  matrix products: 6.81 us -> 0 us
  other arithmetic: 5.58 us -> 1.03 us
  Pallas kernels: 0 us -> 4.51 us
    all_gather x2 -> x0, waiting for transfers between devices: 59.2 us -> none  [the longest x1 39.7 us: local(): values = lax.all_gather(prefix_values, 'blk', axis=0, tiled=True)]
    psum x1 -> x0, waiting for transfers between devices: 32.1 us -> none  [local(): lax.psum(branch.astype(jnp.bfloat16), 'mp').astype(jnp.float32)]
    ppermute x0 -> x16, waiting for transfers between devices: none -> 20.9 us  [the longest x9 11.1 us: along_part(): return lax.ppermute(x, 'blk', pairs)]
    ppermute x0 -> x16, starting transfers between devices: none -> 16.3 us  [the longest x9 10.5 us: along_part(): return lax.ppermute(x, 'blk', pairs)]
    unnamed x1 -> x0, blocking collectives: 13.2 us -> none
    dot_general x10 -> x0, matrix products: 6.81 us -> none  [the longest x1 2.42 us: local(): jnp.dot(normed, w_query, preferred_element_type=jnp.float32)]
    unnamed x25 -> x26, local copies, waits for them, and re-layouts: 3.45 us -> 8.74 us
    pallas_call x0 -> x5, Pallas kernels: none -> 4.51 us  [the longest x1 1.33 us: local(): call(functools.partial(suffix_kernel, heads), [((local_width, rows), f32)...]
  transfers between devices with their start and end apart: 3 -> 16, of which waited for: 3 -> 7; matrix products, arithmetic and copies ran while one was open for 8% -> 0% of each run, Pallas kernels for 0% -> 5%
where the time goes in v1:
time: 53.5 us; the launch traced here: 53.1 us
  waiting for transfers between devices  20.9 us (39%)
  starting transfers between devices  16.3 us (30%)
  local copies, waits for them, and re-layouts  8.74 us (16%)
  Pallas kernels  4.51 us (8%)
  between operations  1.58 us (3%)
  other arithmetic  1.03 us (2%)
    ppermute x9, waiting for transfers between devices, along_part(): return lax.ppermute(x, 'blk', pairs)  11.1 us
    ppermute x9, starting transfers between devices, along_part(): return lax.ppermute(x, 'blk', pairs)  10.5 us
    ppermute x3, waiting for transfers between devices, across_mp(): return lax.ppermute(x, 'mp', [(i, i ^ bit) for i in range(n_mp)])  9.86 us
    unnamed x26, local copies, waits for them, and re-layouts  8.74 us
    ppermute x4, starting transfers between devices, across(): return lax.ppermute(x, 'blk', [(i, i ^ bit) for i in range(n_blk)])  4.05 us
    ppermute x3, starting transfers between devices, across_mp(): return lax.ppermute(x, 'mp', [(i, i ^ bit) for i in range(n_mp)])  1.73 us
    pallas_call x1, Pallas kernels, local(): call(functools.partial(suffix_kernel, heads), [((local_width, rows), f32)...  1.33 us
    pallas_call x1, Pallas kernels, local(): call(functools.partial(query_kernel, heads), [((rows, width), bf16), ((ro...  1.31 us
  transfers between devices with their start and end apart: 16, of which 7 were waited for; matrix products, arithmetic and copies ran while one was open for 0% of the time, Pallas kernels for 5%

profile of v1, /device:TPU:0, one launch (start us, length us, event | category | flops | bytes accessed | tf_op | source)
XLA Modules:
  0.0 53.1 jit_solution(17578962168439939375)
XLA Ops:
  0.0 0.0 copy-start
  1.5 0.0 copy-start.6
  1.5 0.9 %copy-done.6 = bf16[1,128,512]{2,1,0:T(8,128)(2,1)S(1)} copy-done((bf16[1,128,512]{2,1,0:T(8,128)(2,1)S(1)}, bf16[1,128,512]{2,1,0:T(8,128)(2,1)}, u32[]{:S(2)}) %copy-start.6) | copy-done | bytes 131096
  2.4 0.0 copy-start.7
  2.4 0.9 %copy-done.7 = bf16[1,128,512]{2,1,0:T(8,128)(2,1)S(1)} copy-done((bf16[1,128,512]{2,1,0:T(8,128)(2,1)S(1)}, bf16[1,128,512]{2,1,0:T(8,128)(2,1)}, u32[]{:S(2)}) %copy-start.7) | copy-done | bytes 131096
  3.3 0.1 shard_map.129
  3.3 3.1 %collective-permute-start.3 = (bf16[272,128]{1,0:T(8,128)(2,1)S(1)}, bf16[272,128]{1,0:T(8,128)(2,1)S(1)}, u32[]{:S(2)}, u32[]{:S(2)}) collective-permute-start(bf16[272,128]{1,0:T(8,128)(2,1)S(1)} %get-tuple-element.32), channel_id=1, source_target_pairs={{0,8},{4,12},{8,16},{12,20},{16,24},{20,28},{24,0},{28,4},{1,9},{5... | collective-permute-start | bytes 208904 | tf_op jit(solution)/shard_map/ppermute | solution.py:231
  6.4 2.6 %collective-permute-start.4 = (bf16[272,128]{1,0:T(8,128)(2,1)S(1)}, bf16[272,128]{1,0:T(8,128)(2,1)S(1)}, u32[]{:S(2)}, u32[]{:S(2)}) collective-permute-start(bf16[272,128]{1,0:T(8,128)(2,1)S(1)} %get-tuple-element.33), channel_id=1, source_target_pairs={{0,16},{4,20},{8,24},{12,28},{16,0},{20,4},{24,8},{28,12},{1,17},{... | collective-permute-start | bytes 208904 | tf_op jit(solution)/shard_map/ppermute | solution.py:231
  9.0 1.3 %collective-permute-start.5 = (bf16[272,128]{1,0:T(8,128)(2,1)S(1)}, bf16[272,128]{1,0:T(8,128)(2,1)S(1)}, u32[]{:S(2)}, u32[]{:S(2)}) collective-permute-start(bf16[272,128]{1,0:T(8,128)(2,1)S(1)} %get-tuple-element.34), channel_id=1, source_target_pairs={{0,24},{4,28},{8,0},{12,4},{16,8},{20,12},{24,16},{28,20},{1,25},{... | collective-permute-start | bytes 208904 | tf_op jit(solution)/shard_map/ppermute | solution.py:231
  10.3 0.0 copy-start.2
  10.3 1.6 %copy-done.2 = bf16[2048,512]{1,0:T(8,128)(2,1)S(1)} copy-done((bf16[2048,512]{1,0:T(8,128)(2,1)S(1)}, bf16[2048,512]{1,0:T(8,128)(2,1)}, u32[]{:S(2)}) %copy-start.2) | copy-done | bytes 2097176
  11.9 0.0 copy-start.4
  11.9 1.0 %copy-done.4 = bf16[128,2048]{1,0:T(8,128)(2,1)S(1)} copy-done((bf16[128,2048]{1,0:T(8,128)(2,1)S(1)}, bf16[128,2048]{1,0:T(8,128)(2,1)}, u32[]{:S(2)}) %copy-start.4) | copy-done | bytes 524312
  13.0 0.0 copy-start.8
  13.0 0.7 %copy-done.8 = f32[2048]{0:T(1024)S(1)} copy-done((f32[2048]{0:T(1024)S(1)}, f32[2048]{0:T(1024)}, u32[]{:S(2)}) %copy-start.8) | copy-done | bytes 8216
  13.7 0.0 copy-start.9
  13.7 0.7 %copy-done.9 = f32[2048]{0:T(1024)S(1)} copy-done((f32[2048]{0:T(1024)S(1)}, f32[2048]{0:T(1024)}, u32[]{:S(2)}) %copy-start.9) | copy-done | bytes 8216
  14.4 0.0 copy-start.10
  14.4 0.7 %copy-done.10 = s32[1,128]{1,0:T(1,128)S(1)} copy-done((s32[1,128]{1,0:T(1,128)S(1)}, s32[1,128]{1,0:T(1,128)}, u32[]{:S(2)}) %copy-start.10) | copy-done | bytes 536
  15.0 0.0 copy-start.12
  15.0 0.7 %copy-done.12 = s32[1,4]{1,0:T(1,128)S(1)} copy-done((s32[1,4]{1,0:T(1,128)S(1)}, s32[1,4]{1,0:T(1,128)}, u32[]{:S(2)}) %copy-start.12) | copy-done | bytes 40
  15.7 0.0 copy-start.11
  15.7 1.3 %shard_map.127 = (bf16[128,2048]{1,0:T(8,128)(2,1)S(1)}, bf16[128,512]{1,0:T(8,128)(2,1)S(1)}, bf16[144,128]{1,0:T(8,128)(2,1)S(1)}, bf16[144,128]{1,0:T(8,128)(...) custom-call(s32[1]{0:T(128)} %bitcast.part_ref, s32[1,4]{1,0:T(1,128)S(1)} %copy-done.12, ...), custom_call_target="tpu_custom_call" | custom-call | tf_op jit(solution)/shard_map/pallas_call | solution.py:247
  17.0 0.7 %collective-permute-start = (bf16[144,128]{1,0:T(8,128)(2,1)S(1)}, bf16[144,128]{1,0:T(8,128)(2,1)S(1)}, u32[]{:S(2)}, u32[]{:S(2)}) collective-permute-start(bf16[144,128]{1,0:T(8,128)(2,1)S(1)} %get-tuple-element.28), channel_id=1, source_target_pairs={{0,8},{4,12},{8,16},{12,20},{16,24},{20,28},{24,0},{28,4},{1,9},{5... | collective-permute-start | bytes 110600 | tf_op jit(solution)/shard_map/ppermute | solution.py:231
  17.7 0.3 collective-permute-start.1
  18.1 4.8 %collective-permute-done.refs_1_ = bf16[144,128]{1,0:T(8,128)(2,1)S(1)} collective-permute-done((bf16[144,128]{1,0:T(8,128)(2,1)S(1)}, bf16[144,128]{1,0:T(8,128)(2,1)S(1)}, u32[]{:S(2)}, u32[]{:S(2)}) %collective-permute-start) | collective-permute-done | bytes 36896 | tf_op jit(solution)/shard_map/ppermute | solution.py:231
  22.9 1.5 %collective-permute-start.6 = (bf16[272,128]{1,0:T(8,128)(2,1)S(1)}, bf16[272,128]{1,0:T(8,128)(2,1)S(1)}, u32[]{:S(2)}, u32[]{:S(2)}) collective-permute-start(bf16[272,128]{1,0:T(8,128)(2,1)S(1)} %get-tuple-element.31.refs_4_), channel_id=1, source_target_pairs={{0,4},{4,0},{8,12},{12,8},{16,20},{20,16},{24,28},{28,24},{1,5},{5... | collective-permute-start | bytes 208904 | tf_op jit(solution)/shard_map/ppermute | solution.py:234
  24.4 0.0 collective-permute-done.3.refs_5_
  24.4 0.5 %collective-permute-start.7 = (bf16[272,128]{1,0:T(8,128)(2,1)S(1)}, bf16[272,128]{1,0:T(8,128)(2,1)S(1)}, u32[]{:S(2)}, u32[]{:S(2)}) collective-permute-start(bf16[272,128]{1,0:T(8,128)(2,1)S(1)} %collective-permute-done.3.refs_5_), channel_id=1, source_target_pairs={{0,4},{4,0},{8,12},{12,8},{16,20},{20,16},{24,28},{28,24},{1,5},{5... | collective-permute-start | bytes 208904 | tf_op jit(solution)/shard_map/ppermute | solution.py:234
  24.9 0.0 collective-permute-done.4.refs_6_
  24.9 1.5 %collective-permute-start.8 = (bf16[272,128]{1,0:T(8,128)(2,1)S(1)}, bf16[272,128]{1,0:T(8,128)(2,1)S(1)}, u32[]{:S(2)}, u32[]{:S(2)}) collective-permute-start(bf16[272,128]{1,0:T(8,128)(2,1)S(1)} %collective-permute-done.4.refs_6_), channel_id=1, source_target_pairs={{0,4},{4,0},{8,12},{12,8},{16,20},{20,16},{24,28},{28,24},{1,5},{5... | collective-permute-start | bytes 208904 | tf_op jit(solution)/shard_map/ppermute | solution.py:234
  26.4 0.0 collective-permute-done.5.refs_7_
  26.4 0.5 %collective-permute-start.9 = (bf16[272,128]{1,0:T(8,128)(2,1)S(1)}, bf16[272,128]{1,0:T(8,128)(2,1)S(1)}, u32[]{:S(2)}, u32[]{:S(2)}) collective-permute-start(bf16[272,128]{1,0:T(8,128)(2,1)S(1)} %collective-permute-done.5.refs_7_), channel_id=1, source_target_pairs={{0,4},{4,0},{8,12},{12,8},{16,20},{20,16},{24,28},{28,24},{1,5},{5... | collective-permute-start | bytes 208904 | tf_op jit(solution)/shard_map/ppermute | solution.py:234
  27.0 0.0 collective-permute-done.1.refs_2_
  27.0 0.0 collective-permute-start.2
  27.0 4.0 %collective-permute-done.2.refs_3_ = bf16[144,128]{1,0:T(8,128)(2,1)S(1)} collective-permute-done((bf16[144,128]{1,0:T(8,128)(2,1)S(1)}, bf16[144,128]{1,0:T(8,128)(2,1)S(1)}, u32[]{:S(2)}, u32[]{:S(2)}) %collective-permute-start.2) | collective-permute-done | bytes 36896 | tf_op jit(solution)/shard_map/ppermute | solution.py:231
  31.0 0.0 collective-permute-done.6.refs_8_
  31.0 0.0 collective-permute-done.7.refs_9_
  31.0 0.0 collective-permute-done.8.refs_10_
  31.0 0.0 collective-permute-done.9.refs_11_
  31.0 1.2 %shard_map.130 = (bf16[144,128]{1,0:T(8,128)(2,1)S(1)}, bf16[144,128]{1,0:T(8,128)(2,1)S(1)}, bf16[144,128]{1,0:T(8,128)(2,1)S(1)}, bf16[144,128]{1,0:T(8,128)(2,1)S(1)}) custom-call(bf16[144,128]{1,0:T(8,128)(2,1)S(1)} %get-tuple-element.27.refs_0_, bf16[144,128]{1,0:T(8,128)(2,1)S(1)} %collective-permute-done.refs_1_, ...), custom_call_target="tpu_custom_call" | custom-call | tf_op jit(solution)/shard_map/pallas_call | solution.py:274
  32.3 1.8 %collective-permute-start.10 = (bf16[144,128]{1,0:T(8,128)(2,1)S(1)}, bf16[144,128]{1,0:T(8,128)(2,1)S(1)}, u32[]{:S(2)}, u32[]{:S(2)}) collective-permute-start(bf16[144,128]{1,0:T(8,128)(2,1)S(1)} %get-tuple-element.36), channel_id=1, source_target_pairs={{0,24},{4,28},{8,0},{12,4},{16,8},{20,12},{24,16},{28,20},{1,25},{... | collective-permute-start | bytes 110600 | tf_op jit(solution)/shard_map/ppermute | solution.py:231
  34.0 0.0 collective-permute-start.11
  34.0 0.6 %collective-permute-start.12 = (bf16[144,128]{1,0:T(8,128)(2,1)S(1)}, bf16[144,128]{1,0:T(8,128)(2,1)S(1)}, u32[]{:S(2)}, u32[]{:S(2)}) collective-permute-start(bf16[144,128]{1,0:T(8,128)(2,1)S(1)} %get-tuple-element.38), channel_id=1, source_target_pairs={{0,8},{4,12},{8,16},{12,20},{16,24},{20,28},{24,0},{28,4},{1,9},{5... | collective-permute-start | bytes 110600 | tf_op jit(solution)/shard_map/ppermute | solution.py:231
  34.7 0.0 copy-done
  34.7 0.0 copy-done.11
  34.7 0.0 copy-start.1
  34.7 1.6 %copy-done.1 = bf16[2048,512]{1,0:T(8,128)(2,1)S(1)} copy-done((bf16[2048,512]{1,0:T(8,128)(2,1)S(1)}, bf16[2048,512]{1,0:T(8,128)(2,1)}, u32[]{:S(2)}) %copy-start.1) | copy-done | bytes 2097176
  36.3 1.3 %shard_map.128 = (f32[512,128]{1,0:T(8,128)S(1)}, f32[8,128]{1,0:T(8,128)S(1)}) custom-call(bf16[128,2048]{1,0:T(8,128)(2,1)S(1)} %get-tuple-element.23.normed_ref, bf16[128,512]{1,0:T(8,128)(2,1)S(1)} %get-tuple-element.24.query_ref, bf16[2048,512]{1,0:T(8,128)(2,1)S(1)} %copy-done, bf16[2048,512]{1,0:T(8,128)(2,1)S(1)} %copy-done.1, s32[1,128]{1,0:T(1,128)S(1)} %copy-done.11), custom_call_target="tpu_custom_call" | custom-call | tf_op jit(solution)/shard_map/pallas_call | solution.py:268
  37.6 0.0 copy-start.5
  37.6 0.0 collective-permute-done.10.refs_1_
  37.6 1.4 %collective-permute-done.11.refs_2_ = bf16[144,128]{1,0:T(8,128)(2,1)S(1)} collective-permute-done((bf16[144,128]{1,0:T(8,128)(2,1)S(1)}, bf16[144,128]{1,0:T(8,128)(2,1)S(1)}, u32[]{:S(2)}, u32[]{:S(2)}) %collective-permute-start.11) | collective-permute-done | bytes 36896 | tf_op jit(solution)/shard_map/ppermute | solution.py:231
  39.0 0.8 %collective-permute-done.12.refs_3_ = bf16[144,128]{1,0:T(8,128)(2,1)S(1)} collective-permute-done((bf16[144,128]{1,0:T(8,128)(2,1)S(1)}, bf16[144,128]{1,0:T(8,128)(2,1)S(1)}, u32[]{:S(2)}, u32[]{:S(2)}) %collective-permute-start.12) | collective-permute-done | bytes 36896 | tf_op jit(solution)/shard_map/ppermute | solution.py:231
  39.8 0.0 copy-done.3
  39.8 0.6 %shard_map.131 = (f32[64,2048]{1,0:T(8,128)S(1)}, bf16[64,2048]{1,0:T(8,128)(2,1)S(1)}) custom-call(s32[1]{0:T(128)} %bitcast.part_ref, s32[1]{0:T(128)} %bitcast.1.half_ref, f32[512,128]{1,0:T(8,128)S(1)} %get-tuple-element.25.sum_ref, f32[8,128]{1,0:T(8,128)S(1)} %get-tuple-element.26.log_ref, bf16[512,2048]{1,0:T(8,128)(2,1)S(1)} %copy-done.3, ...), custom_call_target="tpu_custom_call" | custom-call | tf_op jit(solution)/shard_map/pallas_call | solution.py:281
  40.4 0.1 collective-permute-start.13
  40.5 1.5 %collective-permute-done.13 = bf16[64,2048]{1,0:T(8,128)(2,1)S(1)} collective-permute-done((bf16[64,2048]{1,0:T(8,128)(2,1)S(1)}, bf16[64,2048]{1,0:T(8,128)(2,1)S(1)}, u32[]{:S(2)}, u32[]{:S(2)}) %collective-permute-start.13) | collective-permute-done | bytes 262176 | tf_op jit(solution)/shard_map/ppermute | solution.py:237
  42.1 1.6 %collective-permute-start.14 = (bf16[64,2048]{1,0:T(8,128)(2,1)S(1)}, bf16[64,2048]{1,0:T(8,128)(2,1)S(1)}, u32[]{:S(2)}, u32[]{:S(2)}) collective-permute-start(bf16[64,2048]{1,0:T(8,128)(2,1)S(1)} %add_convert_fusion.1), channel_id=1, source_target_pairs={{0,2},{1,3},{2,0},{3,1},{4,6},{5,7},{6,4},{7,5},{8,10},{9,11},{10,... | collective-permute-start | bytes 786440 | tf_op jit(solution)/shard_map/ppermute | solution.py:237
  43.7 6.8 %collective-permute-done.14 = bf16[64,2048]{1,0:T(8,128)(2,1)S(1)} collective-permute-done((bf16[64,2048]{1,0:T(8,128)(2,1)S(1)}, bf16[64,2048]{1,0:T(8,128)(2,1)S(1)}, u32[]{:S(2)}, u32[]{:S(2)}) %collective-permute-start.14) | collective-permute-done | bytes 262176 | tf_op jit(solution)/shard_map/ppermute | solution.py:237
  50.5 0.0 copy-done.5
  50.5 0.1 add_convert_fusion
  50.6 0.1 collective-permute-start.15
  50.7 1.5 %collective-permute-done.15 = bf16[64,2048]{1,0:T(8,128)(2,1)S(1)} collective-permute-done((bf16[64,2048]{1,0:T(8,128)(2,1)S(1)}, bf16[64,2048]{1,0:T(8,128)(2,1)S(1)}, u32[]{:S(2)}, u32[]{:S(2)}) %collective-permute-start.15) | collective-permute-done | bytes 262176 | tf_op jit(solution)/shard_map/ppermute | solution.py:237
  52.2 0.8 %pad_maximum_fusion = bf16[128,2048]{1,0:T(8,128)(2,1)} fusion(bf16[64,2048]{1,0:T(8,128)(2,1)S(1)} %get-tuple-element.42, bf16[64,2048]{1,0:T(8,128)(2,1)S(1)} %get-tuple-element.41), kind=kLoop, calls=%fused_computation | loop fusion | flops 1048576 | bytes 1048576 | tf_op jit(solution)/shard_map/concatenate | solution.py:297
  (3 shorter events, 0.1 us)
Async XLA Ops:
  0.0 34.7 %copy-start = (bf16[2048,512]{1,0:T(8,128)(2,1)S(1)}, bf16[2048,512]{1,0:T(8,128)(2,1)}, u32[]{:S(2)}) copy-start(bf16[2048,512]{1,0:T(8,128)(2,1)} %w_key_ref.1) | copy-start | bytes 6291460
  1.5 0.9 %copy-start.6 = (bf16[1,128,512]{2,1,0:T(8,128)(2,1)S(1)}, bf16[1,128,512]{2,1,0:T(8,128)(2,1)}, u32[]{:S(2)}) copy-start(bf16[1,128,512]{2,1,0:T(8,128)(2,1)} %keys_ref.1) | copy-start | bytes 393220
  2.4 0.9 %copy-start.7 = (bf16[1,128,512]{2,1,0:T(8,128)(2,1)S(1)}, bf16[1,128,512]{2,1,0:T(8,128)(2,1)}, u32[]{:S(2)}) copy-start(bf16[1,128,512]{2,1,0:T(8,128)(2,1)} %values_ref.1) | copy-start | bytes 393220
  3.3 21.1 %collective-permute-start.3 = (bf16[272,128]{1,0:T(8,128)(2,1)S(1)}, bf16[272,128]{1,0:T(8,128)(2,1)S(1)}, u32[]{:S(2)}, u32[]{:S(2)}) collective-permute-start(bf16[272,128]{1,0:T(8,128)(2,1)S(1)} %get-tuple-element.32), channel_id=1, source_target_pairs={{0,8},{4,12},{8,16},{12,20},{16,24},{20,28},{24,0},{28,4},{1,9},{5... | collective-permute-start | bytes 208904 | tf_op jit(solution)/shard_map/ppermute | solution.py:231
  6.4 18.5 %collective-permute-start.4 = (bf16[272,128]{1,0:T(8,128)(2,1)S(1)}, bf16[272,128]{1,0:T(8,128)(2,1)S(1)}, u32[]{:S(2)}, u32[]{:S(2)}) collective-permute-start(bf16[272,128]{1,0:T(8,128)(2,1)S(1)} %get-tuple-element.33), channel_id=1, source_target_pairs={{0,16},{4,20},{8,24},{12,28},{16,0},{20,4},{24,8},{28,12},{1,17},{... | collective-permute-start | bytes 208904 | tf_op jit(solution)/shard_map/ppermute | solution.py:231
  9.0 17.4 %collective-permute-start.5 = (bf16[272,128]{1,0:T(8,128)(2,1)S(1)}, bf16[272,128]{1,0:T(8,128)(2,1)S(1)}, u32[]{:S(2)}, u32[]{:S(2)}) collective-permute-start(bf16[272,128]{1,0:T(8,128)(2,1)S(1)} %get-tuple-element.34), channel_id=1, source_target_pairs={{0,24},{4,28},{8,0},{12,4},{16,8},{20,12},{24,16},{28,20},{1,25},{... | collective-permute-start | bytes 208904 | tf_op jit(solution)/shard_map/ppermute | solution.py:231
  10.3 1.6 %copy-start.2 = (bf16[2048,512]{1,0:T(8,128)(2,1)S(1)}, bf16[2048,512]{1,0:T(8,128)(2,1)}, u32[]{:S(2)}) copy-start(bf16[2048,512]{1,0:T(8,128)(2,1)} %w_query_ref.1) | copy-start | bytes 6291460
  11.9 1.0 %copy-start.4 = (bf16[128,2048]{1,0:T(8,128)(2,1)S(1)}, bf16[128,2048]{1,0:T(8,128)(2,1)}, u32[]{:S(2)}) copy-start(bf16[128,2048]{1,0:T(8,128)(2,1)} %hidden_ref.1) | copy-start | bytes 1572868
  13.0 0.7 %copy-start.8 = (f32[2048]{0:T(1024)S(1)}, f32[2048]{0:T(1024)}, u32[]{:S(2)}) copy-start(f32[2048]{0:T(1024)} %param.14) | copy-start | bytes 24580
  13.7 0.7 %copy-start.9 = (f32[2048]{0:T(1024)S(1)}, f32[2048]{0:T(1024)}, u32[]{:S(2)}) copy-start(f32[2048]{0:T(1024)} %param.15) | copy-start | bytes 24580
  14.4 0.7 %copy-start.10 = (s32[1,128]{1,0:T(1,128)S(1)}, s32[1,128]{1,0:T(1,128)}, u32[]{:S(2)}) copy-start(s32[1,128]{1,0:T(1,128)} %segment_ref.3) | copy-start | bytes 1540
  15.0 0.7 %copy-start.12 = (s32[1,4]{1,0:T(1,128)S(1)}, s32[1,4]{1,0:T(1,128)}, u32[]{:S(2)}) copy-start(s32[1,4]{1,0:T(1,128)} %request_group_ref.1) | copy-start | bytes 52
  15.7 19.0 %copy-start.11 = (s32[1,128]{1,0:T(1,128)S(1)}, s32[1,128]{1,0:T(1,128)}, u32[]{:S(2)}) copy-start(s32[1,128]{1,0:T(1,128)} %segment_ref.3) | copy-start | bytes 1540
  17.0 5.9 %collective-permute-start = (bf16[144,128]{1,0:T(8,128)(2,1)S(1)}, bf16[144,128]{1,0:T(8,128)(2,1)S(1)}, u32[]{:S(2)}, u32[]{:S(2)}) collective-permute-start(bf16[144,128]{1,0:T(8,128)(2,1)S(1)} %get-tuple-element.28), channel_id=1, source_target_pairs={{0,8},{4,12},{8,16},{12,20},{16,24},{20,28},{24,0},{28,4},{1,9},{5... | collective-permute-start | bytes 110600 | tf_op jit(solution)/shard_map/ppermute | solution.py:231
  17.7 9.2 %collective-permute-start.1 = (bf16[144,128]{1,0:T(8,128)(2,1)S(1)}, bf16[144,128]{1,0:T(8,128)(2,1)S(1)}, u32[]{:S(2)}, u32[]{:S(2)}) collective-permute-start(bf16[144,128]{1,0:T(8,128)(2,1)S(1)} %get-tuple-element.29), channel_id=1, source_target_pairs={{0,16},{4,20},{8,24},{12,28},{16,0},{20,4},{24,8},{28,12},{1,17},{... | collective-permute-start | bytes 110600 | tf_op jit(solution)/shard_map/ppermute | solution.py:231
  22.9 8.1 %collective-permute-start.6 = (bf16[272,128]{1,0:T(8,128)(2,1)S(1)}, bf16[272,128]{1,0:T(8,128)(2,1)S(1)}, u32[]{:S(2)}, u32[]{:S(2)}) collective-permute-start(bf16[272,128]{1,0:T(8,128)(2,1)S(1)} %get-tuple-element.31.refs_4_), channel_id=1, source_target_pairs={{0,4},{4,0},{8,12},{12,8},{16,20},{20,16},{24,28},{28,24},{1,5},{5... | collective-permute-start | bytes 208904 | tf_op jit(solution)/shard_map/ppermute | solution.py:234
  24.4 6.6 %collective-permute-start.7 = (bf16[272,128]{1,0:T(8,128)(2,1)S(1)}, bf16[272,128]{1,0:T(8,128)(2,1)S(1)}, u32[]{:S(2)}, u32[]{:S(2)}) collective-permute-start(bf16[272,128]{1,0:T(8,128)(2,1)S(1)} %collective-permute-done.3.refs_5_), channel_id=1, source_target_pairs={{0,4},{4,0},{8,12},{12,8},{16,20},{20,16},{24,28},{28,24},{1,5},{5... | collective-permute-start | bytes 208904 | tf_op jit(solution)/shard_map/ppermute | solution.py:234
  24.9 6.1 %collective-permute-start.8 = (bf16[272,128]{1,0:T(8,128)(2,1)S(1)}, bf16[272,128]{1,0:T(8,128)(2,1)S(1)}, u32[]{:S(2)}, u32[]{:S(2)}) collective-permute-start(bf16[272,128]{1,0:T(8,128)(2,1)S(1)} %collective-permute-done.4.refs_6_), channel_id=1, source_target_pairs={{0,4},{4,0},{8,12},{12,8},{16,20},{20,16},{24,28},{28,24},{1,5},{5... | collective-permute-start | bytes 208904 | tf_op jit(solution)/shard_map/ppermute | solution.py:234
  26.4 4.6 %collective-permute-start.9 = (bf16[272,128]{1,0:T(8,128)(2,1)S(1)}, bf16[272,128]{1,0:T(8,128)(2,1)S(1)}, u32[]{:S(2)}, u32[]{:S(2)}) collective-permute-start(bf16[272,128]{1,0:T(8,128)(2,1)S(1)} %collective-permute-done.5.refs_7_), channel_id=1, source_target_pairs={{0,4},{4,0},{8,12},{12,8},{16,20},{20,16},{24,28},{28,24},{1,5},{5... | collective-permute-start | bytes 208904 | tf_op jit(solution)/shard_map/ppermute | solution.py:234
  27.0 4.1 %collective-permute-start.2 = (bf16[144,128]{1,0:T(8,128)(2,1)S(1)}, bf16[144,128]{1,0:T(8,128)(2,1)S(1)}, u32[]{:S(2)}, u32[]{:S(2)}) collective-permute-start(bf16[144,128]{1,0:T(8,128)(2,1)S(1)} %get-tuple-element.30), channel_id=1, source_target_pairs={{0,24},{4,28},{8,0},{12,4},{16,8},{20,12},{24,16},{28,20},{1,25},{... | collective-permute-start | bytes 110600 | tf_op jit(solution)/shard_map/ppermute | solution.py:231
  32.3 5.4 %collective-permute-start.10 = (bf16[144,128]{1,0:T(8,128)(2,1)S(1)}, bf16[144,128]{1,0:T(8,128)(2,1)S(1)}, u32[]{:S(2)}, u32[]{:S(2)}) collective-permute-start(bf16[144,128]{1,0:T(8,128)(2,1)S(1)} %get-tuple-element.36), channel_id=1, source_target_pairs={{0,24},{4,28},{8,0},{12,4},{16,8},{20,12},{24,16},{28,20},{1,25},{... | collective-permute-start | bytes 110600 | tf_op jit(solution)/shard_map/ppermute | solution.py:231
  34.0 5.0 %collective-permute-start.11 = (bf16[144,128]{1,0:T(8,128)(2,1)S(1)}, bf16[144,128]{1,0:T(8,128)(2,1)S(1)}, u32[]{:S(2)}, u32[]{:S(2)}) collective-permute-start(bf16[144,128]{1,0:T(8,128)(2,1)S(1)} %get-tuple-element.37), channel_id=1, source_target_pairs={{0,16},{4,20},{8,24},{12,28},{16,0},{20,4},{24,8},{28,12},{1,17},{... | collective-permute-start | bytes 110600 | tf_op jit(solution)/shard_map/ppermute | solution.py:231
  34.0 5.8 %collective-permute-start.12 = (bf16[144,128]{1,0:T(8,128)(2,1)S(1)}, bf16[144,128]{1,0:T(8,128)(2,1)S(1)}, u32[]{:S(2)}, u32[]{:S(2)}) collective-permute-start(bf16[144,128]{1,0:T(8,128)(2,1)S(1)} %get-tuple-element.38), channel_id=1, source_target_pairs={{0,8},{4,12},{8,16},{12,20},{16,24},{20,28},{24,0},{28,4},{1,9},{5... | collective-permute-start | bytes 110600 | tf_op jit(solution)/shard_map/ppermute | solution.py:231
  34.7 1.6 %copy-start.1 = (bf16[2048,512]{1,0:T(8,128)(2,1)S(1)}, bf16[2048,512]{1,0:T(8,128)(2,1)}, u32[]{:S(2)}) copy-start(bf16[2048,512]{1,0:T(8,128)(2,1)} %w_value_ref.1) | copy-start | bytes 6291460
  36.3 3.5 %copy-start.3 = (bf16[512,2048]{1,0:T(8,128)(2,1)S(1)}, bf16[512,2048]{1,0:T(8,128)(2,1)}, u32[]{:S(2)}) copy-start(bf16[512,2048]{1,0:T(8,128)(2,1)} %w_out_ref.1) | copy-start | bytes 6291460
  37.6 12.9 %copy-start.5 = (bf16[128,2048]{1,0:T(8,128)(2,1)S(1)}, bf16[128,2048]{1,0:T(8,128)(2,1)}, u32[]{:S(2)}) copy-start(bf16[128,2048]{1,0:T(8,128)(2,1)} %hidden_ref.1) | copy-start | bytes 1572868
  40.4 1.6 %collective-permute-start.13 = (bf16[64,2048]{1,0:T(8,128)(2,1)S(1)}, bf16[64,2048]{1,0:T(8,128)(2,1)S(1)}, u32[]{:S(2)}, u32[]{:S(2)}) collective-permute-start(bf16[64,2048]{1,0:T(8,128)(2,1)S(1)} %get-tuple-element.40), channel_id=1, source_target_pairs={{0,1},{1,0},{2,3},{3,2},{4,5},{5,4},{6,7},{7,6},{8,9},{9,8},{10,11... | collective-permute-start | bytes 786440 | tf_op jit(solution)/shard_map/ppermute | solution.py:237
  42.1 8.4 %collective-permute-start.14 = (bf16[64,2048]{1,0:T(8,128)(2,1)S(1)}, bf16[64,2048]{1,0:T(8,128)(2,1)S(1)}, u32[]{:S(2)}, u32[]{:S(2)}) collective-permute-start(bf16[64,2048]{1,0:T(8,128)(2,1)S(1)} %add_convert_fusion.1), channel_id=1, source_target_pairs={{0,2},{1,3},{2,0},{3,1},{4,6},{5,7},{6,4},{7,5},{8,10},{9,11},{10,... | collective-permute-start | bytes 786440 | tf_op jit(solution)/shard_map/ppermute | solution.py:237
  50.6 1.6 %collective-permute-start.15 = (bf16[64,2048]{1,0:T(8,128)(2,1)S(1)}, bf16[64,2048]{1,0:T(8,128)(2,1)S(1)}, u32[]{:S(2)}, u32[]{:S(2)}) collective-permute-start(bf16[64,2048]{1,0:T(8,128)(2,1)S(1)} %add_convert_fusion), channel_id=1, source_target_pairs={{0,1},{1,0},{2,3},{3,2},{4,5},{5,4},{6,7},{7,6},{8,9},{9,8},{10,11... | collective-permute-start | bytes 786440 | tf_op jit(solution)/shard_map/ppermute | solution.py:237

commit v2 on v1

v2 whole, which is shorter than its diff:
```python
import functools

import jax
import jax.numpy as jnp
from jax import lax
from jax.experimental import pallas as pl
from jax.experimental.pallas import tpu as pltpu
from jax.sharding import PartitionSpec as P

HD = 128
GROUPS = 4
NOTE_ROWS = 16
NOTES = 2 * HD
W_CUTS = 4

big = 1e30

VMEM = pl.BlockSpec(memory_space=pltpu.VMEM)
HBM = pl.BlockSpec(memory_space=pltpu.HBM)
NT = (((1,), (1,)), ((), ()))
TN = (((0,), (0,)), ((), ()))


def dot(a, b, dims=(((1,), (0,)), ((), ()))):
    return lax.dot_general(a, b, dims, preferred_element_type=jnp.float32)


def head_at(rest, shift, heads):
    part = lax.div(lax.axis_index("blk"), rest)
    return pl.multiple_of(lax.rem(part + shift, heads) * HD, HD)


def start_all(pairs, sems):
    copies = [pltpu.make_async_copy(a, b, sems.at[i]) for i, (a, b) in enumerate(pairs)]
    for copy in copies:
        copy.start()
    return copies


def front_kernel(heads, rest, *refs):
    keys_ref, values_ref, tag_ref, sources = refs[0], refs[1], refs[2], refs[3:9]
    normed_ref, query_ref = refs[9:11]
    outs, held, sems = refs[11 : 11 + heads], refs[11 + heads : -1], refs[-1]
    hidden_ref, w_query_ref, gain_ref, bias_ref, segment_ref, request_group_ref = held
    rows = hidden_ref.shape[0]
    pairs = list(zip(sources, held))
    for k in range(heads):
        at = pl.ds(head_at(rest, k, heads), HD)
        pairs.append((keys_ref.at[0, :, at], outs[k].at[0:HD, :]))
        pairs.append((values_ref.at[0, :, at], outs[k].at[HD : 2 * HD, :]))
    copies = start_all(pairs, sems)
    copies[0].wait()
    inputs = hidden_ref[...].astype(jnp.float32)
    mean = jnp.mean(inputs, axis=-1, keepdims=True)
    centred = inputs - mean
    var = jnp.mean(centred * centred, axis=-1, keepdims=True)
    copies[2].wait()
    copies[3].wait()
    normed = centred * lax.rsqrt(var + 1e-05) * gain_ref[...] + bias_ref[...]
    normed = normed.astype(jnp.bfloat16)
    normed_ref[...] = normed
    copies[4].wait()
    copies[5].wait()
    segment = segment_ref[...]
    group = jnp.zeros_like(segment)
    for r in range(request_group_ref.shape[1]):
        group = jnp.where(segment == r, request_group_ref[0, r], group)
    tag = tag_ref[...].astype(jnp.float32)
    place = lax.broadcasted_iota(jnp.int32, tag.shape, 0)
    notes = jnp.where(place == 0, tag, group.astype(jnp.float32)).astype(jnp.bfloat16)
    copies[1].wait()
    query = dot(normed, w_query_ref[...]) * (HD**-0.5)
    query_ref[...] = query.astype(jnp.bfloat16)
    for k in range(heads):
        at = pl.ds(head_at(rest, k, heads), HD)
        outs[k][NOTES : NOTES + NOTE_ROWS, :] = notes
        outs[k][NOTES + NOTE_ROWS : NOTES + NOTE_ROWS + rows, :] = query_ref[:, at]
    for copy in copies[6:]:
        copy.wait()


def suffix_kernel(heads, normed_ref, query_ref, *refs):
    sources, (sum_ref, log_ref), held, sems = refs[:3], refs[3:5], refs[5:8], refs[8]
    segment_ref, w_key_ref, w_value_ref = held
    rows, width = normed_ref.shape
    cut = width // W_CUTS
    pairs = [(sources[0], held[0])]
    for source, target in zip(sources[1:], held[1:]):
        pairs += [(source.at[pl.ds(i * cut, cut), :], target.at[pl.ds(i * cut, cut), :]) for i in range(W_CUTS)]
    copies = start_all(pairs, sems)

    def project(target, waits):
        out = jnp.zeros((rows, target.shape[1]), jnp.float32)
        for i, copy in enumerate(waits):
            copy.wait()
            at = slice(i * cut, (i + 1) * cut)
            out = out + dot(normed_ref[:, at], target[at, :])
        return out.astype(jnp.bfloat16)

    key = project(w_key_ref, copies[1 : 1 + W_CUTS])
    value = project(w_value_ref, copies[1 + W_CUTS :])
    copies[0].wait()
    by_token = jnp.broadcast_to(segment_ref[...], (rows, rows))
    key_place = lax.broadcasted_iota(jnp.int32, (rows, rows), 0)
    token_place = lax.broadcasted_iota(jnp.int32, (rows, rows), 1)
    by_key = jnp.sum(
        jnp.where(key_place == token_place, by_token, 0).astype(jnp.float32), axis=1, keepdims=True
    )
    mask = (by_key == by_token.astype(jnp.float32)) & (key_place <= token_place)
    for h in range(heads):
        cols = slice(h * HD, (h + 1) * HD)
        scores = jnp.where(mask, dot(key[:, cols], query_ref[:, cols], NT), -big)
        top = jnp.max(scores, axis=0, keepdims=True)
        weights = jnp.exp(scores - top)
        total = jnp.sum(weights, axis=0, keepdims=True)
        summed = dot(value[:, cols], weights.astype(jnp.bfloat16), TN)
        sum_ref[cols, :] = summed / total
        log_ref[h : h + 1, :] = top + jnp.log(total)


def prefix_kernel(n_queries, n_blocks, rows, *refs):
    blocks, outs = refs[:n_blocks], refs[n_blocks : n_blocks + n_queries]
    step = NOTES + NOTE_ROWS + rows
    query = jnp.concatenate([ref[NOTES + NOTE_ROWS : step, :] for ref in blocks[:n_queries]], axis=0)
    group = jnp.concatenate(
        [
            ref[NOTES : NOTES + NOTE_ROWS, :].astype(jnp.float32)[1:2, :]
            for ref in blocks[:n_queries]
        ],
        axis=1,
    )
    tokens = query.shape[0]

    def one(ref, at):
        tag = ref[pl.ds(at + NOTES, NOTE_ROWS), :].astype(jnp.float32)[0:1, 0:1]
        return dot(ref[pl.ds(at, HD), :], query, NT), group == tag, ref[pl.ds(at + HD, HD), :]

    def absorb(carry, found):
        top, total, summed = carry
        new_top = top
        for scores, mask, _ in found:
            best = jnp.max(scores, axis=0, keepdims=True)
            new_top = jnp.maximum(new_top, jnp.where(mask, best, -big))
        factor = jnp.exp(top - new_top)
        total, summed = total * factor, summed * factor
        for scores, mask, values in found:
            weights = jnp.exp(scores - jnp.where(mask, new_top, big))
            total = total + jnp.sum(weights, axis=0, keepdims=True)
            summed = summed + dot(values, weights.astype(jnp.bfloat16), TN)
        return new_top, total, summed

    carry = (
        jnp.full((1, tokens), -big, jnp.float32),
        jnp.zeros((1, tokens), jnp.float32),
        jnp.zeros((HD, tokens), jnp.float32),
    )
    carry = absorb(carry, [one(ref, 0) for ref in blocks if ref.shape[0] == step])
    for ref in blocks:
        held = ref.shape[0] // step
        if held > 1:

            def body(i, state, ref=ref):
                return absorb(state, [one(ref, pl.multiple_of(i * step, NOTE_ROWS))])

            carry = lax.fori_loop(0, held, body, carry)
    top, total, summed = carry
    found = total > 0.0
    summed = summed * jnp.where(found, 1.0 / jnp.where(found, total, 1.0), 0.0)
    log = jnp.where(found, top + jnp.log(jnp.where(found, total, 1.0)), -big)
    first = log.astype(jnp.bfloat16).astype(jnp.float32)
    second = (log - first).astype(jnp.bfloat16).astype(jnp.float32)
    third = log - first - second
    place = lax.broadcasted_iota(jnp.int32, (NOTE_ROWS, tokens), 0)
    logs = jnp.where(place == 0, first, jnp.where(place == 1, second, jnp.where(place == 2, third, 0.0)))
    for k in range(n_queries):
        cols = slice(k * rows, (k + 1) * rows)
        outs[k][0:HD, :] = summed[:, cols].astype(jnp.bfloat16)
        outs[k][HD : HD + NOTE_ROWS, :] = logs[:, cols].astype(jnp.bfloat16)


def project_kernel(heads, rest, sum_ref, log_ref, w_out_ref, *refs):
    backs = refs[:heads]
    keep_ref, send_ref, attended, branch = refs[heads:]
    for k in range(heads):
        at = head_at(rest, k, heads)
        logs = backs[k][HD : HD + NOTE_ROWS, :].astype(jnp.float32)
        prefix_log = logs[0:1, :] + logs[1:2, :] + logs[2:3, :]
        suffix_log = log_ref[pl.ds(lax.div(at, HD), 1), :]
        top = jnp.maximum(prefix_log, suffix_log)
        prefix_part = jnp.exp(prefix_log - top)
        suffix_part = jnp.exp(suffix_log - top)
        whole = prefix_part + suffix_part
        joined = (
            backs[k][0:HD, :].astype(jnp.float32) * (prefix_part / whole)
            + sum_ref[pl.ds(at, HD), :] * (suffix_part / whole)
        )
        attended[pl.ds(at, HD), :] = joined.astype(jnp.bfloat16)
    branch[...] = dot(attended[...], w_out_ref[...], TN)
    half = keep_ref.shape[0]
    side = lax.rem(lax.axis_index("mp"), 2)
    mine = pl.multiple_of(side * half, half)
    other = pl.multiple_of((1 - side) * half, half)
    keep_ref[...] = branch[pl.ds(mine, half), :]
    send_ref[...] = branch[pl.ds(other, half), :].astype(jnp.bfloat16)


def call(kernel, outs, specs, scratch=()):
    def run(*args):
        pinned = [
            pltpu.with_memory_space_constraint(x, pltpu.HBM) if spec is HBM else x
            for x, spec in zip(args, specs)
        ]
        return inner(*pinned)

    inner = pl.pallas_call(
        kernel,
        out_shape=tuple(jax.ShapeDtypeStruct(s, t) for s, t in outs),
        in_specs=specs,
        out_specs=(VMEM,) * len(outs),
        scratch_shapes=scratch,
        compiler_params=pltpu.CompilerParams(vmem_limit_bytes=40 * 1024 * 1024),
    )
    return run


def local(
    hidden_in,
    norm_gain,
    norm_bias,
    w_query,
    w_key,
    w_value,
    w_out,
    prefix_keys,
    prefix_values,
    segment,
    request_group,
    block_slot,
    block_live,
):
    bf16, f32, i32 = jnp.bfloat16, jnp.float32, jnp.int32
    rows, width = hidden_in.shape
    local_width = w_query.shape[1]
    heads = local_width // HD
    n_blk = lax.axis_size("blk")
    n_mp = lax.axis_size("mp")
    rest = n_blk // heads
    side = lax.rem(lax.axis_index("mp"), 2)

    def exchange(x, shift, back=False):
        pairs = []
        for i in range(n_blk):
            part, place, lane = i // rest, i % rest // 2, i % 2
            for m in range(n_mp):
                other, core = m // 2, m % 2
                blk = (part + shift) % heads * rest + place * 2 + core
                pair = (i * n_mp + m, blk * n_mp + other * 2 + 1 - lane)
                pairs.append(pair[::-1] if back else pair)
        return lax.ppermute(x, ("blk", "mp"), pairs)

    def across(x, bit):
        return lax.ppermute(x, "blk", [(i, i ^ bit) for i in range(n_blk)])

    def across_mp(x, bit):
        return lax.ppermute(x, "mp", [(i, i ^ bit) for i in range(n_mp)])

    group = jnp.where(block_live == 1, block_slot * GROUPS // n_blk, -1).astype(bf16)
    normed, query, *packs = call(
        functools.partial(front_kernel, heads, rest),
        [((rows, width), bf16), ((rows, local_width), bf16)]
        + [((NOTES + NOTE_ROWS + rows, HD), bf16)] * heads,
        (HBM, HBM, VMEM) + (HBM,) * 6,
        [
            pltpu.VMEM((rows, width), bf16),
            pltpu.VMEM(w_query.shape, bf16),
            pltpu.VMEM((1, width), f32),
            pltpu.VMEM((1, width), f32),
            pltpu.VMEM(segment.shape, i32),
            pltpu.SMEM(request_group.shape, i32),
            pltpu.SemaphoreType.DMA((6 + 2 * heads,)),
        ],
    )(
        prefix_keys,
        prefix_values,
        jnp.broadcast_to(group, (NOTE_ROWS, HD)),
        hidden_in,
        w_query,
        norm_gain.reshape(1, width),
        norm_bias.reshape(1, width),
        segment,
        request_group,
    )
    blocks = [exchange(packs[k], k) for k in range(heads)]
    suffix_sum, suffix_log = call(
        functools.partial(suffix_kernel, heads),
        [((local_width, rows), f32), ((max(heads, 8), rows), f32)],
        (VMEM,) * 2 + (HBM,) * 3,
        [
            pltpu.VMEM(segment.shape, i32),
            pltpu.VMEM(w_key.shape, bf16),
            pltpu.VMEM(w_value.shape, bf16),
            pltpu.SemaphoreType.DMA((1 + 2 * W_CUTS,)),
        ],
    )(normed, query, segment, w_key, w_value)
    blocks, suffix_sum, suffix_log = lax.optimization_barrier((blocks, suffix_sum, suffix_log))
    blocks = blocks + [across_mp(x, 1) for x in blocks]
    bit = 2
    while bit < rest:
        blocks = blocks + [across(jnp.concatenate(blocks, axis=0), bit)]
        bit *= 2

    backs = call(
        functools.partial(prefix_kernel, heads, len(blocks), rows),
        [((HD + NOTE_ROWS, rows), bf16)] * heads,
        (VMEM,) * len(blocks),
    )(*blocks)
    backs = [exchange(backs[k], k, back=True) for k in range(heads)]

    keep, send = call(
        functools.partial(project_kernel, heads, rest),
        [((rows // 2, width), f32), ((rows // 2, width), bf16)],
        (VMEM,) * (3 + heads),
        [pltpu.VMEM((local_width, rows), bf16), pltpu.VMEM((rows, width), f32)],
    )(suffix_sum, suffix_log, w_out, *backs)

    mine = (keep + across_mp(send, 1).astype(f32)).astype(bf16)
    bit = 2
    while bit < n_mp:
        mine = (mine.astype(f32) + across_mp(mine, bit).astype(f32)).astype(bf16 if 2 * bit < n_mp else f32)
        bit *= 2
    inputs = lax.dynamic_slice_in_dim(hidden_in, side * (rows // 2), rows // 2, 0)
    done = (inputs.astype(f32) + mine.astype(f32)).astype(bf16)
    other = across_mp(done, 1)
    first = side == 0
    return jnp.concatenate([jnp.where(first, done, other), jnp.where(first, other, done)], axis=0)


def solution(mesh):
    return jax.shard_map(
        local,
        mesh=mesh,
        in_specs=(
            P("blk", None),
            P(),
            P(),
            P(None, "mp"),
            P(None, "mp"),
            P(None, "mp"),
            P("mp", None),
            P("blk", None, "mp"),
            P("blk", None, "mp"),
            P("blk", None),
            P("blk", None),
            P("blk"),
            P("blk"),
        ),
        out_specs=P("blk", None),
        check_vma=False,
    )
```

time: 53.5 us -> 45.3 us (0.85)
  local copies, waits for them, and re-layouts: 8.74 us -> 0.01 us
  Pallas kernels: 4.51 us -> 7.66 us
  waiting for transfers between devices: 20.9 us -> 18.5 us
    unnamed x26 -> x4, local copies, waits for them, and re-layouts: 8.74 us -> 0.01 us
    ppermute x13 -> x8, waiting for transfers between devices: 11.1 us -> 7.91 us  [exchange(): return lax.ppermute(x, ('blk', 'mp'), pairs)]
    pallas_call x5 -> x4, Pallas kernels: 4.51 us -> 7.66 us  [run(): return inner(*pinned)]
    ppermute x3 -> x7, starting transfers between devices: 1.73 us -> 3.23 us  [across_mp(): return lax.ppermute(x, 'mp', [(i, i ^ bit) for i in range(n_mp)])]
    ppermute x13 -> x8, starting transfers between devices: 14.5 us -> 13.3 us  [exchange(): return lax.ppermute(x, ('blk', 'mp'), pairs)]
    ppermute x3 -> x7, waiting for transfers between devices: 9.86 us -> 10.6 us  [across_mp(): return lax.ppermute(x, 'mp', [(i, i ^ bit) for i in range(n_mp)])]
  transfers between devices with their start and end apart: 16 -> 15, of which waited for: 7 -> 12; matrix products, arithmetic and copies ran while one was open for 0% -> 0% of each run, Pallas kernels for 5% -> 8%
where the time goes in v2:
time: 45.3 us; the launch traced here: 45.1 us
  waiting for transfers between devices  18.5 us (41%)
  starting transfers between devices  16.5 us (36%)
  Pallas kernels  7.66 us (17%)
  between operations  1.43 us (3%)
  other arithmetic  1.03 us (2%)
    ppermute x8, starting transfers between devices, exchange(): return lax.ppermute(x, ('blk', 'mp'), pairs)  13.3 us
    ppermute x7, waiting for transfers between devices, across_mp(): return lax.ppermute(x, 'mp', [(i, i ^ bit) for i in range(n_mp)])  10.6 us
    ppermute x8, waiting for transfers between devices, exchange(): return lax.ppermute(x, ('blk', 'mp'), pairs)  7.91 us
    pallas_call x4, Pallas kernels, run(): return inner(*pinned)  7.66 us
    ppermute x7, starting transfers between devices, across_mp(): return lax.ppermute(x, 'mp', [(i, i ^ bit) for i in range(n_mp)])  3.23 us
  transfers between devices with their start and end apart: 15, of which 12 were waited for; matrix products, arithmetic and copies ran while one was open for 0% of the time, Pallas kernels for 8%

profile of v2, /device:TPU:0, one launch (start us, length us, event | category | flops | bytes accessed | tf_op | source)
XLA Modules:
  0.0 45.1 jit_solution(14651596113902915496)
XLA Ops:
  1.3 2.4 %shard_map.127 = (bf16[128,2048]{1,0:T(8,128)(2,1)S(1)}, bf16[128,512]{1,0:T(8,128)(2,1)S(1)}, bf16[400,128]{1,0:T(8,128)(2,1)S(1)}, bf16[400,128]{1,0:T(8,128)(...) custom-call(bf16[1,128,512]{2,1,0:T(8,128)(2,1)} %refs_0_.2, bf16[1,128,512]{2,1,0:T(8,128)(2,1)} %refs_1_.2, ...), custom_call_target="tpu_custom_call" | custom-call | tf_op jit(solution)/shard_map/pallas_call | solution.py:213
  3.7 0.5 %collective-permute-start = (bf16[400,128]{1,0:T(8,128)(2,1)S(1)}, bf16[400,128]{1,0:T(8,128)(2,1)S(1)}, u32[]{:S(2)}, u32[]{:S(2)}) collective-permute-start(bf16[400,128]{1,0:T(8,128)(2,1)S(1)} %get-tuple-element.25), channel_id=1, source_target_pairs={{0,1},{1,5},{2,3},{3,7},{4,0},{5,4},{6,2},{7,6},{8,9},{9,13},{10,1... | collective-permute-start | bytes 307208 | tf_op jit(solution)/shard_map/ppermute | solution.py:259
  4.2 3.2 %collective-permute-start.1 = (bf16[400,128]{1,0:T(8,128)(2,1)S(1)}, bf16[400,128]{1,0:T(8,128)(2,1)S(1)}, u32[]{:S(2)}, u32[]{:S(2)}) collective-permute-start(bf16[400,128]{1,0:T(8,128)(2,1)S(1)} %get-tuple-element.26), channel_id=1, source_target_pairs={{0,9},{1,13},{2,11},{3,15},{4,8},{5,12},{6,10},{7,14},{8,17},{9,21... | collective-permute-start | bytes 307208 | tf_op jit(solution)/shard_map/ppermute | solution.py:259
  7.4 2.7 %collective-permute-start.2 = (bf16[400,128]{1,0:T(8,128)(2,1)S(1)}, bf16[400,128]{1,0:T(8,128)(2,1)S(1)}, u32[]{:S(2)}, u32[]{:S(2)}) collective-permute-start(bf16[400,128]{1,0:T(8,128)(2,1)S(1)} %get-tuple-element.27), channel_id=1, source_target_pairs={{0,17},{1,21},{2,19},{3,23},{4,16},{5,20},{6,18},{7,22},{8,25},{9,... | collective-permute-start | bytes 307208 | tf_op jit(solution)/shard_map/ppermute | solution.py:259
  10.1 1.5 %collective-permute-start.3 = (bf16[400,128]{1,0:T(8,128)(2,1)S(1)}, bf16[400,128]{1,0:T(8,128)(2,1)S(1)}, u32[]{:S(2)}, u32[]{:S(2)}) collective-permute-start(bf16[400,128]{1,0:T(8,128)(2,1)S(1)} %get-tuple-element.28), channel_id=1, source_target_pairs={{0,25},{1,29},{2,27},{3,31},{4,24},{5,28},{6,26},{7,30},{8,1},{9,5... | collective-permute-start | bytes 307208 | tf_op jit(solution)/shard_map/ppermute | solution.py:259
  11.6 0.0 copy-start
  11.6 3.4 %shard_map.128 = (f32[512,128]{1,0:T(8,128)S(1)}, f32[8,128]{1,0:T(8,128)S(1)}) custom-call(bf16[128,2048]{1,0:T(8,128)(2,1)S(1)} %get-tuple-element.29.normed_ref, bf16[128,512]{1,0:T(8,128)(2,1)S(1)} %get-tuple-element.30.query_ref, s32[1,128]{1,0:T(1,128)} %refs_0_.3, bf16[2048,512]{1,0:T(8,128)(2,1)} %refs_1_.3, bf16[2048,512]{1,0:T(8,128)(2,1)} %refs_2_.1), custom_call_target="tpu_custom_call" | custom-call | tf_op jit(solution)/shard_map/pallas_call | solution.py:213
  15.0 0.0 collective-permute-done.refs_0_
  15.0 0.0 collective-permute-done.1.refs_1_
  15.0 2.8 %collective-permute-done.2.refs_2_ = bf16[400,128]{1,0:T(8,128)(2,1)S(1)} collective-permute-done((bf16[400,128]{1,0:T(8,128)(2,1)S(1)}, bf16[400,128]{1,0:T(8,128)(2,1)S(1)}, u32[]{:S(2)}, u32[]{:S(2)}) %collective-permute-start.2) | collective-permute-done | bytes 102432 | tf_op jit(solution)/shard_map/ppermute | solution.py:259
  17.8 0.4 collective-permute-done.3.refs_3_
  18.3 0.0 copy-start.1
  18.3 0.0 collective-permute-start.4
  18.3 0.5 %collective-permute-start.5 = (bf16[400,128]{1,0:T(8,128)(2,1)S(1)}, bf16[400,128]{1,0:T(8,128)(2,1)S(1)}, u32[]{:S(2)}, u32[]{:S(2)}) collective-permute-start(bf16[400,128]{1,0:T(8,128)(2,1)S(1)} %collective-permute-done.1.refs_1_), channel_id=1, source_target_pairs={{0,1},{1,0},{2,3},{3,2},{4,5},{5,4},{6,7},{7,6},{8,9},{9,8},{10,11... | collective-permute-start | bytes 307208 | tf_op jit(solution)/shard_map/ppermute | solution.py:265
  18.8 0.0 collective-permute-start.6
  18.8 0.5 %collective-permute-start.7 = (bf16[400,128]{1,0:T(8,128)(2,1)S(1)}, bf16[400,128]{1,0:T(8,128)(2,1)S(1)}, u32[]{:S(2)}, u32[]{:S(2)}) collective-permute-start(bf16[400,128]{1,0:T(8,128)(2,1)S(1)} %collective-permute-done.3.refs_3_), channel_id=1, source_target_pairs={{0,1},{1,0},{2,3},{3,2},{4,5},{5,4},{6,7},{7,6},{8,9},{9,8},{10,11... | collective-permute-start | bytes 307208 | tf_op jit(solution)/shard_map/ppermute | solution.py:265
  19.3 0.3 collective-permute-done.4.refs_4_
  19.6 0.2 collective-permute-done.5.refs_5_
  19.7 0.4 collective-permute-done.6.refs_6_
  20.1 0.2 collective-permute-done.7.refs_7_
  20.2 1.2 %shard_map.129 = (bf16[144,128]{1,0:T(8,128)(2,1)S(1)}, bf16[144,128]{1,0:T(8,128)(2,1)S(1)}, bf16[144,128]{1,0:T(8,128)(2,1)S(1)}, bf16[144,128]{1,0:T(8,128)(2,1)S(1)}) custom-call(bf16[400,128]{1,0:T(8,128)(2,1)S(1)} %collective-permute-done.refs_0_, bf16[400,128]{1,0:T(8,128)(2,1)S(1)} %collective-permute-done.1.refs_1_, ...), custom_call_target="tpu_custom_call" | custom-call | tf_op jit(solution)/shard_map/pallas_call | solution.py:213
  21.5 0.5 %collective-permute-start.8 = (bf16[144,128]{1,0:T(8,128)(2,1)S(1)}, bf16[144,128]{1,0:T(8,128)(2,1)S(1)}, u32[]{:S(2)}, u32[]{:S(2)}) collective-permute-start(bf16[144,128]{1,0:T(8,128)(2,1)S(1)} %get-tuple-element.39), channel_id=1, source_target_pairs={{1,0},{5,1},{3,2},{7,3},{0,4},{4,5},{2,6},{6,7},{9,8},{13,9},{11,1... | collective-permute-start | bytes 110600 | tf_op jit(solution)/shard_map/ppermute | solution.py:259
  21.9 3.4 %collective-permute-start.9 = (bf16[144,128]{1,0:T(8,128)(2,1)S(1)}, bf16[144,128]{1,0:T(8,128)(2,1)S(1)}, u32[]{:S(2)}, u32[]{:S(2)}) collective-permute-start(bf16[144,128]{1,0:T(8,128)(2,1)S(1)} %get-tuple-element.40), channel_id=1, source_target_pairs={{9,0},{13,1},{11,2},{15,3},{8,4},{12,5},{10,6},{14,7},{17,8},{21,9... | collective-permute-start | bytes 110600 | tf_op jit(solution)/shard_map/ppermute | solution.py:259
  25.4 0.9 %collective-permute-start.10 = (bf16[144,128]{1,0:T(8,128)(2,1)S(1)}, bf16[144,128]{1,0:T(8,128)(2,1)S(1)}, u32[]{:S(2)}, u32[]{:S(2)}) collective-permute-start(bf16[144,128]{1,0:T(8,128)(2,1)S(1)} %get-tuple-element.41), channel_id=1, source_target_pairs={{17,0},{21,1},{19,2},{23,3},{16,4},{20,5},{18,6},{22,7},{25,8},{29... | collective-permute-start | bytes 110600 | tf_op jit(solution)/shard_map/ppermute | solution.py:259
  26.3 0.5 %collective-permute-start.11 = (bf16[144,128]{1,0:T(8,128)(2,1)S(1)}, bf16[144,128]{1,0:T(8,128)(2,1)S(1)}, u32[]{:S(2)}, u32[]{:S(2)}) collective-permute-start(bf16[144,128]{1,0:T(8,128)(2,1)S(1)} %get-tuple-element.42), channel_id=1, source_target_pairs={{25,0},{29,1},{27,2},{31,3},{24,4},{28,5},{26,6},{30,7},{1,8},{5,9... | collective-permute-start | bytes 110600 | tf_op jit(solution)/shard_map/ppermute | solution.py:259
  26.8 0.0 collective-permute-done.8.refs_0_
  26.8 0.4 collective-permute-done.9.refs_1_
  27.3 2.4 %collective-permute-done.10.refs_2_ = bf16[144,128]{1,0:T(8,128)(2,1)S(1)} collective-permute-done((bf16[144,128]{1,0:T(8,128)(2,1)S(1)}, bf16[144,128]{1,0:T(8,128)(2,1)S(1)}, u32[]{:S(2)}, u32[]{:S(2)}) %collective-permute-start.10) | collective-permute-done | bytes 36896 | tf_op jit(solution)/shard_map/ppermute | solution.py:259
  29.7 1.9 %collective-permute-done.11.refs_3_ = bf16[144,128]{1,0:T(8,128)(2,1)S(1)} collective-permute-done((bf16[144,128]{1,0:T(8,128)(2,1)S(1)}, bf16[144,128]{1,0:T(8,128)(2,1)S(1)}, u32[]{:S(2)}, u32[]{:S(2)}) %collective-permute-start.11) | collective-permute-done | bytes 36896 | tf_op jit(solution)/shard_map/ppermute | solution.py:259
  31.5 0.0 copy-done
  31.5 0.7 %shard_map.130 = (f32[64,2048]{1,0:T(8,128)S(1)}, bf16[64,2048]{1,0:T(8,128)(2,1)S(1)}) custom-call(f32[512,128]{1,0:T(8,128)S(1)} %get-tuple-element.33.sum_ref, f32[8,128]{1,0:T(8,128)S(1)} %get-tuple-element.34.log_ref, bf16[512,2048]{1,0:T(8,128)(2,1)S(1)} %copy-done, bf16[144,128]{1,0:T(8,128)(2,1)S(1)} %collective-permute-done.8.refs_0_, ...), custom_call_target="tpu_custom_call" | custom-call | tf_op jit(solution)/shard_map/pallas_call | solution.py:213
  32.2 0.1 collective-permute-start.12
  32.3 1.5 %collective-permute-done.12 = bf16[64,2048]{1,0:T(8,128)(2,1)S(1)} collective-permute-done((bf16[64,2048]{1,0:T(8,128)(2,1)S(1)}, bf16[64,2048]{1,0:T(8,128)(2,1)S(1)}, u32[]{:S(2)}, u32[]{:S(2)}) %collective-permute-start.12) | collective-permute-done | bytes 262176 | tf_op jit(solution)/shard_map/ppermute | solution.py:265
  33.8 2.1 %collective-permute-start.13 = (bf16[64,2048]{1,0:T(8,128)(2,1)S(1)}, bf16[64,2048]{1,0:T(8,128)(2,1)S(1)}, u32[]{:S(2)}, u32[]{:S(2)}) collective-permute-start(bf16[64,2048]{1,0:T(8,128)(2,1)S(1)} %add_convert_fusion.1), channel_id=1, source_target_pairs={{0,2},{1,3},{2,0},{3,1},{4,6},{5,7},{6,4},{7,5},{8,10},{9,11},{10,... | collective-permute-start | bytes 786440 | tf_op jit(solution)/shard_map/ppermute | solution.py:265
  35.9 6.6 %collective-permute-done.13 = bf16[64,2048]{1,0:T(8,128)(2,1)S(1)} collective-permute-done((bf16[64,2048]{1,0:T(8,128)(2,1)S(1)}, bf16[64,2048]{1,0:T(8,128)(2,1)S(1)}, u32[]{:S(2)}, u32[]{:S(2)}) %collective-permute-start.13) | collective-permute-done | bytes 262176 | tf_op jit(solution)/shard_map/ppermute | solution.py:265
  42.5 0.0 copy-done.1
  42.5 0.1 add_convert_fusion
  42.6 0.1 collective-permute-start.14
  42.7 1.5 %collective-permute-done.14 = bf16[64,2048]{1,0:T(8,128)(2,1)S(1)} collective-permute-done((bf16[64,2048]{1,0:T(8,128)(2,1)S(1)}, bf16[64,2048]{1,0:T(8,128)(2,1)S(1)}, u32[]{:S(2)}, u32[]{:S(2)}) %collective-permute-start.14) | collective-permute-done | bytes 262176 | tf_op jit(solution)/shard_map/ppermute | solution.py:265
  44.3 0.8 %pad_maximum_fusion = bf16[128,2048]{1,0:T(8,128)(2,1)} fusion(bf16[64,2048]{1,0:T(8,128)(2,1)S(1)} %get-tuple-element.46, bf16[64,2048]{1,0:T(8,128)(2,1)S(1)} %get-tuple-element.45), kind=kLoop, calls=%fused_computation | loop fusion | flops 1048576 | bytes 1048576 | tf_op jit(solution)/shard_map/concatenate | solution.py:335
  (3 shorter events, 0.1 us)
Async XLA Ops:
  3.7 11.3 %collective-permute-start = (bf16[400,128]{1,0:T(8,128)(2,1)S(1)}, bf16[400,128]{1,0:T(8,128)(2,1)S(1)}, u32[]{:S(2)}, u32[]{:S(2)}) collective-permute-start(bf16[400,128]{1,0:T(8,128)(2,1)S(1)} %get-tuple-element.25), channel_id=1, source_target_pairs={{0,1},{1,5},{2,3},{3,7},{4,0},{5,4},{6,2},{7,6},{8,9},{9,13},{10,1... | collective-permute-start | bytes 307208 | tf_op jit(solution)/shard_map/ppermute | solution.py:259
  4.2 10.8 %collective-permute-start.1 = (bf16[400,128]{1,0:T(8,128)(2,1)S(1)}, bf16[400,128]{1,0:T(8,128)(2,1)S(1)}, u32[]{:S(2)}, u32[]{:S(2)}) collective-permute-start(bf16[400,128]{1,0:T(8,128)(2,1)S(1)} %get-tuple-element.26), channel_id=1, source_target_pairs={{0,9},{1,13},{2,11},{3,15},{4,8},{5,12},{6,10},{7,14},{8,17},{9,21... | collective-permute-start | bytes 307208 | tf_op jit(solution)/shard_map/ppermute | solution.py:259
  7.4 10.4 %collective-permute-start.2 = (bf16[400,128]{1,0:T(8,128)(2,1)S(1)}, bf16[400,128]{1,0:T(8,128)(2,1)S(1)}, u32[]{:S(2)}, u32[]{:S(2)}) collective-permute-start(bf16[400,128]{1,0:T(8,128)(2,1)S(1)} %get-tuple-element.27), channel_id=1, source_target_pairs={{0,17},{1,21},{2,19},{3,23},{4,16},{5,20},{6,18},{7,22},{8,25},{9,... | collective-permute-start | bytes 307208 | tf_op jit(solution)/shard_map/ppermute | solution.py:259
  10.1 8.1 %collective-permute-start.3 = (bf16[400,128]{1,0:T(8,128)(2,1)S(1)}, bf16[400,128]{1,0:T(8,128)(2,1)S(1)}, u32[]{:S(2)}, u32[]{:S(2)}) collective-permute-start(bf16[400,128]{1,0:T(8,128)(2,1)S(1)} %get-tuple-element.28), channel_id=1, source_target_pairs={{0,25},{1,29},{2,27},{3,31},{4,24},{5,28},{6,26},{7,30},{8,1},{9,5... | collective-permute-start | bytes 307208 | tf_op jit(solution)/shard_map/ppermute | solution.py:259
  11.6 19.9 %copy-start = (bf16[512,2048]{1,0:T(8,128)(2,1)S(1)}, bf16[512,2048]{1,0:T(8,128)(2,1)}, u32[]{:S(2)}) copy-start(bf16[512,2048]{1,0:T(8,128)(2,1)} %w_out_ref.1) | copy-start | bytes 6291460
  18.3 24.3 %copy-start.1 = (bf16[128,2048]{1,0:T(8,128)(2,1)S(1)}, bf16[128,2048]{1,0:T(8,128)(2,1)}, u32[]{:S(2)}) copy-start(bf16[128,2048]{1,0:T(8,128)(2,1)} %refs_3_.1) | copy-start | bytes 1572868
  18.3 1.3 %collective-permute-start.4 = (bf16[400,128]{1,0:T(8,128)(2,1)S(1)}, bf16[400,128]{1,0:T(8,128)(2,1)S(1)}, u32[]{:S(2)}, u32[]{:S(2)}) collective-permute-start(bf16[400,128]{1,0:T(8,128)(2,1)S(1)} %collective-permute-done.refs_0_), channel_id=1, source_target_pairs={{0,1},{1,0},{2,3},{3,2},{4,5},{5,4},{6,7},{7,6},{8,9},{9,8},{10,11... | collective-permute-start | bytes 307208 | tf_op jit(solution)/shard_map/ppermute | solution.py:265
  18.3 1.5 %collective-permute-start.5 = (bf16[400,128]{1,0:T(8,128)(2,1)S(1)}, bf16[400,128]{1,0:T(8,128)(2,1)S(1)}, u32[]{:S(2)}, u32[]{:S(2)}) collective-permute-start(bf16[400,128]{1,0:T(8,128)(2,1)S(1)} %collective-permute-done.1.refs_1_), channel_id=1, source_target_pairs={{0,1},{1,0},{2,3},{3,2},{4,5},{5,4},{6,7},{7,6},{8,9},{9,8},{10,11... | collective-permute-start | bytes 307208 | tf_op jit(solution)/shard_map/ppermute | solution.py:265
  18.8 1.3 %collective-permute-start.6 = (bf16[400,128]{1,0:T(8,128)(2,1)S(1)}, bf16[400,128]{1,0:T(8,128)(2,1)S(1)}, u32[]{:S(2)}, u32[]{:S(2)}) collective-permute-start(bf16[400,128]{1,0:T(8,128)(2,1)S(1)} %collective-permute-done.2.refs_2_), channel_id=1, source_target_pairs={{0,1},{1,0},{2,3},{3,2},{4,5},{5,4},{6,7},{7,6},{8,9},{9,8},{10,11... | collective-permute-start | bytes 307208 | tf_op jit(solution)/shard_map/ppermute | solution.py:265
  18.8 1.5 %collective-permute-start.7 = (bf16[400,128]{1,0:T(8,128)(2,1)S(1)}, bf16[400,128]{1,0:T(8,128)(2,1)S(1)}, u32[]{:S(2)}, u32[]{:S(2)}) collective-permute-start(bf16[400,128]{1,0:T(8,128)(2,1)S(1)} %collective-permute-done.3.refs_3_), channel_id=1, source_target_pairs={{0,1},{1,0},{2,3},{3,2},{4,5},{5,4},{6,7},{7,6},{8,9},{9,8},{10,11... | collective-permute-start | bytes 307208 | tf_op jit(solution)/shard_map/ppermute | solution.py:265
  21.5 5.4 %collective-permute-start.8 = (bf16[144,128]{1,0:T(8,128)(2,1)S(1)}, bf16[144,128]{1,0:T(8,128)(2,1)S(1)}, u32[]{:S(2)}, u32[]{:S(2)}) collective-permute-start(bf16[144,128]{1,0:T(8,128)(2,1)S(1)} %get-tuple-element.39), channel_id=1, source_target_pairs={{1,0},{5,1},{3,2},{7,3},{0,4},{4,5},{2,6},{6,7},{9,8},{13,9},{11,1... | collective-permute-start | bytes 110600 | tf_op jit(solution)/shard_map/ppermute | solution.py:259
  21.9 5.3 %collective-permute-start.9 = (bf16[144,128]{1,0:T(8,128)(2,1)S(1)}, bf16[144,128]{1,0:T(8,128)(2,1)S(1)}, u32[]{:S(2)}, u32[]{:S(2)}) collective-permute-start(bf16[144,128]{1,0:T(8,128)(2,1)S(1)} %get-tuple-element.40), channel_id=1, source_target_pairs={{9,0},{13,1},{11,2},{15,3},{8,4},{12,5},{10,6},{14,7},{17,8},{21,9... | collective-permute-start | bytes 110600 | tf_op jit(solution)/shard_map/ppermute | solution.py:259
  25.4 4.3 %collective-permute-start.10 = (bf16[144,128]{1,0:T(8,128)(2,1)S(1)}, bf16[144,128]{1,0:T(8,128)(2,1)S(1)}, u32[]{:S(2)}, u32[]{:S(2)}) collective-permute-start(bf16[144,128]{1,0:T(8,128)(2,1)S(1)} %get-tuple-element.41), channel_id=1, source_target_pairs={{17,0},{21,1},{19,2},{23,3},{16,4},{20,5},{18,6},{22,7},{25,8},{29... | collective-permute-start | bytes 110600 | tf_op jit(solution)/shard_map/ppermute | solution.py:259
  26.3 5.2 %collective-permute-start.11 = (bf16[144,128]{1,0:T(8,128)(2,1)S(1)}, bf16[144,128]{1,0:T(8,128)(2,1)S(1)}, u32[]{:S(2)}, u32[]{:S(2)}) collective-permute-start(bf16[144,128]{1,0:T(8,128)(2,1)S(1)} %get-tuple-element.42), channel_id=1, source_target_pairs={{25,0},{29,1},{27,2},{31,3},{24,4},{28,5},{26,6},{30,7},{1,8},{5,9... | collective-permute-start | bytes 110600 | tf_op jit(solution)/shard_map/ppermute | solution.py:259
  32.2 1.6 %collective-permute-start.12 = (bf16[64,2048]{1,0:T(8,128)(2,1)S(1)}, bf16[64,2048]{1,0:T(8,128)(2,1)S(1)}, u32[]{:S(2)}, u32[]{:S(2)}) collective-permute-start(bf16[64,2048]{1,0:T(8,128)(2,1)S(1)} %get-tuple-element.44), channel_id=1, source_target_pairs={{0,1},{1,0},{2,3},{3,2},{4,5},{5,4},{6,7},{7,6},{8,9},{9,8},{10,11... | collective-permute-start | bytes 786440 | tf_op jit(solution)/shard_map/ppermute | solution.py:265
  33.8 8.7 %collective-permute-start.13 = (bf16[64,2048]{1,0:T(8,128)(2,1)S(1)}, bf16[64,2048]{1,0:T(8,128)(2,1)S(1)}, u32[]{:S(2)}, u32[]{:S(2)}) collective-permute-start(bf16[64,2048]{1,0:T(8,128)(2,1)S(1)} %add_convert_fusion.1), channel_id=1, source_target_pairs={{0,2},{1,3},{2,0},{3,1},{4,6},{5,7},{6,4},{7,5},{8,10},{9,11},{10,... | collective-permute-start | bytes 786440 | tf_op jit(solution)/shard_map/ppermute | solution.py:265
  42.6 1.6 %collective-permute-start.14 = (bf16[64,2048]{1,0:T(8,128)(2,1)S(1)}, bf16[64,2048]{1,0:T(8,128)(2,1)S(1)}, u32[]{:S(2)}, u32[]{:S(2)}) collective-permute-start(bf16[64,2048]{1,0:T(8,128)(2,1)S(1)} %add_convert_fusion), channel_id=1, source_target_pairs={{0,1},{1,0},{2,3},{3,2},{4,5},{5,4},{6,7},{7,6},{8,9},{9,8},{10,11... | collective-permute-start | bytes 786440 | tf_op jit(solution)/shard_map/ppermute | solution.py:265

commit v3 on v2

v3 whole, which is shorter than its diff:
```python
import functools

import jax
import jax.numpy as jnp
from jax import lax
from jax.experimental import pallas as pl
from jax.experimental.pallas import tpu as pltpu
from jax.sharding import PartitionSpec as P

HD = 128
GROUPS = 4
NOTE_ROWS = 16
ASK_ROWS = NOTE_ROWS + 128
W_CUTS = 4
ROW_CUTS = 2

big = 1e30

VMEM = pl.BlockSpec(memory_space=pltpu.VMEM)
HBM = pl.BlockSpec(memory_space=pltpu.HBM)
NT = (((1,), (1,)), ((), ()))
TN = (((0,), (0,)), ((), ()))


def dot(a, b, dims=(((1,), (0,)), ((), ()))):
    return lax.dot_general(a, b, dims, preferred_element_type=jnp.float32)


def head_at(rest, bits):
    part = lax.div(lax.axis_index("blk"), rest)
    return pl.multiple_of((part ^ bits) * HD, HD)


def start_all(pairs, sems):
    copies = [pltpu.make_async_copy(a, b, sems.at[i]) for i, (a, b) in enumerate(pairs)]
    for copy in copies:
        copy.start()
    return copies


def block_copies(rest, bits, keys_ref, values_ref, out, at):
    cols = pl.ds(head_at(rest, bits), HD)
    return [
        (keys_ref.at[0, :, cols], out.at[at : at + HD, :]),
        (values_ref.at[0, :, cols], out.at[at + HD : at + 2 * HD, :]),
    ]


def query_kernel(heads, rest, *refs):
    keys_ref, values_ref, tag_ref, hidden_in, w_query, *sources = refs[:9]
    normed_ref, query_ref = refs[9:11]
    outs, held, sems = refs[11 : 11 + heads], refs[11 + heads : -1], refs[-1]
    hidden_ref, w_query_ref, gain_ref, bias_ref, segment_ref, request_group_ref = held
    rows, width = hidden_ref.shape
    row_cuts = [pl.ds(i * (rows // ROW_CUTS), rows // ROW_CUTS) for i in range(ROW_CUTS)]
    w_cuts = [pl.ds(i * (width // W_CUTS), width // W_CUTS) for i in range(W_CUTS)]
    pairs = [(hidden_in.at[cut, :], hidden_ref.at[cut, :]) for cut in row_cuts]
    pairs += list(zip(sources, held[2:]))
    pairs += [(w_query.at[cut, :], w_query_ref.at[cut, :]) for cut in w_cuts]
    for k, out in enumerate(outs):
        pairs += block_copies(rest, k, keys_ref, values_ref, out, NOTE_ROWS + rows)
    copies = start_all(pairs, sems)
    small = copies[ROW_CUTS : ROW_CUTS + 4]
    weights = copies[ROW_CUTS + 4 : ROW_CUTS + 4 + W_CUTS]
    for cut, copy in zip(row_cuts, copies):
        copy.wait()
        if cut is row_cuts[0]:
            small[0].wait()
            small[1].wait()
        inputs = hidden_ref[cut, :].astype(jnp.float32)
        mean = jnp.mean(inputs, axis=-1, keepdims=True)
        centred = inputs - mean
        var = jnp.mean(centred * centred, axis=-1, keepdims=True)
        normed = centred * lax.rsqrt(var + 1e-05) * gain_ref[...] + bias_ref[...]
        normed_ref[cut, :] = normed.astype(jnp.bfloat16)
    small[2].wait()
    small[3].wait()
    segment = segment_ref[...]
    group = jnp.zeros_like(segment)
    for r in range(request_group_ref.shape[1]):
        group = jnp.where(segment == r, request_group_ref[0, r], group)
    tag = tag_ref[...].astype(jnp.float32)
    place = lax.broadcasted_iota(jnp.int32, tag.shape, 0)
    notes = jnp.where(place == 0, tag, group.astype(jnp.float32)).astype(jnp.bfloat16)
    query = jnp.zeros(query_ref.shape, jnp.float32)
    for cut, copy in zip(w_cuts, weights):
        copy.wait()
        query = query + dot(normed_ref[:, cut], w_query_ref[cut, :])
    query_ref[...] = (query * (HD**-0.5)).astype(jnp.bfloat16)
    for k, out in enumerate(outs):
        out[0:NOTE_ROWS, :] = notes
        out[NOTE_ROWS : NOTE_ROWS + rows, :] = query_ref[:, pl.ds(head_at(rest, k), HD)]
    for copy in copies[ROW_CUTS + 4 + W_CUTS :]:
        copy.wait()


def suffix_kernel(heads, normed_ref, query_ref, *refs):
    sources, (sum_ref, log_ref), held, sems = refs[:3], refs[3:5], refs[5:8], refs[8]
    segment_ref, w_key_ref, w_value_ref = held
    rows, width = normed_ref.shape
    cut = width // W_CUTS
    pairs = [(sources[0], held[0])]
    for source, target in zip(sources[1:], held[1:]):
        parts = [pl.ds(i * cut, cut) for i in range(W_CUTS)]
        pairs += [(source.at[part, :], target.at[part, :]) for part in parts]
    copies = start_all(pairs, sems)

    def project(target, waits):
        out = jnp.zeros((rows, target.shape[1]), jnp.float32)
        for i, copy in enumerate(waits):
            copy.wait()
            at = slice(i * cut, (i + 1) * cut)
            out = out + dot(normed_ref[:, at], target[at, :])
        return out.astype(jnp.bfloat16)

    key = project(w_key_ref, copies[1 : 1 + W_CUTS])
    value = project(w_value_ref, copies[1 + W_CUTS :])
    copies[0].wait()
    by_token = jnp.broadcast_to(segment_ref[...], (rows, rows))
    key_place = lax.broadcasted_iota(jnp.int32, (rows, rows), 0)
    token_place = lax.broadcasted_iota(jnp.int32, (rows, rows), 1)
    by_key = jnp.sum(
        jnp.where(key_place == token_place, by_token, 0).astype(jnp.float32), axis=1, keepdims=True
    )
    mask = (by_key == by_token.astype(jnp.float32)) & (key_place <= token_place)
    for h in range(heads):
        cols = slice(h * HD, (h + 1) * HD)
        scores = jnp.where(mask, dot(key[:, cols], query_ref[:, cols], NT), -big)
        top = jnp.max(scores, axis=0, keepdims=True)
        weights = jnp.exp(scores - top)
        total = jnp.sum(weights, axis=0, keepdims=True)
        summed = dot(value[:, cols], weights.astype(jnp.bfloat16), TN)
        sum_ref[cols, :] = summed / total
        log_ref[h : h + 1, :] = top + jnp.log(total)


def absorb(carry, found):
    top, total, summed = carry
    new_top = top
    for scores, mask, _ in found:
        best = jnp.max(scores, axis=0, keepdims=True)
        new_top = jnp.maximum(new_top, jnp.where(mask, best, -big))
    factor = jnp.exp(top - new_top)
    total, summed = total * factor, summed * factor
    for scores, mask, values in found:
        weights = jnp.exp(scores - jnp.where(mask, new_top, big))
        total = total + jnp.sum(weights, axis=0, keepdims=True)
        summed = summed + dot(values, weights.astype(jnp.bfloat16), TN)
    return new_top, total, summed


def questions(asks, rows):
    query = jnp.concatenate([ref[NOTE_ROWS : NOTE_ROWS + rows, :] for ref in asks], axis=0)
    notes = [ref[0:NOTE_ROWS, :].astype(jnp.float32) for ref in asks]
    return query, jnp.concatenate([note[1:2, :] for note in notes], axis=1), notes


def first_kernel(rows, *refs):
    asks, (state_ref, sum_ref) = refs[:-2], refs[-2:]
    query, group, notes = questions(asks, rows)
    tokens = query.shape[0]
    found = []
    at = NOTE_ROWS + rows
    for ref, note in zip(asks, notes):
        scores = dot(ref[at : at + HD, :], query, NT)
        found.append((scores, group == note[0:1, 0:1], ref[at + HD : at + 2 * HD, :]))
    carry = (
        jnp.full((1, tokens), -big, jnp.float32),
        jnp.zeros((1, tokens), jnp.float32),
        jnp.zeros((HD, tokens), jnp.float32),
    )
    top, total, summed = absorb(carry, found)
    state_ref[0:1, :] = top
    state_ref[1:2, :] = total
    sum_ref[...] = summed


def second_kernel(rows, n_asks, *refs):
    asks, state_ref, sum_ref, notes_ref = refs[:n_asks], *refs[n_asks : n_asks + 3]
    blocks, outs = refs[n_asks + 3 : -n_asks], refs[-n_asks:]
    query, group, _ = questions(asks, rows)
    tokens = query.shape[0]

    def one(ref, at, place):
        tag = notes_ref[pl.ds(place, NOTE_ROWS), :].astype(jnp.float32)[0:1, 0:1]
        return dot(ref[pl.ds(at, HD), :], query, NT), group == tag, ref[pl.ds(at + HD, HD), :]

    carry = (state_ref[0:1, :], state_ref[1:2, :], sum_ref[...])
    singles, place = [], 0
    for ref in blocks:
        held = ref.shape[0] // (2 * HD)
        if held == 1:
            singles.append(one(ref, 0, place))
        place += held * NOTE_ROWS
    carry = absorb(carry, singles)
    place = 0
    for ref in blocks:
        held = ref.shape[0] // (2 * HD)
        if held > 1:

            def body(i, state, ref=ref, place=place):
                at = pl.multiple_of(i * 2 * HD, HD)
                return absorb(state, [one(ref, at, pl.multiple_of(place + i * NOTE_ROWS, NOTE_ROWS))])

            carry = lax.fori_loop(0, held, body, carry)
        place += held * NOTE_ROWS
    top, total, summed = carry
    found = total > 0.0
    summed = summed * jnp.where(found, 1.0 / jnp.where(found, total, 1.0), 0.0)
    log = jnp.where(found, top + jnp.log(jnp.where(found, total, 1.0)), -big)
    first = log.astype(jnp.bfloat16).astype(jnp.float32)
    second = (log - first).astype(jnp.bfloat16).astype(jnp.float32)
    third = log - first - second
    place = lax.broadcasted_iota(jnp.int32, (NOTE_ROWS, tokens), 0)
    logs = jnp.where(place == 0, first, jnp.where(place == 1, second, jnp.where(place == 2, third, 0.0)))
    for k, out in enumerate(outs):
        cols = slice(k * rows, (k + 1) * rows)
        out[0:HD, :] = summed[:, cols].astype(jnp.bfloat16)
        out[HD : HD + NOTE_ROWS, :] = logs[:, cols].astype(jnp.bfloat16)


def project_kernel(rest, order, sum_ref, log_ref, w_out_ref, *refs):
    backs = refs[: len(order)]
    keep_ref, send_ref, attended, branch = refs[len(order) :]
    for bits, back in zip(order, backs):
        at = head_at(rest, bits)
        logs = back[HD : HD + NOTE_ROWS, :].astype(jnp.float32)
        prefix_log = logs[0:1, :] + logs[1:2, :] + logs[2:3, :]
        suffix_log = log_ref[pl.ds(lax.div(at, HD), 1), :]
        top = jnp.maximum(prefix_log, suffix_log)
        prefix_part = jnp.exp(prefix_log - top)
        suffix_part = jnp.exp(suffix_log - top)
        whole = prefix_part + suffix_part
        joined = (
            back[0:HD, :].astype(jnp.float32) * (prefix_part / whole)
            + sum_ref[pl.ds(at, HD), :] * (suffix_part / whole)
        )
        attended[pl.ds(at, HD), :] = joined.astype(jnp.bfloat16)
    branch[...] = dot(attended[...], w_out_ref[...], TN)
    half = keep_ref.shape[0]
    side = lax.rem(lax.axis_index("mp"), 2)
    keep_ref[...] = branch[pl.ds(pl.multiple_of(side * half, half), half), :]
    other = branch[pl.ds(pl.multiple_of((1 - side) * half, half), half), :]
    send_ref[...] = other.astype(jnp.bfloat16)


def own_half_kernel(half_ref, out_ref, sem):
    half = half_ref.shape[0]
    side = lax.rem(lax.axis_index("mp"), 2)
    rows = pl.ds(pl.multiple_of(side * half, half), half)
    copy = pltpu.make_async_copy(half_ref, out_ref.at[rows, :], sem.at[0])
    copy.start()
    copy.wait()


def other_half_kernel(half_ref, _, out_ref, sem):
    half = half_ref.shape[0]
    side = lax.rem(lax.axis_index("mp"), 2)
    rows = pl.ds(pl.multiple_of((1 - side) * half, half), half)
    copy = pltpu.make_async_copy(half_ref, out_ref.at[rows, :], sem.at[0])
    copy.start()
    copy.wait()


def call(kernel, outs, specs, scratch=(), out_specs=None, aliases=None):
    def run(*args):
        pinned = [
            pltpu.with_memory_space_constraint(x, pltpu.HBM) if spec is HBM else x
            for x, spec in zip(args, specs)
        ]
        return inner(*pinned)

    inner = pl.pallas_call(
        kernel,
        out_shape=tuple(jax.ShapeDtypeStruct(s, t) for s, t in outs),
        in_specs=specs,
        out_specs=out_specs or (VMEM,) * len(outs),
        scratch_shapes=scratch,
        input_output_aliases=aliases or {},
        compiler_params=pltpu.CompilerParams(vmem_limit_bytes=40 * 1024 * 1024),
    )
    return run


def local(
    hidden_in,
    norm_gain,
    norm_bias,
    w_query,
    w_key,
    w_value,
    w_out,
    prefix_keys,
    prefix_values,
    segment,
    request_group,
    block_slot,
    block_live,
):
    bf16, f32, i32 = jnp.bfloat16, jnp.float32, jnp.int32
    rows, width = hidden_in.shape
    local_width = w_query.shape[1]
    heads = local_width // HD
    n_blk = lax.axis_size("blk")
    n_mp = lax.axis_size("mp")
    rest = n_blk // heads
    side = lax.rem(lax.axis_index("mp"), 2)
    order = tuple(reversed(range(heads)))

    def exchange(x, bits, back=False):
        pairs = []
        for i in range(n_blk):
            part, place, lane = i // rest, i % rest // 2, i % 2
            for m in range(n_mp):
                other, core = m // 2, m % 2
                blk = (part ^ bits) * rest + place * 2 + core
                pair = (i * n_mp + m, blk * n_mp + other * 2 + 1 - lane)
                pairs.append(pair[::-1] if back else pair)
        return lax.ppermute(x, ("blk", "mp"), pairs)

    def across(x, bit):
        return lax.ppermute(x, "blk", [(i, i ^ bit) for i in range(n_blk)])

    def across_mp(x, bit):
        return lax.ppermute(x, "mp", [(i, i ^ bit) for i in range(n_mp)])

    group = jnp.where(block_live == 1, block_slot * GROUPS // n_blk, -1).astype(bf16)
    normed, query, *packs = call(
        functools.partial(query_kernel, heads, rest),
        [((rows, width), bf16), ((rows, local_width), bf16)]
        + [((NOTE_ROWS + rows + 2 * HD, HD), bf16)] * heads,
        (HBM, HBM, VMEM) + (HBM,) * 6,
        [
            pltpu.VMEM((rows, width), bf16),
            pltpu.VMEM(w_query.shape, bf16),
            pltpu.VMEM((1, width), f32),
            pltpu.VMEM((1, width), f32),
            pltpu.VMEM(segment.shape, i32),
            pltpu.SMEM(request_group.shape, i32),
            pltpu.SemaphoreType.DMA((4 + ROW_CUTS + W_CUTS + 2 * heads,)),
        ],
    )(
        prefix_keys,
        prefix_values,
        jnp.broadcast_to(group, (NOTE_ROWS, HD)),
        hidden_in,
        w_query,
        norm_gain.reshape(1, width),
        norm_bias.reshape(1, width),
        segment,
        request_group,
    )
    asks = [exchange(packs[k], k) for k in order]
    suffix_sum, suffix_log = call(
        functools.partial(suffix_kernel, heads),
        [((local_width, rows), f32), ((max(heads, 8), rows), f32)],
        (VMEM,) * 2 + (HBM,) * 3,
        [
            pltpu.VMEM(segment.shape, i32),
            pltpu.VMEM(w_key.shape, bf16),
            pltpu.VMEM(w_value.shape, bf16),
            pltpu.SemaphoreType.DMA((1 + 2 * W_CUTS,)),
        ],
    )(normed, query, segment, w_key, w_value)
    asks, suffix_sum, suffix_log = lax.optimization_barrier((asks, suffix_sum, suffix_log))

    blocks = [x[NOTE_ROWS + rows :] for x in asks]
    notes = jnp.concatenate([x[:NOTE_ROWS] for x in asks], axis=0)
    state, summed = call(
        functools.partial(first_kernel, rows),
        [((8, heads * rows), f32), ((HD, heads * rows), f32)],
        (VMEM,) * heads,
    )(*asks)
    others = [across_mp(x, 1) for x in blocks]
    other_notes = across_mp(notes, 1)
    bit = 2
    while bit < rest:
        everything = jnp.concatenate(blocks + others, axis=0)
        all_notes = jnp.concatenate([notes, other_notes], axis=0)
        others = others + [across(everything, bit)]
        other_notes = jnp.concatenate([other_notes, across(all_notes, bit)], axis=0)
        bit *= 2
    backs = call(
        functools.partial(second_kernel, rows, heads),
        [((HD + NOTE_ROWS, rows), bf16)] * heads,
        (VMEM,) * (heads + 3 + len(others)),
    )(*asks, state, summed, other_notes, *others)
    backs = [exchange(x, k, back=True) for k, x in zip(order, backs)]

    keep, send = call(
        functools.partial(project_kernel, rest, order),
        [((rows // 2, width), f32), ((rows // 2, width), bf16)],
        (VMEM,) * (3 + heads),
        [pltpu.VMEM((local_width, rows), bf16), pltpu.VMEM((rows, width), f32)],
    )(suffix_sum, suffix_log, w_out, *backs)

    mine = (keep + across_mp(send, 1).astype(f32)).astype(bf16)
    bit = 2
    while bit < n_mp:
        mine = (mine.astype(f32) + across_mp(mine, bit).astype(f32)).astype(bf16 if 2 * bit < n_mp else f32)
        bit *= 2
    inputs = lax.dynamic_slice_in_dim(hidden_in, side * (rows // 2), rows // 2, 0)
    done = (inputs.astype(f32) + mine.astype(f32)).astype(bf16)
    other = across_mp(done, 1)
    whole = call(
        own_half_kernel,
        [((rows, width), bf16)],
        (VMEM,),
        [pltpu.SemaphoreType.DMA((1,))],
        (HBM,),
    )(done)[0]
    return call(
        other_half_kernel,
        [((rows, width), bf16)],
        (VMEM, HBM),
        [pltpu.SemaphoreType.DMA((1,))],
        (HBM,),
        {1: 0},
    )(other, whole)[0]


def solution(mesh):
    return jax.shard_map(
        local,
        mesh=mesh,
        in_specs=(
            P("blk", None),
            P(),
            P(),
            P(None, "mp"),
            P(None, "mp"),
            P(None, "mp"),
            P("mp", None),
            P("blk", None, "mp"),
            P("blk", None, "mp"),
            P("blk", None),
            P("blk", None),
            P("blk"),
            P("blk"),
        ),
        out_specs=P("blk", None),
        check_vma=False,
    )
```

time: 45.3 us -> 42.6 us (0.940)
  waiting for transfers between devices: 18.5 us -> 16.6 us
  starting transfers between devices: 16.5 us -> 14.9 us
  Pallas kernels: 7.66 us -> 9.25 us
  other arithmetic: 1.03 us -> 0.15 us
    pallas_call x4 -> x7, Pallas kernels: 7.66 us -> 9.25 us  [run(): return inner(*pinned)]
    ppermute x8, starting transfers between devices: 13.3 us -> 11.9 us  [exchange(): return lax.ppermute(x, ('blk', 'mp'), pairs)]
    ppermute x7 -> x8, waiting for transfers between devices: 10.6 us -> 9.45 us  [across_mp(): return lax.ppermute(x, 'mp', [(i, i ^ bit) for i in range(n_mp)])]
    concatenate x1, other arithmetic: 0.84 us -> 0.01 us  [local(): notes = jnp.concatenate([x[:NOTE_ROWS] for x in asks], axis=0)]
    ppermute x8, waiting for transfers between devices: 7.91 us -> 7.12 us  [exchange(): return lax.ppermute(x, ('blk', 'mp'), pairs)]
    ppermute x7 -> x8, starting transfers between devices: 3.23 us -> 3.03 us  [across_mp(): return lax.ppermute(x, 'mp', [(i, i ^ bit) for i in range(n_mp)])]
  transfers between devices with their start and end apart: 15 -> 16, of which waited for: 12 -> 7; matrix products, arithmetic and copies ran while one was open for 0% -> 0% of each run, Pallas kernels for 8% -> 11%
where the time goes in v3:
time: 42.6 us; the launch traced here: 42.4 us
  waiting for transfers between devices  16.6 us (39%)
  starting transfers between devices  14.9 us (35%)
  Pallas kernels  9.25 us (22%)
  between operations  1.51 us (4%)
    ppermute x8, starting transfers between devices, exchange(): return lax.ppermute(x, ('blk', 'mp'), pairs)  11.9 us
    ppermute x8, waiting for transfers between devices, across_mp(): return lax.ppermute(x, 'mp', [(i, i ^ bit) for i in range(n_mp)])  9.45 us
    pallas_call x7, Pallas kernels, run(): return inner(*pinned)  9.25 us
    ppermute x8, waiting for transfers between devices, exchange(): return lax.ppermute(x, ('blk', 'mp'), pairs)  7.12 us
    ppermute x8, starting transfers between devices, across_mp(): return lax.ppermute(x, 'mp', [(i, i ^ bit) for i in range(n_mp)])  3.03 us
  transfers between devices with their start and end apart: 16, of which 7 were waited for; matrix products, arithmetic and copies ran while one was open for 0% of the time, Pallas kernels for 11%

profile of v3, /device:TPU:0, one launch (start us, length us, event | category | flops | bytes accessed | tf_op | source)
XLA Modules:
  0.0 42.4 jit_solution(966879590544522277)
XLA Ops:
  1.3 2.3 %shard_map.127 = (bf16[128,2048]{1,0:T(8,128)(2,1)S(1)}, bf16[128,512]{1,0:T(8,128)(2,1)S(1)}, bf16[400,128]{1,0:T(8,128)(2,1)S(1)}, bf16[400,128]{1,0:T(8,128)(...) custom-call(bf16[1,128,512]{2,1,0:T(8,128)(2,1)} %refs_0_.2, bf16[1,128,512]{2,1,0:T(8,128)(2,1)} %refs_1_.2, ...), custom_call_target="tpu_custom_call" | custom-call | tf_op jit(solution)/shard_map/pallas_call | solution.py:271
  3.7 4.5 %collective-permute-start = (bf16[400,128]{1,0:T(8,128)(2,1)S(1)}, bf16[400,128]{1,0:T(8,128)(2,1)S(1)}, u32[]{:S(2)}, u32[]{:S(2)}) collective-permute-start(bf16[400,128]{1,0:T(8,128)(2,1)S(1)} %get-tuple-element.27), channel_id=1, source_target_pairs={{0,25},{1,29},{2,27},{3,31},{4,24},{5,28},{6,26},{7,30},{8,17},{9,... | collective-permute-start | bytes 307208 | tf_op jit(solution)/shard_map/ppermute | solution.py:319
  8.2 0.1 collective-permute-start.1
  8.3 1.6 %collective-permute-start.2 = (bf16[400,128]{1,0:T(8,128)(2,1)S(1)}, bf16[400,128]{1,0:T(8,128)(2,1)S(1)}, u32[]{:S(2)}, u32[]{:S(2)}) collective-permute-start(bf16[400,128]{1,0:T(8,128)(2,1)S(1)} %get-tuple-element.29), channel_id=1, source_target_pairs={{0,9},{1,13},{2,11},{3,15},{4,8},{5,12},{6,10},{7,14},{8,1},{9,5},... | collective-permute-start | bytes 307208 | tf_op jit(solution)/shard_map/ppermute | solution.py:319
  9.9 0.2 collective-permute-start.3
  10.2 0.0 copy-start
  10.2 3.4 %shard_map.128 = (f32[512,128]{1,0:T(8,128)S(1)}, f32[8,128]{1,0:T(8,128)S(1)}) custom-call(bf16[128,2048]{1,0:T(8,128)(2,1)S(1)} %get-tuple-element.31.normed_ref, bf16[128,512]{1,0:T(8,128)(2,1)S(1)} %get-tuple-element.32.query_ref, s32[1,128]{1,0:T(1,128)} %refs_0_.3, bf16[2048,512]{1,0:T(8,128)(2,1)} %refs_1_.3, bf16[2048,512]{1,0:T(8,128)(2,1)} %refs_2_.1), custom_call_target="tpu_custom_call" | custom-call | tf_op jit(solution)/shard_map/pallas_call | solution.py:271
  13.6 0.0 collective-permute-done.refs_0_
  13.6 5.3 %collective-permute-done.1.refs_1_ = bf16[400,128]{1,0:T(8,128)(2,1)S(1)} collective-permute-done((bf16[400,128]{1,0:T(8,128)(2,1)S(1)}, bf16[400,128]{1,0:T(8,128)(2,1)S(1)}, u32[]{:S(2)}, u32[]{:S(2)}) %collective-permute-start.1) | collective-permute-done | bytes 102432 | tf_op jit(solution)/shard_map/ppermute | solution.py:319
  18.9 0.0 collective-permute-done.2.refs_2_
  18.9 0.0 collective-permute-done.3.refs_3_
  19.0 0.1 collective-permute-start.5
  19.1 0.5 %collective-permute-start.6 = (bf16[256,128]{1,0:T(8,128)(2,1)S(1)}, bf16[256,128]{1,0:T(8,128)(2,1)S(1)}, u32[]{:S(2)}, u32[]{:S(2)}) collective-permute-start(bf16[256,128]{1,0:T(8,128)(2,1)S(1)} %slice.29), channel_id=1, source_target_pairs={{0,1},{1,0},{2,3},{3,2},{4,5},{5,4},{6,7},{7,6},{8,9},{9,8},{10,11... | collective-permute-start | bytes 196616 | tf_op jit(solution)/shard_map/ppermute | solution.py:325
  19.6 0.1 collective-permute-start.7
  19.6 0.4 %collective-permute-start.8 = (bf16[256,128]{1,0:T(8,128)(2,1)S(1)}, bf16[256,128]{1,0:T(8,128)(2,1)S(1)}, u32[]{:S(2)}, u32[]{:S(2)}) collective-permute-start(bf16[256,128]{1,0:T(8,128)(2,1)S(1)} %slice.31), channel_id=1, source_target_pairs={{0,1},{1,0},{2,3},{3,2},{4,5},{5,4},{6,7},{7,6},{8,9},{9,8},{10,11... | collective-permute-start | bytes 196616 | tf_op jit(solution)/shard_map/ppermute | solution.py:325
  20.1 0.1 collective-permute-start.4
  20.2 0.7 %shard_map.129 = (f32[8,512]{1,0:T(8,128)S(1)}, f32[128,512]{1,0:T(8,128)S(1)}) custom-call(bf16[400,128]{1,0:T(8,128)(2,1)S(1)} %collective-permute-done.refs_0_, bf16[400,128]{1,0:T(8,128)(2,1)S(1)} %collective-permute-done.1.refs_1_, bf16[400,128]{1,0:T(8,128)(2,1)S(1)} %collective-permute-done.2.refs_2_, bf16[400,128]{1,0:T(8,128)(2,1)S(1)} %collective-permute-done.3.refs_3_), custom_call_target="tpu_custom_call" | custom-call | tf_op jit(solution)/shard_map/pallas_call | solution.py:271
  20.8 0.4 %collective-permute-done.4.refs_6_ = bf16[64,128]{1,0:T(8,128)(2,1)S(1)} collective-permute-done((bf16[64,128]{1,0:T(8,128)(2,1)S(1)}, bf16[64,128]{1,0:T(8,128)(2,1)S(1)}, u32[]{:S(2)}, u32[]{:S(2)}) %collective-permute-start.4) | collective-permute-done | bytes 16416 | tf_op jit(solution)/shard_map/ppermute | solution.py:325
  21.3 0.0 collective-permute-done.5.refs_7_
  21.3 0.0 collective-permute-done.6.refs_8_
  21.3 0.0 collective-permute-done.7.refs_9_
  21.3 0.0 collective-permute-done.8.refs_10_
  21.3 0.0 copy-start.1
  21.3 0.8 %shard_map.130 = (bf16[144,128]{1,0:T(8,128)(2,1)S(1)}, bf16[144,128]{1,0:T(8,128)(2,1)S(1)}, bf16[144,128]{1,0:T(8,128)(2,1)S(1)}, bf16[144,128]{1,0:T(8,128)(2,1)S(1)}) custom-call(bf16[400,128]{1,0:T(8,128)(2,1)S(1)} %collective-permute-done.refs_0_, bf16[400,128]{1,0:T(8,128)(2,1)S(1)} %collective-permute-done.1.refs_1_, ...), custom_call_target="tpu_custom_call" | custom-call | tf_op jit(solution)/shard_map/pallas_call | solution.py:271
  22.1 2.1 %collective-permute-start.9 = (bf16[144,128]{1,0:T(8,128)(2,1)S(1)}, bf16[144,128]{1,0:T(8,128)(2,1)S(1)}, u32[]{:S(2)}, u32[]{:S(2)}) collective-permute-start(bf16[144,128]{1,0:T(8,128)(2,1)S(1)} %get-tuple-element.43), channel_id=1, source_target_pairs={{25,0},{29,1},{27,2},{31,3},{24,4},{28,5},{26,6},{30,7},{17,8},{21... | collective-permute-start | bytes 110600 | tf_op jit(solution)/shard_map/ppermute | solution.py:319
  24.1 0.0 collective-permute-start.10
  24.1 2.8 %collective-permute-start.11 = (bf16[144,128]{1,0:T(8,128)(2,1)S(1)}, bf16[144,128]{1,0:T(8,128)(2,1)S(1)}, u32[]{:S(2)}, u32[]{:S(2)}) collective-permute-start(bf16[144,128]{1,0:T(8,128)(2,1)S(1)} %get-tuple-element.45), channel_id=1, source_target_pairs={{9,0},{13,1},{11,2},{15,3},{8,4},{12,5},{10,6},{14,7},{1,8},{5,9},... | collective-permute-start | bytes 110600 | tf_op jit(solution)/shard_map/ppermute | solution.py:319
  26.9 0.5 %collective-permute-start.12 = (bf16[144,128]{1,0:T(8,128)(2,1)S(1)}, bf16[144,128]{1,0:T(8,128)(2,1)S(1)}, u32[]{:S(2)}, u32[]{:S(2)}) collective-permute-start(bf16[144,128]{1,0:T(8,128)(2,1)S(1)} %get-tuple-element.46), channel_id=1, source_target_pairs={{1,0},{5,1},{3,2},{7,3},{0,4},{4,5},{2,6},{6,7},{9,8},{13,9},{11,1... | collective-permute-start | bytes 110600 | tf_op jit(solution)/shard_map/ppermute | solution.py:319
  27.4 0.2 collective-permute-done.9.refs_0_
  27.6 1.7 %collective-permute-done.10.refs_1_ = bf16[144,128]{1,0:T(8,128)(2,1)S(1)} collective-permute-done((bf16[144,128]{1,0:T(8,128)(2,1)S(1)}, bf16[144,128]{1,0:T(8,128)(2,1)S(1)}, u32[]{:S(2)}, u32[]{:S(2)}) %collective-permute-start.10) | collective-permute-done | bytes 36896 | tf_op jit(solution)/shard_map/ppermute | solution.py:319
  29.2 0.0 collective-permute-done.11.refs_2_
  29.3 0.0 collective-permute-done.12.refs_3_
  29.3 0.0 copy-done
  29.3 0.7 %shard_map.131 = (f32[64,2048]{1,0:T(8,128)S(1)}, bf16[64,2048]{1,0:T(8,128)(2,1)S(1)}) custom-call(f32[512,128]{1,0:T(8,128)S(1)} %get-tuple-element.35.sum_ref, f32[8,128]{1,0:T(8,128)S(1)} %get-tuple-element.36.log_ref, bf16[512,2048]{1,0:T(8,128)(2,1)S(1)} %copy-done, bf16[144,128]{1,0:T(8,128)(2,1)S(1)} %collective-permute-done.9.refs_0_, ...), custom_call_target="tpu_custom_call" | custom-call | tf_op jit(solution)/shard_map/pallas_call | solution.py:271
  29.9 0.2 collective-permute-start.13
  30.1 1.4 %collective-permute-done.13 = bf16[64,2048]{1,0:T(8,128)(2,1)S(1)} collective-permute-done((bf16[64,2048]{1,0:T(8,128)(2,1)S(1)}, bf16[64,2048]{1,0:T(8,128)(2,1)S(1)}, u32[]{:S(2)}, u32[]{:S(2)}) %collective-permute-start.13) | collective-permute-done | bytes 262176 | tf_op jit(solution)/shard_map/ppermute | solution.py:325
  31.6 1.6 %collective-permute-start.14 = (bf16[64,2048]{1,0:T(8,128)(2,1)S(1)}, bf16[64,2048]{1,0:T(8,128)(2,1)S(1)}, u32[]{:S(2)}, u32[]{:S(2)}) collective-permute-start(bf16[64,2048]{1,0:T(8,128)(2,1)S(1)} %add_convert_fusion.1), channel_id=1, source_target_pairs={{0,2},{1,3},{2,0},{3,1},{4,6},{5,7},{6,4},{7,5},{8,10},{9,11},{10,... | collective-permute-start | bytes 786440 | tf_op jit(solution)/shard_map/ppermute | solution.py:325
  33.2 6.8 %collective-permute-done.14 = bf16[64,2048]{1,0:T(8,128)(2,1)S(1)} collective-permute-done((bf16[64,2048]{1,0:T(8,128)(2,1)S(1)}, bf16[64,2048]{1,0:T(8,128)(2,1)S(1)}, u32[]{:S(2)}, u32[]{:S(2)}) %collective-permute-start.14) | collective-permute-done | bytes 262176 | tf_op jit(solution)/shard_map/ppermute | solution.py:325
  40.0 0.0 copy-done.1
  40.0 0.1 add_convert_fusion.half_ref
  40.1 0.1 collective-permute-start.15
  40.2 0.7 %shard_map.132._ = bf16[128,2048]{1,0:T(8,128)(2,1)} custom-call(bf16[64,2048]{1,0:T(8,128)(2,1)S(1)} %add_convert_fusion.half_ref), custom_call_target="tpu_custom_call" | custom-call | tf_op jit(solution)/shard_map/pallas_call | solution.py:271
  40.9 0.8 %collective-permute-done.15.half_ref = bf16[64,2048]{1,0:T(8,128)(2,1)S(1)} collective-permute-done((bf16[64,2048]{1,0:T(8,128)(2,1)S(1)}, bf16[64,2048]{1,0:T(8,128)(2,1)S(1)}, u32[]{:S(2)}, u32[]{:S(2)}) %collective-permute-start.15) | collective-permute-done | bytes 262176 | tf_op jit(solution)/shard_map/ppermute | solution.py:325
  41.7 0.7 %shard_map.133 = bf16[128,2048]{1,0:T(8,128)(2,1)} custom-call(bf16[64,2048]{1,0:T(8,128)(2,1)S(1)} %collective-permute-done.15.half_ref, bf16[128,2048]{1,0:T(8,128)(2,1)} %shard_map.132._), custom_call_target="tpu_custom_call", output_to_operand_aliasing={{}: (1, {})} | custom-call | tf_op jit(solution)/shard_map/pallas_call | solution.py:271
  (11 shorter events, 0.1 us)
Async XLA Ops:
  3.7 9.9 %collective-permute-start = (bf16[400,128]{1,0:T(8,128)(2,1)S(1)}, bf16[400,128]{1,0:T(8,128)(2,1)S(1)}, u32[]{:S(2)}, u32[]{:S(2)}) collective-permute-start(bf16[400,128]{1,0:T(8,128)(2,1)S(1)} %get-tuple-element.27), channel_id=1, source_target_pairs={{0,25},{1,29},{2,27},{3,31},{4,24},{5,28},{6,26},{7,30},{8,17},{9,... | collective-permute-start | bytes 307208 | tf_op jit(solution)/shard_map/ppermute | solution.py:319
  8.2 10.7 %collective-permute-start.1 = (bf16[400,128]{1,0:T(8,128)(2,1)S(1)}, bf16[400,128]{1,0:T(8,128)(2,1)S(1)}, u32[]{:S(2)}, u32[]{:S(2)}) collective-permute-start(bf16[400,128]{1,0:T(8,128)(2,1)S(1)} %get-tuple-element.28), channel_id=1, source_target_pairs={{0,17},{1,21},{2,19},{3,23},{4,16},{5,20},{6,18},{7,22},{8,25},{9,... | collective-permute-start | bytes 307208 | tf_op jit(solution)/shard_map/ppermute | solution.py:319
  8.3 10.6 %collective-permute-start.2 = (bf16[400,128]{1,0:T(8,128)(2,1)S(1)}, bf16[400,128]{1,0:T(8,128)(2,1)S(1)}, u32[]{:S(2)}, u32[]{:S(2)}) collective-permute-start(bf16[400,128]{1,0:T(8,128)(2,1)S(1)} %get-tuple-element.29), channel_id=1, source_target_pairs={{0,9},{1,13},{2,11},{3,15},{4,8},{5,12},{6,10},{7,14},{8,1},{9,5},... | collective-permute-start | bytes 307208 | tf_op jit(solution)/shard_map/ppermute | solution.py:319
  9.9 9.0 %collective-permute-start.3 = (bf16[400,128]{1,0:T(8,128)(2,1)S(1)}, bf16[400,128]{1,0:T(8,128)(2,1)S(1)}, u32[]{:S(2)}, u32[]{:S(2)}) collective-permute-start(bf16[400,128]{1,0:T(8,128)(2,1)S(1)} %get-tuple-element.30), channel_id=1, source_target_pairs={{0,1},{1,5},{2,3},{3,7},{4,0},{5,4},{6,2},{7,6},{8,9},{9,13},{10,1... | collective-permute-start | bytes 307208 | tf_op jit(solution)/shard_map/ppermute | solution.py:319
  10.2 19.1 %copy-start = (bf16[512,2048]{1,0:T(8,128)(2,1)S(1)}, bf16[512,2048]{1,0:T(8,128)(2,1)}, u32[]{:S(2)}) copy-start(bf16[512,2048]{1,0:T(8,128)(2,1)} %w_out_ref.1) | copy-start | bytes 6291460
  19.0 2.3 %collective-permute-start.5 = (bf16[256,128]{1,0:T(8,128)(2,1)S(1)}, bf16[256,128]{1,0:T(8,128)(2,1)S(1)}, u32[]{:S(2)}, u32[]{:S(2)}) collective-permute-start(bf16[256,128]{1,0:T(8,128)(2,1)S(1)} %slice.28), channel_id=1, source_target_pairs={{0,1},{1,0},{2,3},{3,2},{4,5},{5,4},{6,7},{7,6},{8,9},{9,8},{10,11... | collective-permute-start | bytes 196616 | tf_op jit(solution)/shard_map/ppermute | solution.py:325
  19.1 2.2 %collective-permute-start.6 = (bf16[256,128]{1,0:T(8,128)(2,1)S(1)}, bf16[256,128]{1,0:T(8,128)(2,1)S(1)}, u32[]{:S(2)}, u32[]{:S(2)}) collective-permute-start(bf16[256,128]{1,0:T(8,128)(2,1)S(1)} %slice.29), channel_id=1, source_target_pairs={{0,1},{1,0},{2,3},{3,2},{4,5},{5,4},{6,7},{7,6},{8,9},{9,8},{10,11... | collective-permute-start | bytes 196616 | tf_op jit(solution)/shard_map/ppermute | solution.py:325
  19.6 1.7 %collective-permute-start.7 = (bf16[256,128]{1,0:T(8,128)(2,1)S(1)}, bf16[256,128]{1,0:T(8,128)(2,1)S(1)}, u32[]{:S(2)}, u32[]{:S(2)}) collective-permute-start(bf16[256,128]{1,0:T(8,128)(2,1)S(1)} %slice.30), channel_id=1, source_target_pairs={{0,1},{1,0},{2,3},{3,2},{4,5},{5,4},{6,7},{7,6},{8,9},{9,8},{10,11... | collective-permute-start | bytes 196616 | tf_op jit(solution)/shard_map/ppermute | solution.py:325
  19.6 1.6 %collective-permute-start.8 = (bf16[256,128]{1,0:T(8,128)(2,1)S(1)}, bf16[256,128]{1,0:T(8,128)(2,1)S(1)}, u32[]{:S(2)}, u32[]{:S(2)}) collective-permute-start(bf16[256,128]{1,0:T(8,128)(2,1)S(1)} %slice.31), channel_id=1, source_target_pairs={{0,1},{1,0},{2,3},{3,2},{4,5},{5,4},{6,7},{7,6},{8,9},{9,8},{10,11... | collective-permute-start | bytes 196616 | tf_op jit(solution)/shard_map/ppermute | solution.py:325
  20.1 1.2 %collective-permute-start.4 = (bf16[64,128]{1,0:T(8,128)(2,1)S(1)}, bf16[64,128]{1,0:T(8,128)(2,1)S(1)}, u32[]{:S(2)}, u32[]{:S(2)}) collective-permute-start(bf16[64,128]{1,0:T(8,128)(2,1)S(1)} %pad_maximum_fusion), channel_id=1, source_target_pairs={{0,1},{1,0},{2,3},{3,2},{4,5},{5,4},{6,7},{7,6},{8,9},{9,8},{10,11... | collective-permute-start | bytes 49160 | tf_op jit(solution)/shard_map/ppermute | solution.py:325
  21.3 18.7 %copy-start.1 = (bf16[128,2048]{1,0:T(8,128)(2,1)S(1)}, bf16[128,2048]{1,0:T(8,128)(2,1)}, u32[]{:S(2)}) copy-start(bf16[128,2048]{1,0:T(8,128)(2,1)} %refs_3_.1) | copy-start | bytes 1572868
  22.1 5.5 %collective-permute-start.9 = (bf16[144,128]{1,0:T(8,128)(2,1)S(1)}, bf16[144,128]{1,0:T(8,128)(2,1)S(1)}, u32[]{:S(2)}, u32[]{:S(2)}) collective-permute-start(bf16[144,128]{1,0:T(8,128)(2,1)S(1)} %get-tuple-element.43), channel_id=1, source_target_pairs={{25,0},{29,1},{27,2},{31,3},{24,4},{28,5},{26,6},{30,7},{17,8},{21... | collective-permute-start | bytes 110600 | tf_op jit(solution)/shard_map/ppermute | solution.py:319
  24.1 5.1 %collective-permute-start.10 = (bf16[144,128]{1,0:T(8,128)(2,1)S(1)}, bf16[144,128]{1,0:T(8,128)(2,1)S(1)}, u32[]{:S(2)}, u32[]{:S(2)}) collective-permute-start(bf16[144,128]{1,0:T(8,128)(2,1)S(1)} %get-tuple-element.44), channel_id=1, source_target_pairs={{17,0},{21,1},{19,2},{23,3},{16,4},{20,5},{18,6},{22,7},{25,8},{29... | collective-permute-start | bytes 110600 | tf_op jit(solution)/shard_map/ppermute | solution.py:319
  24.1 5.1 %collective-permute-start.11 = (bf16[144,128]{1,0:T(8,128)(2,1)S(1)}, bf16[144,128]{1,0:T(8,128)(2,1)S(1)}, u32[]{:S(2)}, u32[]{:S(2)}) collective-permute-start(bf16[144,128]{1,0:T(8,128)(2,1)S(1)} %get-tuple-element.45), channel_id=1, source_target_pairs={{9,0},{13,1},{11,2},{15,3},{8,4},{12,5},{10,6},{14,7},{1,8},{5,9},... | collective-permute-start | bytes 110600 | tf_op jit(solution)/shard_map/ppermute | solution.py:319
  26.9 2.3 %collective-permute-start.12 = (bf16[144,128]{1,0:T(8,128)(2,1)S(1)}, bf16[144,128]{1,0:T(8,128)(2,1)S(1)}, u32[]{:S(2)}, u32[]{:S(2)}) collective-permute-start(bf16[144,128]{1,0:T(8,128)(2,1)S(1)} %get-tuple-element.46), channel_id=1, source_target_pairs={{1,0},{5,1},{3,2},{7,3},{0,4},{4,5},{2,6},{6,7},{9,8},{13,9},{11,1... | collective-permute-start | bytes 110600 | tf_op jit(solution)/shard_map/ppermute | solution.py:319
  29.9 1.6 %collective-permute-start.13 = (bf16[64,2048]{1,0:T(8,128)(2,1)S(1)}, bf16[64,2048]{1,0:T(8,128)(2,1)S(1)}, u32[]{:S(2)}, u32[]{:S(2)}) collective-permute-start(bf16[64,2048]{1,0:T(8,128)(2,1)S(1)} %get-tuple-element.48), channel_id=1, source_target_pairs={{0,1},{1,0},{2,3},{3,2},{4,5},{5,4},{6,7},{7,6},{8,9},{9,8},{10,11... | collective-permute-start | bytes 786440 | tf_op jit(solution)/shard_map/ppermute | solution.py:325
  31.6 8.4 %collective-permute-start.14 = (bf16[64,2048]{1,0:T(8,128)(2,1)S(1)}, bf16[64,2048]{1,0:T(8,128)(2,1)S(1)}, u32[]{:S(2)}, u32[]{:S(2)}) collective-permute-start(bf16[64,2048]{1,0:T(8,128)(2,1)S(1)} %add_convert_fusion.1), channel_id=1, source_target_pairs={{0,2},{1,3},{2,0},{3,1},{4,6},{5,7},{6,4},{7,5},{8,10},{9,11},{10,... | collective-permute-start | bytes 786440 | tf_op jit(solution)/shard_map/ppermute | solution.py:325
  40.1 1.6 %collective-permute-start.15 = (bf16[64,2048]{1,0:T(8,128)(2,1)S(1)}, bf16[64,2048]{1,0:T(8,128)(2,1)S(1)}, u32[]{:S(2)}, u32[]{:S(2)}) collective-permute-start(bf16[64,2048]{1,0:T(8,128)(2,1)S(1)} %add_convert_fusion.half_ref), channel_id=1, source_target_pairs={{0,1},{1,0},{2,3},{3,2},{4,5},{5,4},{6,7},{7,6},{8,9},{9,8},{10,11... | collective-permute-start | bytes 786440 | tf_op jit(solution)/shard_map/ppermute | solution.py:325

commit v4 on v3

--- a/solution.py
+++ b/solution.py
@@ -14,7 +14,12 @@
 W_CUTS = 4
 ROW_CUTS = 2
 
+ORDER = (1, 0)
+
 big = 1e30
+Q = 3
+SFX = 10
+JOIN = 30
 
 VMEM = pl.BlockSpec(memory_space=pltpu.VMEM)
 HBM = pl.BlockSpec(memory_space=pltpu.HBM)
@@ -26,9 +31,9 @@
     return lax.dot_general(a, b, dims, preferred_element_type=jnp.float32)
 
 
-def head_at(rest, bits):
-    part = lax.div(lax.axis_index("blk"), rest)
-    return pl.multiple_of((part ^ bits) * HD, HD)
+def head_at(bits, i, per):
+    pair = lax.rem(lax.div(lax.axis_index("blk"), 2), 2)
+    return pl.multiple_of(((pair ^ bits) * per + i) * HD, HD)
 
 
 def start_all(pairs, sems):
@@ -38,18 +43,38 @@
     return copies
 
 
-def block_copies(rest, bits, keys_ref, values_ref, out, at):
-    cols = pl.ds(head_at(rest, bits), HD)
-    return [
-        (keys_ref.at[0, :, cols], out.at[at : at + HD, :]),
-        (values_ref.at[0, :, cols], out.at[at + HD : at + 2 * HD, :]),
-    ]
-
-
-def query_kernel(heads, rest, *refs):
+def block_copies(per, bits, keys_ref, values_ref, out, at):
+    pairs = []
+    for i in range(per):
+        cols = pl.ds(head_at(bits, i, per), HD)
+        pairs.append((keys_ref.at[0, :, cols], out.at[at : at + HD, :]))
+        pairs.append((values_ref.at[0, :, cols], out.at[at + HD : at + 2 * HD, :]))
+        at += 2 * HD
+    return pairs
+
+
+def far_kernel(per, keys_ref, values_ref, tag_ref, *refs):
+    outs, sems = refs[:2], refs[2]
+    pairs = []
+    for bits, out in enumerate(outs):
+        pairs += block_copies(per, bits, keys_ref, values_ref, out, 0)
+    copies = start_all(pairs, sems)
+    for out in outs:
+        out[2 * HD * per : 2 * HD * per + NOTE_ROWS, :] = tag_ref[...]
+    for copy in copies:
+        copy.wait()
+
+
+def join_kernel(_, *refs):
+    out = refs[-1]
+    for i, ref in enumerate(refs[:-1]):
+        out[i * ref.shape[0] : (i + 1) * ref.shape[0], :] = ref[...]
+
+
+def query_kernel(per, *refs):
     keys_ref, values_ref, tag_ref, hidden_in, w_query, *sources = refs[:9]
     normed_ref, query_ref = refs[9:11]
-    outs, held, sems = refs[11 : 11 + heads], refs[11 + heads : -1], refs[-1]
+    outs, held, sems = refs[11:13], refs[13:-1], refs[-1]
     hidden_ref, w_query_ref, gain_ref, bias_ref, segment_ref, request_group_ref = held
     rows, width = hidden_ref.shape
     row_cuts = [pl.ds(i * (rows // ROW_CUTS), rows // ROW_CUTS) for i in range(ROW_CUTS)]
@@ -57,8 +82,8 @@
     pairs = [(hidden_in.at[cut, :], hidden_ref.at[cut, :]) for cut in row_cuts]
     pairs += list(zip(sources, held[2:]))
     pairs += [(w_query.at[cut, :], w_query_ref.at[cut, :]) for cut in w_cuts]
-    for k, out in enumerate(outs):
-        pairs += block_copies(rest, k, keys_ref, values_ref, out, NOTE_ROWS + rows)
+    for bits, out in enumerate(outs):
+        pairs += block_copies(per, bits, keys_ref, values_ref, out, per * rows)
     copies = start_all(pairs, sems)
     small = copies[ROW_CUTS : ROW_CUTS + 4]
     weights = copies[ROW_CUTS + 4 : ROW_CUTS + 4 + W_CUTS]
@@ -87,9 +112,11 @@
         copy.wait()
         query = query + dot(normed_ref[:, cut], w_query_ref[cut, :])
     query_ref[...] = (query * (HD**-0.5)).astype(jnp.bfloat16)
-    for k, out in enumerate(outs):
-        out[0:NOTE_ROWS, :] = notes
-        out[NOTE_ROWS : NOTE_ROWS + rows, :] = query_ref[:, pl.ds(head_at(rest, k), HD)]
+    for bits, out in enumerate(outs):
+        for i in range(per):
+            out[i * rows : (i + 1) * rows, :] = query_ref[:, pl.ds(head_at(bits, i, per), HD)]
+        at = per * (rows + 2 * HD)
+        out[at : at + NOTE_ROWS, :] = notes
     for copy in copies[ROW_CUTS + 4 + W_CUTS :]:
         copy.wait()
 
@@ -149,93 +176,102 @@
     return new_top, total, summed
 
 
-def questions(asks, rows):
-    query = jnp.concatenate([ref[NOTE_ROWS : NOTE_ROWS + rows, :] for ref in asks], axis=0)
-    notes = [ref[0:NOTE_ROWS, :].astype(jnp.float32) for ref in asks]
-    return query, jnp.concatenate([note[1:2, :] for note in notes], axis=1), notes
-
-
-def first_kernel(rows, *refs):
-    asks, (state_ref, sum_ref) = refs[:-2], refs[-2:]
-    query, group, notes = questions(asks, rows)
-    tokens = query.shape[0]
+def questions(asks, rows, per):
+    queries = [
+        jnp.concatenate([ref[i * rows : (i + 1) * rows, :] for ref in asks], axis=0) for i in range(per)
+    ]
+    at = per * (rows + 2 * HD)
+    notes = [ref[at : at + NOTE_ROWS, :].astype(jnp.float32)[1:2, :] for ref in asks]
+    return queries, jnp.concatenate(notes, axis=1)
+
+
+def block_scores(ref, at, queries, group):
+    per = len(queries)
+    tag = ref[pl.ds(at + 2 * HD * per, NOTE_ROWS), :].astype(jnp.float32)[0:1, 0:1]
     found = []
-    at = NOTE_ROWS + rows
-    for ref, note in zip(asks, notes):
-        scores = dot(ref[at : at + HD, :], query, NT)
-        found.append((scores, group == note[0:1, 0:1], ref[at + HD : at + 2 * HD, :]))
-    carry = (
-        jnp.full((1, tokens), -big, jnp.float32),
-        jnp.zeros((1, tokens), jnp.float32),
-        jnp.zeros((HD, tokens), jnp.float32),
-    )
-    top, total, summed = absorb(carry, found)
-    state_ref[0:1, :] = top
-    state_ref[1:2, :] = total
-    sum_ref[...] = summed
-
-
-def second_kernel(rows, n_asks, *refs):
-    asks, state_ref, sum_ref, notes_ref = refs[:n_asks], *refs[n_asks : n_asks + 3]
-    blocks, outs = refs[n_asks + 3 : -n_asks], refs[-n_asks:]
-    query, group, _ = questions(asks, rows)
-    tokens = query.shape[0]
-
-    def one(ref, at, place):
-        tag = notes_ref[pl.ds(place, NOTE_ROWS), :].astype(jnp.float32)[0:1, 0:1]
-        return dot(ref[pl.ds(at, HD), :], query, NT), group == tag, ref[pl.ds(at + HD, HD), :]
-
-    carry = (state_ref[0:1, :], state_ref[1:2, :], sum_ref[...])
-    singles, place = [], 0
+    for i, query in enumerate(queries):
+        keys, values = (ref[pl.ds(at + j * HD, HD), :] for j in (2 * i, 2 * i + 1))
+        found.append((dot(keys, query, NT), group == tag, values))
+    return found
+
+
+def first_kernel(rows, per, *refs):
+    asks, fars, (state_ref, sum_ref) = refs[:2], refs[2:-2], refs[-2:]
+    queries, group = questions(asks, rows, per)
+    tokens = group.shape[1]
+    found = [block_scores(ref, per * rows, queries, group) for ref in asks]
+    step = 2 * HD * per + NOTE_ROWS
+    for ref in fars:
+        found += [block_scores(ref, at, queries, group) for at in range(0, ref.shape[0], step)]
+    for i in range(per):
+        carry = (
+            jnp.full((1, tokens), -big, jnp.float32),
+            jnp.zeros((1, tokens), jnp.float32),
+            jnp.zeros((HD, tokens), jnp.float32),
+        )
+        top, total, summed = absorb(carry, [block[i] for block in found])
+        cols = slice(i * tokens, (i + 1) * tokens)
+        state_ref[0:1, cols] = top
+        state_ref[1:2, cols] = total
+        sum_ref[:, cols] = summed
+
+
+def second_kernel(rows, per, *refs):
+    asks, (state_ref, sum_ref), blocks, outs = refs[:2], refs[2:4], refs[4:-2], refs[-2:]
+    queries, group = questions(asks, rows, per)
+    tokens = group.shape[1]
+    step = 2 * HD * per + NOTE_ROWS
+    cols = [slice(i * tokens, (i + 1) * tokens) for i in range(per)]
+    carry = [(state_ref[0:1, at], state_ref[1:2, at], sum_ref[:, at]) for at in cols]
+    found = [
+        block_scores(ref, at, queries, group)
+        for ref in blocks
+        if ref.shape[0] <= 2 * step
+        for at in range(0, ref.shape[0], step)
+    ]
+    carry = tuple(absorb(carry[i], [block[i] for block in found]) for i in range(per))
     for ref in blocks:
-        held = ref.shape[0] // (2 * HD)
-        if held == 1:
-            singles.append(one(ref, 0, place))
-        place += held * NOTE_ROWS
-    carry = absorb(carry, singles)
-    place = 0
-    for ref in blocks:
-        held = ref.shape[0] // (2 * HD)
-        if held > 1:
-
-            def body(i, state, ref=ref, place=place):
-                at = pl.multiple_of(i * 2 * HD, HD)
-                return absorb(state, [one(ref, at, pl.multiple_of(place + i * NOTE_ROWS, NOTE_ROWS))])
-
-            carry = lax.fori_loop(0, held, body, carry)
-        place += held * NOTE_ROWS
-    top, total, summed = carry
-    found = total > 0.0
-    summed = summed * jnp.where(found, 1.0 / jnp.where(found, total, 1.0), 0.0)
-    log = jnp.where(found, top + jnp.log(jnp.where(found, total, 1.0)), -big)
-    first = log.astype(jnp.bfloat16).astype(jnp.float32)
-    second = (log - first).astype(jnp.bfloat16).astype(jnp.float32)
-    third = log - first - second
-    place = lax.broadcasted_iota(jnp.int32, (NOTE_ROWS, tokens), 0)
-    logs = jnp.where(place == 0, first, jnp.where(place == 1, second, jnp.where(place == 2, third, 0.0)))
+        if ref.shape[0] > 2 * step:
+
+            def body(b, state, ref=ref):
+                block = block_scores(ref, pl.multiple_of(b * step, NOTE_ROWS), queries, group)
+                return tuple(absorb(state[i], [block[i]]) for i in range(per))
+
+            carry = lax.fori_loop(0, ref.shape[0] // step, body, carry)
+    logs = [jnp.zeros((NOTE_ROWS, rows), jnp.float32)] * len(outs)
+    place = lax.broadcasted_iota(jnp.int32, (NOTE_ROWS, rows), 0)
+    for i, (top, total, summed) in enumerate(carry):
+        found = total > 0.0
+        summed = summed * jnp.where(found, 1.0 / jnp.where(found, total, 1.0), 0.0)
+        log = jnp.where(found, top + jnp.log(jnp.where(found, total, 1.0)), -big)
+        first = log.astype(jnp.bfloat16).astype(jnp.float32)
+        second = (log - first).astype(jnp.bfloat16).astype(jnp.float32)
+        for k, out in enumerate(outs):
+            at = slice(k * rows, (k + 1) * rows)
+            out[i * HD : (i + 1) * HD, :] = summed[:, at].astype(jnp.bfloat16)
+            for j, term in enumerate((first, second, log - first - second)):
+                logs[k] = jnp.where(place == 3 * i + j, term[:, at], logs[k])
     for k, out in enumerate(outs):
-        cols = slice(k * rows, (k + 1) * rows)
-        out[0:HD, :] = summed[:, cols].astype(jnp.bfloat16)
-        out[HD : HD + NOTE_ROWS, :] = logs[:, cols].astype(jnp.bfloat16)
-
-
-def project_kernel(rest, order, sum_ref, log_ref, w_out_ref, *refs):
-    backs = refs[: len(order)]
-    keep_ref, send_ref, attended, branch = refs[len(order) :]
-    for bits, back in zip(order, backs):
-        at = head_at(rest, bits)
-        logs = back[HD : HD + NOTE_ROWS, :].astype(jnp.float32)
-        prefix_log = logs[0:1, :] + logs[1:2, :] + logs[2:3, :]
-        suffix_log = log_ref[pl.ds(lax.div(at, HD), 1), :]
-        top = jnp.maximum(prefix_log, suffix_log)
-        prefix_part = jnp.exp(prefix_log - top)
-        suffix_part = jnp.exp(suffix_log - top)
-        whole = prefix_part + suffix_part
-        joined = (
-            back[0:HD, :].astype(jnp.float32) * (prefix_part / whole)
-            + sum_ref[pl.ds(at, HD), :] * (suffix_part / whole)
-        )
-        attended[pl.ds(at, HD), :] = joined.astype(jnp.bfloat16)
+        out[per * HD : per * HD + NOTE_ROWS, :] = logs[k].astype(jnp.bfloat16)
+
+
+def project_kernel(per, sum_ref, log_ref, w_out_ref, *refs):
+    backs, (keep_ref, send_ref, attended, branch) = refs[:2], refs[2:]
+    for bits, back in zip(ORDER, backs):
+        logs = back[per * HD : per * HD + NOTE_ROWS, :].astype(jnp.float32)
+        for i in range(per):
+            at = head_at(bits, i, per)
+            prefix_log = logs[3 * i : 3 * i + 1, :] + logs[3 * i + 1 : 3 * i + 2, :] + logs[3 * i + 2 : 3 * i + 3, :]
+            suffix_log = log_ref[pl.ds(lax.div(at, HD), 1), :]
+            top = jnp.maximum(prefix_log, suffix_log)
+            prefix_part = jnp.exp(prefix_log - top)
+            suffix_part = jnp.exp(suffix_log - top)
+            whole = prefix_part + suffix_part
+            joined = (
+                back[i * HD : (i + 1) * HD, :].astype(jnp.float32) * (prefix_part / whole)
+                + sum_ref[pl.ds(at, HD), :] * (suffix_part / whole)
+            )
+            attended[pl.ds(at, HD), :] = joined.astype(jnp.bfloat16)
     branch[...] = dot(attended[...], w_out_ref[...], TN)
     half = keep_ref.shape[0]
     side = lax.rem(lax.axis_index("mp"), 2)
@@ -262,7 +298,7 @@
     copy.wait()
 
 
-def call(kernel, outs, specs, scratch=(), out_specs=None, aliases=None):
+def call(kernel, outs, specs, scratch=(), out_specs=None, aliases=None, cost=1):
     def run(*args):
         pinned = [
             pltpu.with_memory_space_constraint(x, pltpu.HBM) if spec is HBM else x
@@ -278,6 +314,7 @@
         scratch_shapes=scratch,
         input_output_aliases=aliases or {},
         compiler_params=pltpu.CompilerParams(vmem_limit_bytes=40 * 1024 * 1024),
+        cost_estimate=pl.CostEstimate(flops=int(cost * 10**9), bytes_accessed=1, transcendentals=0),
     )
     return run
 
@@ -303,19 +340,19 @@
     heads = local_width // HD
     n_blk = lax.axis_size("blk")
     n_mp = lax.axis_size("mp")
-    rest = n_blk // heads
+    per = heads // 2
+    step = 2 * HD * per + NOTE_ROWS
     side = lax.rem(lax.axis_index("mp"), 2)
-    order = tuple(reversed(range(heads)))
-
-    def exchange(x, bits, back=False):
+
+    def exchange(x, bits, far=0, back=False):
         pairs = []
         for i in range(n_blk):
-            part, place, lane = i // rest, i % rest // 2, i % 2
+            square, pair, lane = i // 4, i // 2 % 2, i % 2
             for m in range(n_mp):
                 other, core = m // 2, m % 2
-                blk = (part ^ bits) * rest + place * 2 + core
-                pair = (i * n_mp + m, blk * n_mp + other * 2 + 1 - lane)
-                pairs.append(pair[::-1] if back else pair)
+                blk = (square ^ far) * 4 + (pair ^ bits) * 2 + core
+                link = (i * n_mp + m, blk * n_mp + other * 2 + 1 - lane)
+                pairs.append(link[::-1] if back else link)
         return lax.ppermute(x, ("blk", "mp"), pairs)
 
     def across(x, bit):
@@ -325,10 +362,20 @@
         return lax.ppermute(x, "mp", [(i, i ^ bit) for i in range(n_mp)])
 
     group = jnp.where(block_live == 1, block_slot * GROUPS // n_blk, -1).astype(bf16)
+    tag = jnp.broadcast_to(group, (NOTE_ROWS, HD))
+    fars = []
+    if n_blk == 8:
+        fars = call(
+            functools.partial(far_kernel, per),
+            [((step, HD), bf16)] * 2,
+            (HBM, HBM, VMEM),
+            [pltpu.SemaphoreType.DMA((4 * per,))],
+        )(prefix_keys, prefix_values, tag)
+        fars = [exchange(fars[k], k, far=1) for k in ORDER]
     normed, query, *packs = call(
-        functools.partial(query_kernel, heads, rest),
+        functools.partial(query_kernel, per),
         [((rows, width), bf16), ((rows, local_width), bf16)]
-        + [((NOTE_ROWS + rows + 2 * HD, HD), bf16)] * heads,
+        + [((per * rows + step, HD), bf16)] * 2,
         (HBM, HBM, VMEM) + (HBM,) * 6,
         [
             pltpu.VMEM((rows, width), bf16),
@@ -339,10 +386,11 @@
             pltpu.SMEM(request_group.shape, i32),
             pltpu.SemaphoreType.DMA((4 + ROW_CUTS + W_CUTS + 2 * heads,)),
         ],
+        cost=Q,
     )(
         prefix_keys,
         prefix_values,
-        jnp.broadcast_to(group, (NOTE_ROWS, HD)),
+        tag,
         hidden_in,
         w_query,
         norm_gain.reshape(1, width),
@@ -350,7 +398,7 @@
         segment,
         request_group,
     )
-    asks = [exchange(packs[k], k) for k in order]
+    asks = [exchange(packs[k], k) for k in ORDER]
     suffix_sum, suffix_log = call(
         functools.partial(suffix_kernel, heads),
         [((local_width, rows), f32), ((max(heads, 8), rows), f32)],
@@ -361,36 +409,33 @@
             pltpu.VMEM(w_value.shape, bf16),
             pltpu.SemaphoreType.DMA((1 + 2 * W_CUTS,)),
         ],
+        cost=SFX,
     )(normed, query, segment, w_key, w_value)
-    asks, suffix_sum, suffix_log = lax.optimization_barrier((asks, suffix_sum, suffix_log))
-
-    blocks = [x[NOTE_ROWS + rows :] for x in asks]
-    notes = jnp.concatenate([x[:NOTE_ROWS] for x in asks], axis=0)
+    if fars:
+        fars = list(call(join_kernel, [((2 * step, HD), bf16)], (VMEM,) * 3, cost=JOIN)(suffix_log, *fars))
+
+    blocks = [x[per * rows :] for x in asks] + fars
     state, summed = call(
-        functools.partial(first_kernel, rows),
+        functools.partial(first_kernel, rows, per),
         [((8, heads * rows), f32), ((HD, heads * rows), f32)],
-        (VMEM,) * heads,
-    )(*asks)
+        (VMEM,) * (2 + len(fars)),
+    )(*asks, *fars)
     others = [across_mp(x, 1) for x in blocks]
-    other_notes = across_mp(notes, 1)
-    bit = 2
-    while bit < rest:
-        everything = jnp.concatenate(blocks + others, axis=0)
-        all_notes = jnp.concatenate([notes, other_notes], axis=0)
-        others = others + [across(everything, bit)]
-        other_notes = jnp.concatenate([other_notes, across(all_notes, bit)], axis=0)
+    bit = 4
+    while bit < n_blk and not fars:
+        others = others + [across(jnp.concatenate(blocks + others, axis=0), bit)]
         bit *= 2
     backs = call(
-        functools.partial(second_kernel, rows, heads),
-        [((HD + NOTE_ROWS, rows), bf16)] * heads,
-        (VMEM,) * (heads + 3 + len(others)),
-    )(*asks, state, summed, other_notes, *others)
-    backs = [exchange(x, k, back=True) for k, x in zip(order, backs)]
+        functools.partial(second_kernel, rows, per),
+        [((per * HD + NOTE_ROWS, rows), bf16)] * 2,
+        (VMEM,) * (4 + len(others)),
+    )(*asks, state, summed, *others)
+    backs = [exchange(x, k, back=True) for k, x in zip(ORDER, backs)]
 
     keep, send = call(
-        functools.partial(project_kernel, rest, order),
+        functools.partial(project_kernel, per),
         [((rows // 2, width), f32), ((rows // 2, width), bf16)],
-        (VMEM,) * (3 + heads),
+        (VMEM,) * 5,
         [pltpu.VMEM((local_width, rows), bf16), pltpu.VMEM((rows, width), f32)],
     )(suffix_sum, suffix_log, w_out, *backs)
 

time: 42.6 us -> 41.6 us (0.977)
  starting transfers between devices: 14.9 us -> 11.2 us
  waiting for transfers between devices: 16.6 us -> 18.5 us
  Pallas kernels: 9.25 us -> 10.1 us
    ppermute x8 -> x6, starting transfers between devices: 11.9 us -> 7.53 us  [exchange(): return lax.ppermute(x, ('blk', 'mp'), pairs)]
    ppermute x8 -> x6, waiting for transfers between devices: 7.12 us -> 9.16 us  [exchange(): return lax.ppermute(x, ('blk', 'mp'), pairs)]
    pallas_call x7 -> x9, Pallas kernels: 9.25 us -> 10.1 us  [run(): return inner(*pinned)]
    ppermute x8 -> x6, starting transfers between devices: 3.03 us -> 3.65 us  [across_mp(): return lax.ppermute(x, 'mp', [(i, i ^ bit) for i in range(n_mp)])]
    ppermute x8 -> x6, waiting for transfers between devices: 9.45 us -> 9.31 us  [across_mp(): return lax.ppermute(x, 'mp', [(i, i ^ bit) for i in range(n_mp)])]
  transfers between devices with their start and end apart: 16 -> 12, of which waited for: 7 -> 8; matrix products, arithmetic and copies ran while one was open for 0% -> 0% of each run, Pallas kernels for 11% -> 17%
where the time goes in v4:
time: 41.6 us; the launch traced here: 41.4 us
  waiting for transfers between devices  18.5 us (44%)
  starting transfers between devices  11.2 us (27%)
  Pallas kernels  10.1 us (24%)
  between operations  1.45 us (3%)
    pallas_call x9, Pallas kernels, run(): return inner(*pinned)  10.1 us
    ppermute x6, waiting for transfers between devices, across_mp(): return lax.ppermute(x, 'mp', [(i, i ^ bit) for i in range(n_mp)])  9.31 us
    ppermute x6, waiting for transfers between devices, exchange(): return lax.ppermute(x, ('blk', 'mp'), pairs)  9.16 us
    ppermute x6, starting transfers between devices, exchange(): return lax.ppermute(x, ('blk', 'mp'), pairs)  7.53 us
    ppermute x6, starting transfers between devices, across_mp(): return lax.ppermute(x, 'mp', [(i, i ^ bit) for i in range(n_mp)])  3.65 us
  transfers between devices with their start and end apart: 12, of which 8 were waited for; matrix products, arithmetic and copies ran while one was open for 0% of the time, Pallas kernels for 17%

profile of v4, /device:TPU:0, one launch (start us, length us, event | category | flops | bytes accessed | tf_op | source)
XLA Modules:
  0.0 41.4 jit_solution(9294085774582432823)
XLA Ops:
  1.3 1.0 %shard_map.129 = (bf16[528,128]{1,0:T(8,128)(2,1)S(1)}, bf16[528,128]{1,0:T(8,128)(2,1)S(1)}) custom-call(bf16[1,128,512]{2,1,0:T(8,128)(2,1)} %keys_ref.1, bf16[1,128,512]{2,1,0:T(8,128)(2,1)} %values_ref.1, bf16[16,128]{1,0:T(8,128)(2,1)S(1)} %broadcast_in_dim.4.refs_2_.tag_ref), custom_call_target="tpu_custom_call" | custom-call | flops 1000000000 | bytes 1 | tf_op jit(solution)/shard_map/pallas_call | solution.py:307
  2.3 4.5 %collective-permute-start.2 = (bf16[528,128]{1,0:T(8,128)(2,1)S(1)}, bf16[528,128]{1,0:T(8,128)(2,1)S(1)}, u32[]{:S(2)}, u32[]{:S(2)}) collective-permute-start(bf16[528,128]{1,0:T(8,128)(2,1)S(1)} %get-tuple-element.25), channel_id=1, source_target_pairs={{0,25},{1,29},{2,27},{3,31},{4,24},{5,28},{6,26},{7,30},{8,17},{9,... | collective-permute-start | bytes 405512 | tf_op jit(solution)/shard_map/ppermute | solution.py:356
  6.9 0.1 collective-permute-start.3
  6.9 2.3 %shard_map.127 = (bf16[128,2048]{1,0:T(8,128)(2,1)S(1)}, bf16[128,512]{1,0:T(8,128)(2,1)S(1)}, bf16[784,128]{1,0:T(8,128)(2,1)S(1)}, bf16[784,128]{1,0:T(8,128)(2,1)S(1)}) custom-call(bf16[1,128,512]{2,1,0:T(8,128)(2,1)} %keys_ref.1, bf16[1,128,512]{2,1,0:T(8,128)(2,1)} %values_ref.1, bf16[16,128]{1,0:T(8,128)(2,1)S(1)} %broadcast_in_dim.4.refs_2_.tag_ref, ...), custom_call_target="tpu_custom_call" | custom-call | flops 3000000000 | bytes 1 | tf_op jit(solution)/shard_map/pallas_call | solution.py:307
  9.3 1.7 %collective-permute-start = (bf16[784,128]{1,0:T(8,128)(2,1)S(1)}, bf16[784,128]{1,0:T(8,128)(2,1)S(1)}, u32[]{:S(2)}, u32[]{:S(2)}) collective-permute-start(bf16[784,128]{1,0:T(8,128)(2,1)S(1)} %get-tuple-element.23), channel_id=1, source_target_pairs={{0,9},{1,13},{2,11},{3,15},{4,8},{5,12},{6,10},{7,14},{8,1},{9,5},... | collective-permute-start | bytes 602120 | tf_op jit(solution)/shard_map/ppermute | solution.py:356
  11.0 0.2 collective-permute-start.1
  11.2 3.2 %shard_map.128 = (f32[512,128]{1,0:T(8,128)S(1)}, f32[8,128]{1,0:T(8,128)S(1)}) custom-call(bf16[128,2048]{1,0:T(8,128)(2,1)S(1)} %get-tuple-element.19.normed_ref, bf16[128,512]{1,0:T(8,128)(2,1)S(1)} %get-tuple-element.20.query_ref, s32[1,128]{1,0:T(1,128)} %refs_0_.3, bf16[2048,512]{1,0:T(8,128)(2,1)} %refs_1_.3, bf16[2048,512]{1,0:T(8,128)(2,1)} %refs_2_.1), custom_call_target="tpu_custom_call" | custom-call | flops 10000000000 | bytes 1 | tf_op jit(solution)/shard_map/pallas_call | solution.py:307
  14.5 0.0 collective-permute-done.2.refs_0_
  14.5 5.9 %collective-permute-done.3.refs_1_ = bf16[528,128]{1,0:T(8,128)(2,1)S(1)} collective-permute-done((bf16[528,128]{1,0:T(8,128)(2,1)S(1)}, bf16[528,128]{1,0:T(8,128)(2,1)S(1)}, u32[]{:S(2)}, u32[]{:S(2)}) %collective-permute-start.3) | collective-permute-done | bytes 135200 | tf_op jit(solution)/shard_map/ppermute | solution.py:356
  20.5 0.1 collective-permute-start.6
  20.5 0.4 collective-permute-done.refs_0_
  20.9 0.2 collective-permute-start.4
  21.1 0.0 collective-permute-done.1.refs_1_
  21.1 0.4 %collective-permute-start.5 = (bf16[528,128]{1,0:T(8,128)(2,1)S(1)}, bf16[528,128]{1,0:T(8,128)(2,1)S(1)}, u32[]{:S(2)}, u32[]{:S(2)}) collective-permute-start(bf16[528,128]{1,0:T(8,128)(2,1)S(1)} %slice.9), channel_id=1, source_target_pairs={{0,1},{1,0},{2,3},{3,2},{4,5},{5,4},{6,7},{7,6},{8,9},{9,8},{10,11... | collective-permute-start | bytes 405512 | tf_op jit(solution)/shard_map/ppermute | solution.py:362
  21.6 0.7 %shard_map.131 = (f32[8,512]{1,0:T(8,128)S(1)}, f32[128,512]{1,0:T(8,128)S(1)}) custom-call(bf16[784,128]{1,0:T(8,128)(2,1)S(1)} %collective-permute-done.refs_0_, bf16[784,128]{1,0:T(8,128)(2,1)S(1)} %collective-permute-done.1.refs_1_, bf16[1056,128]{1,0:T(8,128)(2,1)S(1)} %shard_map.130.refs_2_), custom_call_target="tpu_custom_call" | custom-call | flops 1000000000 | bytes 1 | tf_op jit(solution)/shard_map/pallas_call | solution.py:307
  22.3 0.0 copy-start
  22.3 0.1 collective-permute-done.4.refs_4_
  22.3 0.2 collective-permute-done.5.refs_5_
  22.6 0.0 collective-permute-done.6.refs_6_
  22.6 0.8 %shard_map.132 = (bf16[272,128]{1,0:T(8,128)(2,1)S(1)}, bf16[272,128]{1,0:T(8,128)(2,1)S(1)}) custom-call(bf16[784,128]{1,0:T(8,128)(2,1)S(1)} %collective-permute-done.refs_0_, bf16[784,128]{1,0:T(8,128)(2,1)S(1)} %collective-permute-done.1.refs_1_, f32[8,512]{1,0:T(8,128)S(1)} %get-tuple-element.27.refs_2_, f32[128,512]{1,0:T(8,128)S(1)} %get-tuple-element.28.refs_3_, ...), custom_call_target="tpu_custom_call" | custom-call | flops 1000000000 | bytes 1 | tf_op jit(solution)/shard_map/pallas_call | solution.py:307
  23.4 0.3 collective-permute-start.7
  23.7 0.7 %collective-permute-start.8 = (bf16[272,128]{1,0:T(8,128)(2,1)S(1)}, bf16[272,128]{1,0:T(8,128)(2,1)S(1)}, u32[]{:S(2)}, u32[]{:S(2)}) collective-permute-start(bf16[272,128]{1,0:T(8,128)(2,1)S(1)} %get-tuple-element.30), channel_id=1, source_target_pairs={{1,0},{5,1},{3,2},{7,3},{0,4},{4,5},{2,6},{6,7},{9,8},{13,9},{11,1... | collective-permute-start | bytes 208904 | tf_op jit(solution)/shard_map/ppermute | solution.py:356
  24.3 2.8 %collective-permute-done.7.refs_0_ = bf16[272,128]{1,0:T(8,128)(2,1)S(1)} collective-permute-done((bf16[272,128]{1,0:T(8,128)(2,1)S(1)}, bf16[272,128]{1,0:T(8,128)(2,1)S(1)}, u32[]{:S(2)}, u32[]{:S(2)}) %collective-permute-start.7) | collective-permute-done | bytes 69664 | tf_op jit(solution)/shard_map/ppermute | solution.py:356
  27.2 0.0 collective-permute-done.8.refs_1_
  27.2 0.0 copy-done
  27.2 0.0 copy-start.1
  27.2 0.7 %shard_map.133 = (f32[64,2048]{1,0:T(8,128)S(1)}, bf16[64,2048]{1,0:T(8,128)(2,1)S(1)}) custom-call(f32[512,128]{1,0:T(8,128)S(1)} %get-tuple-element.21.sum_ref, f32[8,128]{1,0:T(8,128)S(1)} %get-tuple-element.22._.log_ref, bf16[512,2048]{1,0:T(8,128)(2,1)S(1)} %copy-done, bf16[272,128]{1,0:T(8,128)(2,1)S(1)} %collective-permute-done.7.refs_0_, ...), custom_call_target="tpu_custom_call" | custom-call | flops 1000000000 | bytes 1 | tf_op jit(solution)/shard_map/pallas_call | solution.py:307
  27.9 1.3 %collective-permute-start.9 = (bf16[64,2048]{1,0:T(8,128)(2,1)S(1)}, bf16[64,2048]{1,0:T(8,128)(2,1)S(1)}, u32[]{:S(2)}, u32[]{:S(2)}) collective-permute-start(bf16[64,2048]{1,0:T(8,128)(2,1)S(1)} %get-tuple-element.32), channel_id=1, source_target_pairs={{0,1},{1,0},{2,3},{3,2},{4,5},{5,4},{6,7},{7,6},{8,9},{9,8},{10,11... | collective-permute-start | bytes 786440 | tf_op jit(solution)/shard_map/ppermute | solution.py:362
  29.1 1.2 %collective-permute-done.9 = bf16[64,2048]{1,0:T(8,128)(2,1)S(1)} collective-permute-done((bf16[64,2048]{1,0:T(8,128)(2,1)S(1)}, bf16[64,2048]{1,0:T(8,128)(2,1)S(1)}, u32[]{:S(2)}, u32[]{:S(2)}) %collective-permute-start.9) | collective-permute-done | bytes 262176 | tf_op jit(solution)/shard_map/ppermute | solution.py:362
  30.3 1.6 %collective-permute-start.10 = (bf16[64,2048]{1,0:T(8,128)(2,1)S(1)}, bf16[64,2048]{1,0:T(8,128)(2,1)S(1)}, u32[]{:S(2)}, u32[]{:S(2)}) collective-permute-start(bf16[64,2048]{1,0:T(8,128)(2,1)S(1)} %add_convert_fusion.1), channel_id=1, source_target_pairs={{0,2},{1,3},{2,0},{3,1},{4,6},{5,7},{6,4},{7,5},{8,10},{9,11},{10,... | collective-permute-start | bytes 786440 | tf_op jit(solution)/shard_map/ppermute | solution.py:362
  31.9 7.1 %collective-permute-done.10 = bf16[64,2048]{1,0:T(8,128)(2,1)S(1)} collective-permute-done((bf16[64,2048]{1,0:T(8,128)(2,1)S(1)}, bf16[64,2048]{1,0:T(8,128)(2,1)S(1)}, u32[]{:S(2)}, u32[]{:S(2)}) %collective-permute-start.10) | collective-permute-done | bytes 262176 | tf_op jit(solution)/shard_map/ppermute | solution.py:362
  39.0 0.0 copy-done.1
  39.0 0.1 add_convert_fusion.half_ref
  39.1 0.1 collective-permute-start.11
  39.2 0.7 %shard_map.134._ = bf16[128,2048]{1,0:T(8,128)(2,1)} custom-call(bf16[64,2048]{1,0:T(8,128)(2,1)S(1)} %add_convert_fusion.half_ref), custom_call_target="tpu_custom_call" | custom-call | flops 1000000000 | bytes 1 | tf_op jit(solution)/shard_map/pallas_call | solution.py:307
  39.9 0.8 %collective-permute-done.11.half_ref = bf16[64,2048]{1,0:T(8,128)(2,1)S(1)} collective-permute-done((bf16[64,2048]{1,0:T(8,128)(2,1)S(1)}, bf16[64,2048]{1,0:T(8,128)(2,1)S(1)}, u32[]{:S(2)}, u32[]{:S(2)}) %collective-permute-start.11) | collective-permute-done | bytes 262176 | tf_op jit(solution)/shard_map/ppermute | solution.py:362
  40.7 0.7 %shard_map.135 = bf16[128,2048]{1,0:T(8,128)(2,1)} custom-call(bf16[64,2048]{1,0:T(8,128)(2,1)S(1)} %collective-permute-done.11.half_ref, bf16[128,2048]{1,0:T(8,128)(2,1)} %shard_map.134._), custom_call_target="tpu_custom_call", output_to_operand_aliasing={{}: (1, {})} | custom-call | flops 1000000000 | bytes 1 | tf_op jit(solution)/shard_map/pallas_call | solution.py:307
  (5 shorter events, 0.1 us)
Async XLA Ops:
  2.3 12.2 %collective-permute-start.2 = (bf16[528,128]{1,0:T(8,128)(2,1)S(1)}, bf16[528,128]{1,0:T(8,128)(2,1)S(1)}, u32[]{:S(2)}, u32[]{:S(2)}) collective-permute-start(bf16[528,128]{1,0:T(8,128)(2,1)S(1)} %get-tuple-element.25), channel_id=1, source_target_pairs={{0,25},{1,29},{2,27},{3,31},{4,24},{5,28},{6,26},{7,30},{8,17},{9,... | collective-permute-start | bytes 405512 | tf_op jit(solution)/shard_map/ppermute | solution.py:356
  6.9 13.6 %collective-permute-start.3 = (bf16[528,128]{1,0:T(8,128)(2,1)S(1)}, bf16[528,128]{1,0:T(8,128)(2,1)S(1)}, u32[]{:S(2)}, u32[]{:S(2)}) collective-permute-start(bf16[528,128]{1,0:T(8,128)(2,1)S(1)} %get-tuple-element.26), channel_id=1, source_target_pairs={{0,17},{1,21},{2,19},{3,23},{4,16},{5,20},{6,18},{7,22},{8,25},{9,... | collective-permute-start | bytes 405512 | tf_op jit(solution)/shard_map/ppermute | solution.py:356
  9.3 11.6 %collective-permute-start = (bf16[784,128]{1,0:T(8,128)(2,1)S(1)}, bf16[784,128]{1,0:T(8,128)(2,1)S(1)}, u32[]{:S(2)}, u32[]{:S(2)}) collective-permute-start(bf16[784,128]{1,0:T(8,128)(2,1)S(1)} %get-tuple-element.23), channel_id=1, source_target_pairs={{0,9},{1,13},{2,11},{3,15},{4,8},{5,12},{6,10},{7,14},{8,1},{9,5},... | collective-permute-start | bytes 602120 | tf_op jit(solution)/shard_map/ppermute | solution.py:356
  11.0 10.1 %collective-permute-start.1 = (bf16[784,128]{1,0:T(8,128)(2,1)S(1)}, bf16[784,128]{1,0:T(8,128)(2,1)S(1)}, u32[]{:S(2)}, u32[]{:S(2)}) collective-permute-start(bf16[784,128]{1,0:T(8,128)(2,1)S(1)} %get-tuple-element.24), channel_id=1, source_target_pairs={{0,1},{1,5},{2,3},{3,7},{4,0},{5,4},{6,2},{7,6},{8,9},{9,13},{10,1... | collective-permute-start | bytes 602120 | tf_op jit(solution)/shard_map/ppermute | solution.py:356
  20.5 2.1 %collective-permute-start.6 = (bf16[1056,128]{1,0:T(8,128)(2,1)S(1)}, bf16[1056,128]{1,0:T(8,128)(2,1)S(1)}, u32[]{:S(2)}, u32[]{:S(2)}) collective-permute-start(bf16[1056,128]{1,0:T(8,128)(2,1)S(1)} %shard_map.130.refs_2_), channel_id=1, source_target_pairs={{0,1},{1,0},{2,3},{3,2},{4,5},{5,4},{6,7},{7,6},{8,9},{9,8},{10,11... | collective-permute-start | bytes 811016 | tf_op jit(solution)/shard_map/ppermute | solution.py:362
  20.9 1.4 %collective-permute-start.4 = (bf16[528,128]{1,0:T(8,128)(2,1)S(1)}, bf16[528,128]{1,0:T(8,128)(2,1)S(1)}, u32[]{:S(2)}, u32[]{:S(2)}) collective-permute-start(bf16[528,128]{1,0:T(8,128)(2,1)S(1)} %slice.8), channel_id=1, source_target_pairs={{0,1},{1,0},{2,3},{3,2},{4,5},{5,4},{6,7},{7,6},{8,9},{9,8},{10,11... | collective-permute-start | bytes 405512 | tf_op jit(solution)/shard_map/ppermute | solution.py:362
  21.1 1.4 %collective-permute-start.5 = (bf16[528,128]{1,0:T(8,128)(2,1)S(1)}, bf16[528,128]{1,0:T(8,128)(2,1)S(1)}, u32[]{:S(2)}, u32[]{:S(2)}) collective-permute-start(bf16[528,128]{1,0:T(8,128)(2,1)S(1)} %slice.9), channel_id=1, source_target_pairs={{0,1},{1,0},{2,3},{3,2},{4,5},{5,4},{6,7},{7,6},{8,9},{9,8},{10,11... | collective-permute-start | bytes 405512 | tf_op jit(solution)/shard_map/ppermute | solution.py:362
  22.3 4.9 %copy-start = (bf16[512,2048]{1,0:T(8,128)(2,1)S(1)}, bf16[512,2048]{1,0:T(8,128)(2,1)}, u32[]{:S(2)}) copy-start(bf16[512,2048]{1,0:T(8,128)(2,1)} %w_out_ref.1) | copy-start | bytes 6291460
  23.4 3.8 %collective-permute-start.7 = (bf16[272,128]{1,0:T(8,128)(2,1)S(1)}, bf16[272,128]{1,0:T(8,128)(2,1)S(1)}, u32[]{:S(2)}, u32[]{:S(2)}) collective-permute-start(bf16[272,128]{1,0:T(8,128)(2,1)S(1)} %get-tuple-element.29), channel_id=1, source_target_pairs={{9,0},{13,1},{11,2},{15,3},{8,4},{12,5},{10,6},{14,7},{1,8},{5,9},... | collective-permute-start | bytes 208904 | tf_op jit(solution)/shard_map/ppermute | solution.py:356
  23.7 3.5 %collective-permute-start.8 = (bf16[272,128]{1,0:T(8,128)(2,1)S(1)}, bf16[272,128]{1,0:T(8,128)(2,1)S(1)}, u32[]{:S(2)}, u32[]{:S(2)}) collective-permute-start(bf16[272,128]{1,0:T(8,128)(2,1)S(1)} %get-tuple-element.30), channel_id=1, source_target_pairs={{1,0},{5,1},{3,2},{7,3},{0,4},{4,5},{2,6},{6,7},{9,8},{13,9},{11,1... | collective-permute-start | bytes 208904 | tf_op jit(solution)/shard_map/ppermute | solution.py:356
  27.2 11.8 %copy-start.1 = (bf16[128,2048]{1,0:T(8,128)(2,1)S(1)}, bf16[128,2048]{1,0:T(8,128)(2,1)}, u32[]{:S(2)}) copy-start(bf16[128,2048]{1,0:T(8,128)(2,1)} %refs_3_.1) | copy-start | bytes 1572868
  27.9 2.4 %collective-permute-start.9 = (bf16[64,2048]{1,0:T(8,128)(2,1)S(1)}, bf16[64,2048]{1,0:T(8,128)(2,1)S(1)}, u32[]{:S(2)}, u32[]{:S(2)}) collective-permute-start(bf16[64,2048]{1,0:T(8,128)(2,1)S(1)} %get-tuple-element.32), channel_id=1, source_target_pairs={{0,1},{1,0},{2,3},{3,2},{4,5},{5,4},{6,7},{7,6},{8,9},{9,8},{10,11... | collective-permute-start | bytes 786440 | tf_op jit(solution)/shard_map/ppermute | solution.py:362
  30.3 8.7 %collective-permute-start.10 = (bf16[64,2048]{1,0:T(8,128)(2,1)S(1)}, bf16[64,2048]{1,0:T(8,128)(2,1)S(1)}, u32[]{:S(2)}, u32[]{:S(2)}) collective-permute-start(bf16[64,2048]{1,0:T(8,128)(2,1)S(1)} %add_convert_fusion.1), channel_id=1, source_target_pairs={{0,2},{1,3},{2,0},{3,1},{4,6},{5,7},{6,4},{7,5},{8,10},{9,11},{10,... | collective-permute-start | bytes 786440 | tf_op jit(solution)/shard_map/ppermute | solution.py:362
  39.1 1.6 %collective-permute-start.11 = (bf16[64,2048]{1,0:T(8,128)(2,1)S(1)}, bf16[64,2048]{1,0:T(8,128)(2,1)S(1)}, u32[]{:S(2)}, u32[]{:S(2)}) collective-permute-start(bf16[64,2048]{1,0:T(8,128)(2,1)S(1)} %add_convert_fusion.half_ref), channel_id=1, source_target_pairs={{0,1},{1,0},{2,3},{3,2},{4,5},{5,4},{6,7},{7,6},{8,9},{9,8},{10,11... | collective-permute-start | bytes 786440 | tf_op jit(solution)/shard_map/ppermute | solution.py:362

commit v5 on v4

--- a/solution.py
+++ b/solution.py
@@ -53,10 +53,10 @@
     return pairs
 
 
-def far_kernel(per, keys_ref, values_ref, tag_ref, *refs):
-    outs, sems = refs[:2], refs[2]
+def pack_kernel(per, keys_ref, values_ref, tag_ref, *refs):
+    outs, sems = refs[:-1], refs[-1]
     pairs = []
-    for bits, out in enumerate(outs):
+    for bits, out in zip((1, 0, 1), outs):
         pairs += block_copies(per, bits, keys_ref, values_ref, out, 0)
     copies = start_all(pairs, sems)
     for out in outs:
@@ -82,8 +82,7 @@
     pairs = [(hidden_in.at[cut, :], hidden_ref.at[cut, :]) for cut in row_cuts]
     pairs += list(zip(sources, held[2:]))
     pairs += [(w_query.at[cut, :], w_query_ref.at[cut, :]) for cut in w_cuts]
-    for bits, out in enumerate(outs):
-        pairs += block_copies(per, bits, keys_ref, values_ref, out, per * rows)
+    pairs += block_copies(per, 0, keys_ref, values_ref, outs[0], per * rows)
     copies = start_all(pairs, sems)
     small = copies[ROW_CUTS : ROW_CUTS + 4]
     weights = copies[ROW_CUTS + 4 : ROW_CUTS + 4 + W_CUTS]
@@ -115,8 +114,7 @@
     for bits, out in enumerate(outs):
         for i in range(per):
             out[i * rows : (i + 1) * rows, :] = query_ref[:, pl.ds(head_at(bits, i, per), HD)]
-        at = per * (rows + 2 * HD)
-        out[at : at + NOTE_ROWS, :] = notes
+        out[out.shape[0] - NOTE_ROWS : out.shape[0], :] = notes
     for copy in copies[ROW_CUTS + 4 + W_CUTS :]:
         copy.wait()
 
@@ -180,8 +178,7 @@
     queries = [
         jnp.concatenate([ref[i * rows : (i + 1) * rows, :] for ref in asks], axis=0) for i in range(per)
     ]
-    at = per * (rows + 2 * HD)
-    notes = [ref[at : at + NOTE_ROWS, :].astype(jnp.float32)[1:2, :] for ref in asks]
+    notes = [ref[ref.shape[0] - NOTE_ROWS : ref.shape[0], :].astype(jnp.float32)[1:2, :] for ref in asks]
     return queries, jnp.concatenate(notes, axis=1)
 
 
@@ -196,13 +193,12 @@
 
 
 def first_kernel(rows, per, *refs):
-    asks, fars, (state_ref, sum_ref) = refs[:2], refs[2:-2], refs[-2:]
+    asks, early, (state_ref, sum_ref) = refs[:2], refs[2], refs[3:]
     queries, group = questions(asks, rows, per)
     tokens = group.shape[1]
-    found = [block_scores(ref, per * rows, queries, group) for ref in asks]
     step = 2 * HD * per + NOTE_ROWS
-    for ref in fars:
-        found += [block_scores(ref, at, queries, group) for at in range(0, ref.shape[0], step)]
+    found = [block_scores(asks[1], per * rows, queries, group)]
+    found += [block_scores(early, at, queries, group) for at in range(0, early.shape[0], step)]
     for i in range(per):
         carry = (
             jnp.full((1, tokens), -big, jnp.float32),
@@ -226,12 +222,12 @@
     found = [
         block_scores(ref, at, queries, group)
         for ref in blocks
-        if ref.shape[0] <= 2 * step
+        if ref.shape[0] <= 3 * step
         for at in range(0, ref.shape[0], step)
     ]
     carry = tuple(absorb(carry[i], [block[i] for block in found]) for i in range(per))
     for ref in blocks:
-        if ref.shape[0] > 2 * step:
+        if ref.shape[0] > 3 * step:
 
             def body(b, state, ref=ref):
                 block = block_scores(ref, pl.multiple_of(b * step, NOTE_ROWS), queries, group)
@@ -363,19 +359,18 @@
 
     group = jnp.where(block_live == 1, block_slot * GROUPS // n_blk, -1).astype(bf16)
     tag = jnp.broadcast_to(group, (NOTE_ROWS, HD))
-    fars = []
-    if n_blk == 8:
-        fars = call(
-            functools.partial(far_kernel, per),
-            [((step, HD), bf16)] * 2,
-            (HBM, HBM, VMEM),
-            [pltpu.SemaphoreType.DMA((4 * per,))],
-        )(prefix_keys, prefix_values, tag)
-        fars = [exchange(fars[k], k, far=1) for k in ORDER]
+    early = call(
+        functools.partial(pack_kernel, per),
+        [((step, HD), bf16)] * (3 if n_blk == 8 else 1),
+        (HBM, HBM, VMEM),
+        [pltpu.SemaphoreType.DMA(((6 if n_blk == 8 else 2) * per,))],
+    )(prefix_keys, prefix_values, tag)
+    near = exchange(early[0], 1)
+    fars = [exchange(early[1 + k], k, far=1) for k in (0, 1)] if n_blk == 8 else []
     normed, query, *packs = call(
         functools.partial(query_kernel, per),
         [((rows, width), bf16), ((rows, local_width), bf16)]
-        + [((per * rows + step, HD), bf16)] * 2,
+        + [((per * rows + n, HD), bf16) for n in (step, NOTE_ROWS)],
         (HBM, HBM, VMEM) + (HBM,) * 6,
         [
             pltpu.VMEM((rows, width), bf16),
@@ -384,7 +379,7 @@
             pltpu.VMEM((1, width), f32),
             pltpu.VMEM(segment.shape, i32),
             pltpu.SMEM(request_group.shape, i32),
-            pltpu.SemaphoreType.DMA((4 + ROW_CUTS + W_CUTS + 2 * heads,)),
+            pltpu.SemaphoreType.DMA((4 + ROW_CUTS + W_CUTS + 2 * per,)),
         ],
         cost=Q,
     )(
@@ -411,15 +406,18 @@
         ],
         cost=SFX,
     )(normed, query, segment, w_key, w_value)
+    joined = near
     if fars:
-        fars = list(call(join_kernel, [((2 * step, HD), bf16)], (VMEM,) * 3, cost=JOIN)(suffix_log, *fars))
-
-    blocks = [x[per * rows :] for x in asks] + fars
+        join = call(join_kernel, [((3 * step, HD), bf16)], (VMEM,) * 4, cost=JOIN)
+        joined = join(suffix_log, fars[0], near, fars[1])[0]
+
+    blocks = [joined, asks[1][per * rows :]]
     state, summed = call(
         functools.partial(first_kernel, rows, per),
         [((8, heads * rows), f32), ((HD, heads * rows), f32)],
-        (VMEM,) * (2 + len(fars)),
-    )(*asks, *fars)
+        (VMEM,) * 3,
+        cost=30,
+    )(*asks, joined)
     others = [across_mp(x, 1) for x in blocks]
     bit = 4
     while bit < n_blk and not fars:

time: 41.6 us -> 40.7 us (0.978)
  waiting for transfers between devices: 18.5 us -> 15.5 us
  starting transfers between devices: 11.2 us -> 13.2 us
    ppermute x6 -> x7, waiting for transfers between devices: 9.16 us -> 5.87 us  [exchange(): return lax.ppermute(x, ('blk', 'mp'), pairs)]
    ppermute x6 -> x7, starting transfers between devices: 7.53 us -> 9.6 us  [exchange(): return lax.ppermute(x, ('blk', 'mp'), pairs)]
    ppermute x6 -> x5, waiting for transfers between devices: 9.31 us -> 9.62 us  [across_mp(): return lax.ppermute(x, 'mp', [(i, i ^ bit) for i in range(n_mp)])]
    ppermute x6 -> x5, starting transfers between devices: 3.65 us -> 3.59 us  [across_mp(): return lax.ppermute(x, 'mp', [(i, i ^ bit) for i in range(n_mp)])]
  transfers between devices with their start and end apart: 12 -> 12, of which waited for: 8 -> 7; matrix products, arithmetic and copies ran while one was open for 0% -> 0% of each run, Pallas kernels for 17% -> 17%
where the time goes in v5:
time: 40.7 us; the launch traced here: 40.5 us
  waiting for transfers between devices  15.5 us (38%)
  starting transfers between devices  13.2 us (32%)
  Pallas kernels  10.2 us (25%)
  between operations  1.46 us (4%)
    pallas_call x9, Pallas kernels, run(): return inner(*pinned)  10.2 us
    ppermute x5, waiting for transfers between devices, across_mp(): return lax.ppermute(x, 'mp', [(i, i ^ bit) for i in range(n_mp)])  9.62 us
    ppermute x7, starting transfers between devices, exchange(): return lax.ppermute(x, ('blk', 'mp'), pairs)  9.6 us
    ppermute x7, waiting for transfers between devices, exchange(): return lax.ppermute(x, ('blk', 'mp'), pairs)  5.87 us
    ppermute x5, starting transfers between devices, across_mp(): return lax.ppermute(x, 'mp', [(i, i ^ bit) for i in range(n_mp)])  3.59 us
  transfers between devices with their start and end apart: 12, of which 7 were waited for; matrix products, arithmetic and copies ran while one was open for 0% of the time, Pallas kernels for 17%

profile of v5, /device:TPU:0, one launch (start us, length us, event | category | flops | bytes accessed | tf_op | source)
XLA Modules:
  0.0 40.5 jit_solution(13723997683938626142)
XLA Ops:
  1.3 1.1 %shard_map.129 = (bf16[528,128]{1,0:T(8,128)(2,1)S(1)}, bf16[528,128]{1,0:T(8,128)(2,1)S(1)}, bf16[528,128]{1,0:T(8,128)(2,1)S(1)}) custom-call(bf16[1,128,512]{2,1,0:T(8,128)(2,1)} %keys_ref.1, bf16[1,128,512]{2,1,0:T(8,128)(2,1)} %values_ref.1, bf16[16,128]{1,0:T(8,128)(2,1)S(1)} %broadcast_in_dim.4.refs_2_.tag_ref), custom_call_target="tpu_custom_call" | custom-call | flops 1000000000 | bytes 1 | tf_op jit(solution)/shard_map/pallas_call | solution.py:303
  2.4 3.5 %collective-permute-start.2 = (bf16[528,128]{1,0:T(8,128)(2,1)S(1)}, bf16[528,128]{1,0:T(8,128)(2,1)S(1)}, u32[]{:S(2)}, u32[]{:S(2)}) collective-permute-start(bf16[528,128]{1,0:T(8,128)(2,1)S(1)} %get-tuple-element.26), channel_id=1, source_target_pairs={{0,17},{1,21},{2,19},{3,23},{4,16},{5,20},{6,18},{7,22},{8,25},{9,... | collective-permute-start | bytes 405512 | tf_op jit(solution)/shard_map/ppermute | solution.py:352
  5.9 2.2 %collective-permute-start.3 = (bf16[528,128]{1,0:T(8,128)(2,1)S(1)}, bf16[528,128]{1,0:T(8,128)(2,1)S(1)}, u32[]{:S(2)}, u32[]{:S(2)}) collective-permute-start(bf16[528,128]{1,0:T(8,128)(2,1)S(1)} %get-tuple-element.27), channel_id=1, source_target_pairs={{0,9},{1,13},{2,11},{3,15},{4,8},{5,12},{6,10},{7,14},{8,1},{9,5},... | collective-permute-start | bytes 405512 | tf_op jit(solution)/shard_map/ppermute | solution.py:352
  8.2 0.5 %collective-permute-start.4 = (bf16[528,128]{1,0:T(8,128)(2,1)S(1)}, bf16[528,128]{1,0:T(8,128)(2,1)S(1)}, u32[]{:S(2)}, u32[]{:S(2)}) collective-permute-start(bf16[528,128]{1,0:T(8,128)(2,1)S(1)} %get-tuple-element.28), channel_id=1, source_target_pairs={{0,25},{1,29},{2,27},{3,31},{4,24},{5,28},{6,26},{7,30},{8,17},{9,... | collective-permute-start | bytes 405512 | tf_op jit(solution)/shard_map/ppermute | solution.py:352
  8.7 2.3 %shard_map.127 = (bf16[128,2048]{1,0:T(8,128)(2,1)S(1)}, bf16[128,512]{1,0:T(8,128)(2,1)S(1)}, bf16[784,128]{1,0:T(8,128)(2,1)S(1)}, bf16[272,128]{1,0:T(8,128)(2,1)S(1)}) custom-call(bf16[1,128,512]{2,1,0:T(8,128)(2,1)} %keys_ref.1, bf16[1,128,512]{2,1,0:T(8,128)(2,1)} %values_ref.1, bf16[16,128]{1,0:T(8,128)(2,1)S(1)} %broadcast_in_dim.4.refs_2_.tag_ref, ...), custom_call_target="tpu_custom_call" | custom-call | flops 3000000000 | bytes 1 | tf_op jit(solution)/shard_map/pallas_call | solution.py:303
  11.0 0.2 collective-permute-start.1
  11.2 0.8 %collective-permute-start = (bf16[272,128]{1,0:T(8,128)(2,1)S(1)}, bf16[272,128]{1,0:T(8,128)(2,1)S(1)}, u32[]{:S(2)}, u32[]{:S(2)}) collective-permute-start(bf16[272,128]{1,0:T(8,128)(2,1)S(1)} %get-tuple-element.24), channel_id=1, source_target_pairs={{0,9},{1,13},{2,11},{3,15},{4,8},{5,12},{6,10},{7,14},{8,1},{9,5},... | collective-permute-start | bytes 208904 | tf_op jit(solution)/shard_map/ppermute | solution.py:352
  11.9 3.3 %shard_map.128 = (f32[512,128]{1,0:T(8,128)S(1)}, f32[8,128]{1,0:T(8,128)S(1)}) custom-call(bf16[128,2048]{1,0:T(8,128)(2,1)S(1)} %get-tuple-element.20.normed_ref, bf16[128,512]{1,0:T(8,128)(2,1)S(1)} %get-tuple-element.21.query_ref, s32[1,128]{1,0:T(1,128)} %refs_0_.3, bf16[2048,512]{1,0:T(8,128)(2,1)} %refs_1_.3, bf16[2048,512]{1,0:T(8,128)(2,1)} %refs_2_.1), custom_call_target="tpu_custom_call" | custom-call | flops 10000000000 | bytes 1 | tf_op jit(solution)/shard_map/pallas_call | solution.py:303
  15.2 0.0 collective-permute-done.2.refs_0_
  15.2 0.0 collective-permute-done.3.refs_1_
  15.2 3.8 %collective-permute-done.4.refs_2_ = bf16[528,128]{1,0:T(8,128)(2,1)S(1)} collective-permute-done((bf16[528,128]{1,0:T(8,128)(2,1)S(1)}, bf16[528,128]{1,0:T(8,128)(2,1)S(1)}, u32[]{:S(2)}, u32[]{:S(2)}) %collective-permute-start.4) | collective-permute-done | bytes 135200 | tf_op jit(solution)/shard_map/ppermute | solution.py:352
  19.0 0.1 collective-permute-start.5
  19.1 0.0 collective-permute-done.1.refs_1_
  19.1 0.6 %collective-permute-start.6 = (bf16[528,128]{1,0:T(8,128)(2,1)S(1)}, bf16[528,128]{1,0:T(8,128)(2,1)S(1)}, u32[]{:S(2)}, u32[]{:S(2)}) collective-permute-start(bf16[528,128]{1,0:T(8,128)(2,1)S(1)} %slice.4), channel_id=1, source_target_pairs={{0,1},{1,0},{2,3},{3,2},{4,5},{5,4},{6,7},{7,6},{8,9},{9,8},{10,11... | collective-permute-start | bytes 405512 | tf_op jit(solution)/shard_map/ppermute | solution.py:358
  19.7 0.0 collective-permute-done.refs_0_
  19.7 0.7 %shard_map.131 = (f32[8,512]{1,0:T(8,128)S(1)}, f32[128,512]{1,0:T(8,128)S(1)}) custom-call(bf16[272,128]{1,0:T(8,128)(2,1)S(1)} %collective-permute-done.refs_0_, bf16[784,128]{1,0:T(8,128)(2,1)S(1)} %collective-permute-done.1.refs_1_, bf16[1584,128]{1,0:T(8,128)(2,1)S(1)} %shard_map.130.refs_2_), custom_call_target="tpu_custom_call" | custom-call | flops 30000001024 | bytes 1 | tf_op jit(solution)/shard_map/pallas_call | solution.py:303
  20.4 0.0 copy-start
  20.4 0.6 %collective-permute-done.6.refs_5_ = bf16[528,128]{1,0:T(8,128)(2,1)S(1)} collective-permute-done((bf16[528,128]{1,0:T(8,128)(2,1)S(1)}, bf16[528,128]{1,0:T(8,128)(2,1)S(1)}, u32[]{:S(2)}, u32[]{:S(2)}) %collective-permute-start.6) | collective-permute-done | bytes 135200 | tf_op jit(solution)/shard_map/ppermute | solution.py:358
  21.0 0.0 collective-permute-done.5.refs_4_
  21.0 0.8 %shard_map.132 = (bf16[272,128]{1,0:T(8,128)(2,1)S(1)}, bf16[272,128]{1,0:T(8,128)(2,1)S(1)}) custom-call(bf16[272,128]{1,0:T(8,128)(2,1)S(1)} %collective-permute-done.refs_0_, bf16[784,128]{1,0:T(8,128)(2,1)S(1)} %collective-permute-done.1.refs_1_, f32[8,512]{1,0:T(8,128)S(1)} %get-tuple-element.29.refs_2_, f32[128,512]{1,0:T(8,128)S(1)} %get-tuple-element.30.refs_3_, ...), custom_call_target="tpu_custom_call" | custom-call | flops 1000000000 | bytes 1 | tf_op jit(solution)/shard_map/pallas_call | solution.py:303
  21.8 2.1 %collective-permute-start.7 = (bf16[272,128]{1,0:T(8,128)(2,1)S(1)}, bf16[272,128]{1,0:T(8,128)(2,1)S(1)}, u32[]{:S(2)}, u32[]{:S(2)}) collective-permute-start(bf16[272,128]{1,0:T(8,128)(2,1)S(1)} %get-tuple-element.31), channel_id=1, source_target_pairs={{9,0},{13,1},{11,2},{15,3},{8,4},{12,5},{10,6},{14,7},{1,8},{5,9},... | collective-permute-start | bytes 208904 | tf_op jit(solution)/shard_map/ppermute | solution.py:352
  23.9 0.3 collective-permute-start.8
  24.2 1.9 %collective-permute-done.7.refs_0_ = bf16[272,128]{1,0:T(8,128)(2,1)S(1)} collective-permute-done((bf16[272,128]{1,0:T(8,128)(2,1)S(1)}, bf16[272,128]{1,0:T(8,128)(2,1)S(1)}, u32[]{:S(2)}, u32[]{:S(2)}) %collective-permute-start.7) | collective-permute-done | bytes 69664 | tf_op jit(solution)/shard_map/ppermute | solution.py:352
  26.1 0.2 collective-permute-done.8.refs_1_
  26.3 0.0 copy-done
  26.3 0.0 copy-start.1
  26.3 0.7 %shard_map.133 = (f32[64,2048]{1,0:T(8,128)S(1)}, bf16[64,2048]{1,0:T(8,128)(2,1)S(1)}) custom-call(f32[512,128]{1,0:T(8,128)S(1)} %get-tuple-element.22.sum_ref, f32[8,128]{1,0:T(8,128)S(1)} %get-tuple-element.23._.log_ref, bf16[512,2048]{1,0:T(8,128)(2,1)S(1)} %copy-done, bf16[272,128]{1,0:T(8,128)(2,1)S(1)} %collective-permute-done.7.refs_0_, ...), custom_call_target="tpu_custom_call" | custom-call | flops 1000000000 | bytes 1 | tf_op jit(solution)/shard_map/pallas_call | solution.py:303
  26.9 1.3 %collective-permute-start.9 = (bf16[64,2048]{1,0:T(8,128)(2,1)S(1)}, bf16[64,2048]{1,0:T(8,128)(2,1)S(1)}, u32[]{:S(2)}, u32[]{:S(2)}) collective-permute-start(bf16[64,2048]{1,0:T(8,128)(2,1)S(1)} %get-tuple-element.34), channel_id=1, source_target_pairs={{0,1},{1,0},{2,3},{3,2},{4,5},{5,4},{6,7},{7,6},{8,9},{9,8},{10,11... | collective-permute-start | bytes 786440 | tf_op jit(solution)/shard_map/ppermute | solution.py:358
  28.2 1.2 %collective-permute-done.9 = bf16[64,2048]{1,0:T(8,128)(2,1)S(1)} collective-permute-done((bf16[64,2048]{1,0:T(8,128)(2,1)S(1)}, bf16[64,2048]{1,0:T(8,128)(2,1)S(1)}, u32[]{:S(2)}, u32[]{:S(2)}) %collective-permute-start.9) | collective-permute-done | bytes 262176 | tf_op jit(solution)/shard_map/ppermute | solution.py:358
  29.4 1.6 %collective-permute-start.10 = (bf16[64,2048]{1,0:T(8,128)(2,1)S(1)}, bf16[64,2048]{1,0:T(8,128)(2,1)S(1)}, u32[]{:S(2)}, u32[]{:S(2)}) collective-permute-start(bf16[64,2048]{1,0:T(8,128)(2,1)S(1)} %add_convert_fusion.1), channel_id=1, source_target_pairs={{0,2},{1,3},{2,0},{3,1},{4,6},{5,7},{6,4},{7,5},{8,10},{9,11},{10,... | collective-permute-start | bytes 786440 | tf_op jit(solution)/shard_map/ppermute | solution.py:358
  31.1 7.0 %collective-permute-done.10 = bf16[64,2048]{1,0:T(8,128)(2,1)S(1)} collective-permute-done((bf16[64,2048]{1,0:T(8,128)(2,1)S(1)}, bf16[64,2048]{1,0:T(8,128)(2,1)S(1)}, u32[]{:S(2)}, u32[]{:S(2)}) %collective-permute-start.10) | collective-permute-done | bytes 262176 | tf_op jit(solution)/shard_map/ppermute | solution.py:358
  38.1 0.0 copy-done.1
  38.1 0.1 add_convert_fusion.half_ref
  38.2 0.1 collective-permute-start.11
  38.3 0.7 %shard_map.134._ = bf16[128,2048]{1,0:T(8,128)(2,1)} custom-call(bf16[64,2048]{1,0:T(8,128)(2,1)S(1)} %add_convert_fusion.half_ref), custom_call_target="tpu_custom_call" | custom-call | flops 1000000000 | bytes 1 | tf_op jit(solution)/shard_map/pallas_call | solution.py:303
  39.0 0.8 %collective-permute-done.11.half_ref = bf16[64,2048]{1,0:T(8,128)(2,1)S(1)} collective-permute-done((bf16[64,2048]{1,0:T(8,128)(2,1)S(1)}, bf16[64,2048]{1,0:T(8,128)(2,1)S(1)}, u32[]{:S(2)}, u32[]{:S(2)}) %collective-permute-start.11) | collective-permute-done | bytes 262176 | tf_op jit(solution)/shard_map/ppermute | solution.py:358
  39.8 0.7 %shard_map.135 = bf16[128,2048]{1,0:T(8,128)(2,1)} custom-call(bf16[64,2048]{1,0:T(8,128)(2,1)S(1)} %collective-permute-done.11.half_ref, bf16[128,2048]{1,0:T(8,128)(2,1)} %shard_map.134._), custom_call_target="tpu_custom_call", output_to_operand_aliasing={{}: (1, {})} | custom-call | flops 1000000000 | bytes 1 | tf_op jit(solution)/shard_map/pallas_call | solution.py:303
  (4 shorter events, 0.1 us)
Async XLA Ops:
  2.4 12.8 %collective-permute-start.2 = (bf16[528,128]{1,0:T(8,128)(2,1)S(1)}, bf16[528,128]{1,0:T(8,128)(2,1)S(1)}, u32[]{:S(2)}, u32[]{:S(2)}) collective-permute-start(bf16[528,128]{1,0:T(8,128)(2,1)S(1)} %get-tuple-element.26), channel_id=1, source_target_pairs={{0,17},{1,21},{2,19},{3,23},{4,16},{5,20},{6,18},{7,22},{8,25},{9,... | collective-permute-start | bytes 405512 | tf_op jit(solution)/shard_map/ppermute | solution.py:352
  5.9 9.3 %collective-permute-start.3 = (bf16[528,128]{1,0:T(8,128)(2,1)S(1)}, bf16[528,128]{1,0:T(8,128)(2,1)S(1)}, u32[]{:S(2)}, u32[]{:S(2)}) collective-permute-start(bf16[528,128]{1,0:T(8,128)(2,1)S(1)} %get-tuple-element.27), channel_id=1, source_target_pairs={{0,9},{1,13},{2,11},{3,15},{4,8},{5,12},{6,10},{7,14},{8,1},{9,5},... | collective-permute-start | bytes 405512 | tf_op jit(solution)/shard_map/ppermute | solution.py:352
  8.2 10.8 %collective-permute-start.4 = (bf16[528,128]{1,0:T(8,128)(2,1)S(1)}, bf16[528,128]{1,0:T(8,128)(2,1)S(1)}, u32[]{:S(2)}, u32[]{:S(2)}) collective-permute-start(bf16[528,128]{1,0:T(8,128)(2,1)S(1)} %get-tuple-element.28), channel_id=1, source_target_pairs={{0,25},{1,29},{2,27},{3,31},{4,24},{5,28},{6,26},{7,30},{8,17},{9,... | collective-permute-start | bytes 405512 | tf_op jit(solution)/shard_map/ppermute | solution.py:352
  11.0 8.2 %collective-permute-start.1 = (bf16[784,128]{1,0:T(8,128)(2,1)S(1)}, bf16[784,128]{1,0:T(8,128)(2,1)S(1)}, u32[]{:S(2)}, u32[]{:S(2)}) collective-permute-start(bf16[784,128]{1,0:T(8,128)(2,1)S(1)} %get-tuple-element.25), channel_id=1, source_target_pairs={{0,1},{1,5},{2,3},{3,7},{4,0},{5,4},{6,2},{7,6},{8,9},{9,13},{10,1... | collective-permute-start | bytes 602120 | tf_op jit(solution)/shard_map/ppermute | solution.py:352
  11.2 8.5 %collective-permute-start = (bf16[272,128]{1,0:T(8,128)(2,1)S(1)}, bf16[272,128]{1,0:T(8,128)(2,1)S(1)}, u32[]{:S(2)}, u32[]{:S(2)}) collective-permute-start(bf16[272,128]{1,0:T(8,128)(2,1)S(1)} %get-tuple-element.24), channel_id=1, source_target_pairs={{0,9},{1,13},{2,11},{3,15},{4,8},{5,12},{6,10},{7,14},{8,1},{9,5},... | collective-permute-start | bytes 208904 | tf_op jit(solution)/shard_map/ppermute | solution.py:352
  19.0 2.0 %collective-permute-start.5 = (bf16[1584,128]{1,0:T(8,128)(2,1)S(1)}, bf16[1584,128]{1,0:T(8,128)(2,1)S(1)}, u32[]{:S(2)}, u32[]{:S(2)}) collective-permute-start(bf16[1584,128]{1,0:T(8,128)(2,1)S(1)} %shard_map.130.refs_2_), channel_id=1, source_target_pairs={{0,1},{1,0},{2,3},{3,2},{4,5},{5,4},{6,7},{7,6},{8,9},{9,8},{10,11... | collective-permute-start | bytes 1216520 | tf_op jit(solution)/shard_map/ppermute | solution.py:358
  19.1 1.9 %collective-permute-start.6 = (bf16[528,128]{1,0:T(8,128)(2,1)S(1)}, bf16[528,128]{1,0:T(8,128)(2,1)S(1)}, u32[]{:S(2)}, u32[]{:S(2)}) collective-permute-start(bf16[528,128]{1,0:T(8,128)(2,1)S(1)} %slice.4), channel_id=1, source_target_pairs={{0,1},{1,0},{2,3},{3,2},{4,5},{5,4},{6,7},{7,6},{8,9},{9,8},{10,11... | collective-permute-start | bytes 405512 | tf_op jit(solution)/shard_map/ppermute | solution.py:358
  20.4 5.9 %copy-start = (bf16[512,2048]{1,0:T(8,128)(2,1)S(1)}, bf16[512,2048]{1,0:T(8,128)(2,1)}, u32[]{:S(2)}) copy-start(bf16[512,2048]{1,0:T(8,128)(2,1)} %w_out_ref.1) | copy-start | bytes 6291460
  21.8 4.2 %collective-permute-start.7 = (bf16[272,128]{1,0:T(8,128)(2,1)S(1)}, bf16[272,128]{1,0:T(8,128)(2,1)S(1)}, u32[]{:S(2)}, u32[]{:S(2)}) collective-permute-start(bf16[272,128]{1,0:T(8,128)(2,1)S(1)} %get-tuple-element.31), channel_id=1, source_target_pairs={{9,0},{13,1},{11,2},{15,3},{8,4},{12,5},{10,6},{14,7},{1,8},{5,9},... | collective-permute-start | bytes 208904 | tf_op jit(solution)/shard_map/ppermute | solution.py:352
  23.9 2.4 %collective-permute-start.8 = (bf16[272,128]{1,0:T(8,128)(2,1)S(1)}, bf16[272,128]{1,0:T(8,128)(2,1)S(1)}, u32[]{:S(2)}, u32[]{:S(2)}) collective-permute-start(bf16[272,128]{1,0:T(8,128)(2,1)S(1)} %get-tuple-element.32), channel_id=1, source_target_pairs={{1,0},{5,1},{3,2},{7,3},{0,4},{4,5},{2,6},{6,7},{9,8},{13,9},{11,1... | collective-permute-start | bytes 208904 | tf_op jit(solution)/shard_map/ppermute | solution.py:352
  26.3 11.8 %copy-start.1 = (bf16[128,2048]{1,0:T(8,128)(2,1)S(1)}, bf16[128,2048]{1,0:T(8,128)(2,1)}, u32[]{:S(2)}) copy-start(bf16[128,2048]{1,0:T(8,128)(2,1)} %refs_3_.1) | copy-start | bytes 1572868
  26.9 2.4 %collective-permute-start.9 = (bf16[64,2048]{1,0:T(8,128)(2,1)S(1)}, bf16[64,2048]{1,0:T(8,128)(2,1)S(1)}, u32[]{:S(2)}, u32[]{:S(2)}) collective-permute-start(bf16[64,2048]{1,0:T(8,128)(2,1)S(1)} %get-tuple-element.34), channel_id=1, source_target_pairs={{0,1},{1,0},{2,3},{3,2},{4,5},{5,4},{6,7},{7,6},{8,9},{9,8},{10,11... | collective-permute-start | bytes 786440 | tf_op jit(solution)/shard_map/ppermute | solution.py:358
  29.4 8.7 %collective-permute-start.10 = (bf16[64,2048]{1,0:T(8,128)(2,1)S(1)}, bf16[64,2048]{1,0:T(8,128)(2,1)S(1)}, u32[]{:S(2)}, u32[]{:S(2)}) collective-permute-start(bf16[64,2048]{1,0:T(8,128)(2,1)S(1)} %add_convert_fusion.1), channel_id=1, source_target_pairs={{0,2},{1,3},{2,0},{3,1},{4,6},{5,7},{6,4},{7,5},{8,10},{9,11},{10,... | collective-permute-start | bytes 786440 | tf_op jit(solution)/shard_map/ppermute | solution.py:358
  38.2 1.6 %collective-permute-start.11 = (bf16[64,2048]{1,0:T(8,128)(2,1)S(1)}, bf16[64,2048]{1,0:T(8,128)(2,1)S(1)}, u32[]{:S(2)}, u32[]{:S(2)}) collective-permute-start(bf16[64,2048]{1,0:T(8,128)(2,1)S(1)} %add_convert_fusion.half_ref), channel_id=1, source_target_pairs={{0,1},{1,0},{2,3},{3,2},{4,5},{5,4},{6,7},{7,6},{8,9},{9,8},{10,11... | collective-permute-start | bytes 786440 | tf_op jit(solution)/shard_map/ppermute | solution.py:358

commit v6 on v5

--- a/solution.py
+++ b/solution.py
@@ -15,11 +15,13 @@
 ROW_CUTS = 2
 
 ORDER = (1, 0)
+BACK = (0, 1)
 
 big = 1e30
-Q = 3
-SFX = 10
+Q = 0.001
+SFX = 0.001
 JOIN = 30
+JOIN1 = 0.001
 
 VMEM = pl.BlockSpec(memory_space=pltpu.VMEM)
 HBM = pl.BlockSpec(memory_space=pltpu.HBM)
@@ -193,12 +195,13 @@
 
 
 def first_kernel(rows, per, *refs):
-    asks, early, (state_ref, sum_ref) = refs[:2], refs[2], refs[3:]
+    asks, early, (state_ref, sum_ref) = refs[:2], refs[2:-2], refs[-2:]
     queries, group = questions(asks, rows, per)
     tokens = group.shape[1]
     step = 2 * HD * per + NOTE_ROWS
     found = [block_scores(asks[1], per * rows, queries, group)]
-    found += [block_scores(early, at, queries, group) for at in range(0, early.shape[0], step)]
+    for ref in early:
+        found += [block_scores(ref, at, queries, group) for at in range(0, ref.shape[0], step)]
     for i in range(per):
         carry = (
             jnp.full((1, tokens), -big, jnp.float32),
@@ -253,7 +256,7 @@
 
 def project_kernel(per, sum_ref, log_ref, w_out_ref, *refs):
     backs, (keep_ref, send_ref, attended, branch) = refs[:2], refs[2:]
-    for bits, back in zip(ORDER, backs):
+    for bits, back in zip(BACK, backs):
         logs = back[per * HD : per * HD + NOTE_ROWS, :].astype(jnp.float32)
         for i in range(per):
             at = head_at(bits, i, per)
@@ -294,7 +297,7 @@
     copy.wait()
 
 
-def call(kernel, outs, specs, scratch=(), out_specs=None, aliases=None, cost=1):
+def call(kernel, outs, specs, scratch=(), out_specs=None, aliases=None, cost=0.001):
     def run(*args):
         pinned = [
             pltpu.with_memory_space_constraint(x, pltpu.HBM) if spec is HBM else x
@@ -406,29 +409,34 @@
         ],
         cost=SFX,
     )(normed, query, segment, w_key, w_value)
-    joined = near
+    last = asks[1][per * rows :]
     if fars:
-        join = call(join_kernel, [((3 * step, HD), bf16)], (VMEM,) * 4, cost=JOIN)
-        joined = join(suffix_log, fars[0], near, fars[1])[0]
-
-    blocks = [joined, asks[1][per * rows :]]
+        join = call(join_kernel, [((2 * step, HD), bf16)], (VMEM,) * 3, cost=JOIN1)
+        first = join(suffix_log, fars[0], near)[0]
+        first_other = across_mp(first, 1)
+        wait = call(join_kernel, [((step, HD), bf16)], (VMEM,) * 2, cost=JOIN)
+        second = wait(first, fars[1])[0]
+        blocks = [first, first_other, second]
+        others = [across_mp(x, 1) for x in (second, last)]
+    else:
+        blocks = [near, across_mp(near, 1)]
+        others, bit = [across_mp(last, 1)], 4
+        while bit < n_blk:
+            others = others + [across(jnp.concatenate(blocks + [last] + others, axis=0), bit)]
+            bit *= 2
     state, summed = call(
         functools.partial(first_kernel, rows, per),
         [((8, heads * rows), f32), ((HD, heads * rows), f32)],
-        (VMEM,) * 3,
+        (VMEM,) * (2 + len(blocks)),
         cost=30,
-    )(*asks, joined)
-    others = [across_mp(x, 1) for x in blocks]
-    bit = 4
-    while bit < n_blk and not fars:
-        others = others + [across(jnp.concatenate(blocks + others, axis=0), bit)]
-        bit *= 2
+    )(*asks, *blocks)
     backs = call(
         functools.partial(second_kernel, rows, per),
         [((per * HD + NOTE_ROWS, rows), bf16)] * 2,
         (VMEM,) * (4 + len(others)),
     )(*asks, state, summed, *others)
-    backs = [exchange(x, k, back=True) for k, x in zip(ORDER, backs)]
+    backs = dict(zip(ORDER, backs))
+    backs = [exchange(backs[k], k, back=True) for k in BACK]
 
     keep, send = call(
         functools.partial(project_kernel, per),

time: 40.7 us -> 40.1 us (0.985)
    ppermute x7, starting transfers between devices: 9.6 us -> 9.12 us  [exchange(): return lax.ppermute(x, ('blk', 'mp'), pairs)]
    ppermute x5 -> x6, waiting for transfers between devices: 9.62 us -> 9.28 us  [across_mp(): return lax.ppermute(x, 'mp', [(i, i ^ bit) for i in range(n_mp)])]
    ppermute x5 -> x6, starting transfers between devices: 3.59 us -> 3.87 us  [across_mp(): return lax.ppermute(x, 'mp', [(i, i ^ bit) for i in range(n_mp)])]
    pallas_call x9 -> x10, Pallas kernels: 10.2 us -> 10.1 us  [run(): return inner(*pinned)]
  transfers between devices with their start and end apart: 12 -> 13, of which waited for: 7 -> 8; matrix products, arithmetic and copies ran while one was open for 0% -> 0% of each run, Pallas kernels for 17% -> 18%
where the time goes in v6:
time: 40.1 us; the launch traced here: 39.8 us
  waiting for transfers between devices  15.1 us (38%)
  starting transfers between devices  13 us (32%)
  Pallas kernels  10.1 us (25%)
  between operations  1.49 us (4%)
    pallas_call x10, Pallas kernels, run(): return inner(*pinned)  10.1 us
    ppermute x6, waiting for transfers between devices, across_mp(): return lax.ppermute(x, 'mp', [(i, i ^ bit) for i in range(n_mp)])  9.28 us
    ppermute x7, starting transfers between devices, exchange(): return lax.ppermute(x, ('blk', 'mp'), pairs)  9.12 us
    ppermute x7, waiting for transfers between devices, exchange(): return lax.ppermute(x, ('blk', 'mp'), pairs)  5.82 us
    ppermute x6, starting transfers between devices, across_mp(): return lax.ppermute(x, 'mp', [(i, i ^ bit) for i in range(n_mp)])  3.87 us
  transfers between devices with their start and end apart: 13, of which 8 were waited for; matrix products, arithmetic and copies ran while one was open for 0% of the time, Pallas kernels for 18%

profile of v6, /device:TPU:0, one launch (start us, length us, event | category | flops | bytes accessed | tf_op | source)
XLA Modules:
  0.0 39.8 jit_solution(48528647208195533)
XLA Ops:
  1.3 1.1 %shard_map.129 = (bf16[528,128]{1,0:T(8,128)(2,1)S(1)}, bf16[528,128]{1,0:T(8,128)(2,1)S(1)}, bf16[528,128]{1,0:T(8,128)(2,1)S(1)}) custom-call(bf16[1,128,512]{2,1,0:T(8,128)(2,1)} %keys_ref.1, bf16[1,128,512]{2,1,0:T(8,128)(2,1)} %values_ref.1, bf16[16,128]{1,0:T(8,128)(2,1)S(1)} %broadcast_in_dim.4.refs_2_.tag_ref), custom_call_target="tpu_custom_call" | custom-call | flops 1000000 | bytes 1 | tf_op jit(solution)/shard_map/pallas_call | solution.py:306
  2.4 3.5 %collective-permute-start.2 = (bf16[528,128]{1,0:T(8,128)(2,1)S(1)}, bf16[528,128]{1,0:T(8,128)(2,1)S(1)}, u32[]{:S(2)}, u32[]{:S(2)}) collective-permute-start(bf16[528,128]{1,0:T(8,128)(2,1)S(1)} %get-tuple-element.26), channel_id=1, source_target_pairs={{0,17},{1,21},{2,19},{3,23},{4,16},{5,20},{6,18},{7,22},{8,25},{9,... | collective-permute-start | bytes 405512 | tf_op jit(solution)/shard_map/ppermute | solution.py:355
  5.9 2.2 %collective-permute-start.3 = (bf16[528,128]{1,0:T(8,128)(2,1)S(1)}, bf16[528,128]{1,0:T(8,128)(2,1)S(1)}, u32[]{:S(2)}, u32[]{:S(2)}) collective-permute-start(bf16[528,128]{1,0:T(8,128)(2,1)S(1)} %get-tuple-element.27), channel_id=1, source_target_pairs={{0,9},{1,13},{2,11},{3,15},{4,8},{5,12},{6,10},{7,14},{8,1},{9,5},... | collective-permute-start | bytes 405512 | tf_op jit(solution)/shard_map/ppermute | solution.py:355
  8.2 0.5 %collective-permute-start.5 = (bf16[528,128]{1,0:T(8,128)(2,1)S(1)}, bf16[528,128]{1,0:T(8,128)(2,1)S(1)}, u32[]{:S(2)}, u32[]{:S(2)}) collective-permute-start(bf16[528,128]{1,0:T(8,128)(2,1)S(1)} %get-tuple-element.28), channel_id=1, source_target_pairs={{0,25},{1,29},{2,27},{3,31},{4,24},{5,28},{6,26},{7,30},{8,17},{9,... | collective-permute-start | bytes 405512 | tf_op jit(solution)/shard_map/ppermute | solution.py:355
  8.7 2.3 %shard_map.127 = (bf16[128,2048]{1,0:T(8,128)(2,1)S(1)}, bf16[128,512]{1,0:T(8,128)(2,1)S(1)}, bf16[784,128]{1,0:T(8,128)(2,1)S(1)}, bf16[272,128]{1,0:T(8,128)(2,1)S(1)}) custom-call(bf16[1,128,512]{2,1,0:T(8,128)(2,1)} %keys_ref.1, bf16[1,128,512]{2,1,0:T(8,128)(2,1)} %values_ref.1, bf16[16,128]{1,0:T(8,128)(2,1)S(1)} %broadcast_in_dim.4.refs_2_.tag_ref, ...), custom_call_target="tpu_custom_call" | custom-call | flops 1000000 | bytes 1 | tf_op jit(solution)/shard_map/pallas_call | solution.py:306
  11.0 0.7 %collective-permute-start = (bf16[272,128]{1,0:T(8,128)(2,1)S(1)}, bf16[272,128]{1,0:T(8,128)(2,1)S(1)}, u32[]{:S(2)}, u32[]{:S(2)}) collective-permute-start(bf16[272,128]{1,0:T(8,128)(2,1)S(1)} %get-tuple-element.24), channel_id=1, source_target_pairs={{0,9},{1,13},{2,11},{3,15},{4,8},{5,12},{6,10},{7,14},{8,1},{9,5},... | collective-permute-start | bytes 208904 | tf_op jit(solution)/shard_map/ppermute | solution.py:355
  11.7 0.1 collective-permute-start.1
  11.8 3.2 %shard_map.128 = (f32[512,128]{1,0:T(8,128)S(1)}, f32[8,128]{1,0:T(8,128)S(1)}) custom-call(bf16[128,2048]{1,0:T(8,128)(2,1)S(1)} %get-tuple-element.20.normed_ref, bf16[128,512]{1,0:T(8,128)(2,1)S(1)} %get-tuple-element.21.query_ref, s32[1,128]{1,0:T(1,128)} %refs_0_.3, bf16[2048,512]{1,0:T(8,128)(2,1)} %refs_1_.3, bf16[2048,512]{1,0:T(8,128)(2,1)} %refs_2_.1), custom_call_target="tpu_custom_call" | custom-call | flops 1000000 | bytes 1 | tf_op jit(solution)/shard_map/pallas_call | solution.py:306
  15.1 0.0 collective-permute-done.2.refs_0_
  15.1 0.2 collective-permute-done.3.refs_1_
  15.3 0.8 %collective-permute-start.4 = (bf16[1056,128]{1,0:T(8,128)(2,1)S(1)}, bf16[1056,128]{1,0:T(8,128)(2,1)S(1)}, u32[]{:S(2)}, u32[]{:S(2)}) collective-permute-start(bf16[1056,128]{1,0:T(8,128)(2,1)S(1)} %shard_map.130._.refs_2_), channel_id=1, source_target_pairs={{0,1},{1,0},{2,3},{3,2},{4,5},{5,4},{6,7},{7,6},{8,9},{9,8},{10,11... | collective-permute-start | bytes 811016 | tf_op jit(solution)/shard_map/ppermute | solution.py:361
  16.1 2.9 %collective-permute-done.5.refs_0_ = bf16[528,128]{1,0:T(8,128)(2,1)S(1)} collective-permute-done((bf16[528,128]{1,0:T(8,128)(2,1)S(1)}, bf16[528,128]{1,0:T(8,128)(2,1)S(1)}, u32[]{:S(2)}, u32[]{:S(2)}) %collective-permute-start.5) | collective-permute-done | bytes 135200 | tf_op jit(solution)/shard_map/ppermute | solution.py:355
  19.0 0.1 collective-permute-start.6
  19.1 0.5 %collective-permute-done.1.refs_1_ = bf16[784,128]{1,0:T(8,128)(2,1)S(1)} collective-permute-done((bf16[784,128]{1,0:T(8,128)(2,1)S(1)}, bf16[784,128]{1,0:T(8,128)(2,1)S(1)}, u32[]{:S(2)}, u32[]{:S(2)}) %collective-permute-start.1) | collective-permute-done | bytes 200736 | tf_op jit(solution)/shard_map/ppermute | solution.py:355
  19.6 0.1 collective-permute-start.7
  19.7 0.0 collective-permute-done.refs_0_
  19.7 0.0 collective-permute-done.4.refs_3_
  19.7 0.0 copy-start
  19.7 0.8 %shard_map.132 = (f32[8,512]{1,0:T(8,128)S(1)}, f32[128,512]{1,0:T(8,128)S(1)}) custom-call(bf16[272,128]{1,0:T(8,128)(2,1)S(1)} %collective-permute-done.refs_0_, bf16[784,128]{1,0:T(8,128)(2,1)S(1)} %collective-permute-done.1.refs_1_, bf16[1056,128]{1,0:T(8,128)(2,1)S(1)} %shard_map.130._.refs_2_, bf16[1056,128]{1,0:T(8,128)(2,1)S(1)} %collective-permute-done.4.refs_3_, ...), custom_call_target="tpu_custom_call" | custom-call | flops 30000001024 | bytes 1 | tf_op jit(solution)/shard_map/pallas_call | solution.py:306
  20.6 0.0 collective-permute-done.6.refs_4_
  20.6 0.5 %collective-permute-done.7.refs_5_ = bf16[528,128]{1,0:T(8,128)(2,1)S(1)} collective-permute-done((bf16[528,128]{1,0:T(8,128)(2,1)S(1)}, bf16[528,128]{1,0:T(8,128)(2,1)S(1)}, u32[]{:S(2)}, u32[]{:S(2)}) %collective-permute-start.7) | collective-permute-done | bytes 135200 | tf_op jit(solution)/shard_map/ppermute | solution.py:361
  21.0 0.0 copy-start.1
  21.0 0.5 %shard_map.133 = (bf16[272,128]{1,0:T(8,128)(2,1)S(1)}, bf16[272,128]{1,0:T(8,128)(2,1)S(1)}) custom-call(bf16[272,128]{1,0:T(8,128)(2,1)S(1)} %collective-permute-done.refs_0_, bf16[784,128]{1,0:T(8,128)(2,1)S(1)} %collective-permute-done.1.refs_1_, f32[8,512]{1,0:T(8,128)S(1)} %get-tuple-element.29.refs_2_, f32[128,512]{1,0:T(8,128)S(1)} %get-tuple-element.30.refs_3_, ...), custom_call_target="tpu_custom_call" | custom-call | flops 1000000 | bytes 1 | tf_op jit(solution)/shard_map/pallas_call | solution.py:306
  21.6 0.0 collective-permute-start.8
  21.6 2.0 %collective-permute-start.9 = (bf16[272,128]{1,0:T(8,128)(2,1)S(1)}, bf16[272,128]{1,0:T(8,128)(2,1)S(1)}, u32[]{:S(2)}, u32[]{:S(2)}) collective-permute-start(bf16[272,128]{1,0:T(8,128)(2,1)S(1)} %get-tuple-element.32), channel_id=1, source_target_pairs={{9,0},{13,1},{11,2},{15,3},{8,4},{12,5},{10,6},{14,7},{1,8},{5,9},... | collective-permute-start | bytes 208904 | tf_op jit(solution)/shard_map/ppermute | solution.py:355
  23.6 0.0 collective-permute-done.8.refs_0_
  23.6 2.2 %collective-permute-done.9.refs_1_ = bf16[272,128]{1,0:T(8,128)(2,1)S(1)} collective-permute-done((bf16[272,128]{1,0:T(8,128)(2,1)S(1)}, bf16[272,128]{1,0:T(8,128)(2,1)S(1)}, u32[]{:S(2)}, u32[]{:S(2)}) %collective-permute-start.9) | collective-permute-done | bytes 69664 | tf_op jit(solution)/shard_map/ppermute | solution.py:355
  25.8 0.0 copy-done
  25.8 0.7 %shard_map.134 = (f32[64,2048]{1,0:T(8,128)S(1)}, bf16[64,2048]{1,0:T(8,128)(2,1)S(1)}) custom-call(f32[512,128]{1,0:T(8,128)S(1)} %get-tuple-element.22.sum_ref, f32[8,128]{1,0:T(8,128)S(1)} %get-tuple-element.23._.log_ref, bf16[512,2048]{1,0:T(8,128)(2,1)S(1)} %copy-done, bf16[272,128]{1,0:T(8,128)(2,1)S(1)} %collective-permute-done.8.refs_0_, ...), custom_call_target="tpu_custom_call" | custom-call | flops 1000000 | bytes 1 | tf_op jit(solution)/shard_map/pallas_call | solution.py:306
  26.5 1.1 %collective-permute-start.10 = (bf16[64,2048]{1,0:T(8,128)(2,1)S(1)}, bf16[64,2048]{1,0:T(8,128)(2,1)S(1)}, u32[]{:S(2)}, u32[]{:S(2)}) collective-permute-start(bf16[64,2048]{1,0:T(8,128)(2,1)S(1)} %get-tuple-element.34), channel_id=1, source_target_pairs={{0,1},{1,0},{2,3},{3,2},{4,5},{5,4},{6,7},{7,6},{8,9},{9,8},{10,11... | collective-permute-start | bytes 786440 | tf_op jit(solution)/shard_map/ppermute | solution.py:361
  27.6 1.2 %collective-permute-done.10 = bf16[64,2048]{1,0:T(8,128)(2,1)S(1)} collective-permute-done((bf16[64,2048]{1,0:T(8,128)(2,1)S(1)}, bf16[64,2048]{1,0:T(8,128)(2,1)S(1)}, u32[]{:S(2)}, u32[]{:S(2)}) %collective-permute-start.10) | collective-permute-done | bytes 262176 | tf_op jit(solution)/shard_map/ppermute | solution.py:361
  28.8 1.8 %collective-permute-start.11 = (bf16[64,2048]{1,0:T(8,128)(2,1)S(1)}, bf16[64,2048]{1,0:T(8,128)(2,1)S(1)}, u32[]{:S(2)}, u32[]{:S(2)}) collective-permute-start(bf16[64,2048]{1,0:T(8,128)(2,1)S(1)} %add_convert_fusion.1), channel_id=1, source_target_pairs={{0,2},{1,3},{2,0},{3,1},{4,6},{5,7},{6,4},{7,5},{8,10},{9,11},{10,... | collective-permute-start | bytes 786440 | tf_op jit(solution)/shard_map/ppermute | solution.py:361
  30.6 6.9 %collective-permute-done.11 = bf16[64,2048]{1,0:T(8,128)(2,1)S(1)} collective-permute-done((bf16[64,2048]{1,0:T(8,128)(2,1)S(1)}, bf16[64,2048]{1,0:T(8,128)(2,1)S(1)}, u32[]{:S(2)}, u32[]{:S(2)}) %collective-permute-start.11) | collective-permute-done | bytes 262176 | tf_op jit(solution)/shard_map/ppermute | solution.py:361
  37.4 0.0 copy-done.1
  37.4 0.1 add_convert_fusion.half_ref
  37.5 0.1 collective-permute-start.12
  37.6 0.7 %shard_map.135._ = bf16[128,2048]{1,0:T(8,128)(2,1)} custom-call(bf16[64,2048]{1,0:T(8,128)(2,1)S(1)} %add_convert_fusion.half_ref), custom_call_target="tpu_custom_call" | custom-call | flops 1000000 | bytes 1 | tf_op jit(solution)/shard_map/pallas_call | solution.py:306
  38.3 0.8 %collective-permute-done.12.half_ref = bf16[64,2048]{1,0:T(8,128)(2,1)S(1)} collective-permute-done((bf16[64,2048]{1,0:T(8,128)(2,1)S(1)}, bf16[64,2048]{1,0:T(8,128)(2,1)S(1)}, u32[]{:S(2)}, u32[]{:S(2)}) %collective-permute-start.12) | collective-permute-done | bytes 262176 | tf_op jit(solution)/shard_map/ppermute | solution.py:361
  39.1 0.7 %shard_map.136 = bf16[128,2048]{1,0:T(8,128)(2,1)} custom-call(bf16[64,2048]{1,0:T(8,128)(2,1)S(1)} %collective-permute-done.12.half_ref, bf16[128,2048]{1,0:T(8,128)(2,1)} %shard_map.135._), custom_call_target="tpu_custom_call", output_to_operand_aliasing={{}: (1, {})} | custom-call | flops 1000000 | bytes 1 | tf_op jit(solution)/shard_map/pallas_call | solution.py:306
  (5 shorter events, 0.1 us)
Async XLA Ops:
  2.4 12.7 %collective-permute-start.2 = (bf16[528,128]{1,0:T(8,128)(2,1)S(1)}, bf16[528,128]{1,0:T(8,128)(2,1)S(1)}, u32[]{:S(2)}, u32[]{:S(2)}) collective-permute-start(bf16[528,128]{1,0:T(8,128)(2,1)S(1)} %get-tuple-element.26), channel_id=1, source_target_pairs={{0,17},{1,21},{2,19},{3,23},{4,16},{5,20},{6,18},{7,22},{8,25},{9,... | collective-permute-start | bytes 405512 | tf_op jit(solution)/shard_map/ppermute | solution.py:355
  5.9 9.3 %collective-permute-start.3 = (bf16[528,128]{1,0:T(8,128)(2,1)S(1)}, bf16[528,128]{1,0:T(8,128)(2,1)S(1)}, u32[]{:S(2)}, u32[]{:S(2)}) collective-permute-start(bf16[528,128]{1,0:T(8,128)(2,1)S(1)} %get-tuple-element.27), channel_id=1, source_target_pairs={{0,9},{1,13},{2,11},{3,15},{4,8},{5,12},{6,10},{7,14},{8,1},{9,5},... | collective-permute-start | bytes 405512 | tf_op jit(solution)/shard_map/ppermute | solution.py:355
  8.2 10.8 %collective-permute-start.5 = (bf16[528,128]{1,0:T(8,128)(2,1)S(1)}, bf16[528,128]{1,0:T(8,128)(2,1)S(1)}, u32[]{:S(2)}, u32[]{:S(2)}) collective-permute-start(bf16[528,128]{1,0:T(8,128)(2,1)S(1)} %get-tuple-element.28), channel_id=1, source_target_pairs={{0,25},{1,29},{2,27},{3,31},{4,24},{5,28},{6,26},{7,30},{8,17},{9,... | collective-permute-start | bytes 405512 | tf_op jit(solution)/shard_map/ppermute | solution.py:355
  11.0 8.7 %collective-permute-start = (bf16[272,128]{1,0:T(8,128)(2,1)S(1)}, bf16[272,128]{1,0:T(8,128)(2,1)S(1)}, u32[]{:S(2)}, u32[]{:S(2)}) collective-permute-start(bf16[272,128]{1,0:T(8,128)(2,1)S(1)} %get-tuple-element.24), channel_id=1, source_target_pairs={{0,9},{1,13},{2,11},{3,15},{4,8},{5,12},{6,10},{7,14},{8,1},{9,5},... | collective-permute-start | bytes 208904 | tf_op jit(solution)/shard_map/ppermute | solution.py:355
  11.7 7.9 %collective-permute-start.1 = (bf16[784,128]{1,0:T(8,128)(2,1)S(1)}, bf16[784,128]{1,0:T(8,128)(2,1)S(1)}, u32[]{:S(2)}, u32[]{:S(2)}) collective-permute-start(bf16[784,128]{1,0:T(8,128)(2,1)S(1)} %get-tuple-element.25), channel_id=1, source_target_pairs={{0,1},{1,5},{2,3},{3,7},{4,0},{5,4},{6,2},{7,6},{8,9},{9,13},{10,1... | collective-permute-start | bytes 602120 | tf_op jit(solution)/shard_map/ppermute | solution.py:355
  15.3 4.4 %collective-permute-start.4 = (bf16[1056,128]{1,0:T(8,128)(2,1)S(1)}, bf16[1056,128]{1,0:T(8,128)(2,1)S(1)}, u32[]{:S(2)}, u32[]{:S(2)}) collective-permute-start(bf16[1056,128]{1,0:T(8,128)(2,1)S(1)} %shard_map.130._.refs_2_), channel_id=1, source_target_pairs={{0,1},{1,0},{2,3},{3,2},{4,5},{5,4},{6,7},{7,6},{8,9},{9,8},{10,11... | collective-permute-start | bytes 811016 | tf_op jit(solution)/shard_map/ppermute | solution.py:361
  19.0 1.5 %collective-permute-start.6 = (bf16[528,128]{1,0:T(8,128)(2,1)S(1)}, bf16[528,128]{1,0:T(8,128)(2,1)S(1)}, u32[]{:S(2)}, u32[]{:S(2)}) collective-permute-start(bf16[528,128]{1,0:T(8,128)(2,1)S(1)} %shard_map.131.refs_4_), channel_id=1, source_target_pairs={{0,1},{1,0},{2,3},{3,2},{4,5},{5,4},{6,7},{7,6},{8,9},{9,8},{10,11... | collective-permute-start | bytes 405512 | tf_op jit(solution)/shard_map/ppermute | solution.py:361
  19.6 1.4 %collective-permute-start.7 = (bf16[528,128]{1,0:T(8,128)(2,1)S(1)}, bf16[528,128]{1,0:T(8,128)(2,1)S(1)}, u32[]{:S(2)}, u32[]{:S(2)}) collective-permute-start(bf16[528,128]{1,0:T(8,128)(2,1)S(1)} %slice.4), channel_id=1, source_target_pairs={{0,1},{1,0},{2,3},{3,2},{4,5},{5,4},{6,7},{7,6},{8,9},{9,8},{10,11... | collective-permute-start | bytes 405512 | tf_op jit(solution)/shard_map/ppermute | solution.py:361
  19.7 6.1 %copy-start = (bf16[512,2048]{1,0:T(8,128)(2,1)S(1)}, bf16[512,2048]{1,0:T(8,128)(2,1)}, u32[]{:S(2)}) copy-start(bf16[512,2048]{1,0:T(8,128)(2,1)} %w_out_ref.1) | copy-start | bytes 6291460
  21.0 16.4 %copy-start.1 = (bf16[128,2048]{1,0:T(8,128)(2,1)S(1)}, bf16[128,2048]{1,0:T(8,128)(2,1)}, u32[]{:S(2)}) copy-start(bf16[128,2048]{1,0:T(8,128)(2,1)} %refs_3_.1) | copy-start | bytes 1572868
  21.6 2.0 %collective-permute-start.8 = (bf16[272,128]{1,0:T(8,128)(2,1)S(1)}, bf16[272,128]{1,0:T(8,128)(2,1)S(1)}, u32[]{:S(2)}, u32[]{:S(2)}) collective-permute-start(bf16[272,128]{1,0:T(8,128)(2,1)S(1)} %get-tuple-element.31), channel_id=1, source_target_pairs={{1,0},{5,1},{3,2},{7,3},{0,4},{4,5},{2,6},{6,7},{9,8},{13,9},{11,1... | collective-permute-start | bytes 208904 | tf_op jit(solution)/shard_map/ppermute | solution.py:355
  21.6 4.2 %collective-permute-start.9 = (bf16[272,128]{1,0:T(8,128)(2,1)S(1)}, bf16[272,128]{1,0:T(8,128)(2,1)S(1)}, u32[]{:S(2)}, u32[]{:S(2)}) collective-permute-start(bf16[272,128]{1,0:T(8,128)(2,1)S(1)} %get-tuple-element.32), channel_id=1, source_target_pairs={{9,0},{13,1},{11,2},{15,3},{8,4},{12,5},{10,6},{14,7},{1,8},{5,9},... | collective-permute-start | bytes 208904 | tf_op jit(solution)/shard_map/ppermute | solution.py:355
  26.5 2.2 %collective-permute-start.10 = (bf16[64,2048]{1,0:T(8,128)(2,1)S(1)}, bf16[64,2048]{1,0:T(8,128)(2,1)S(1)}, u32[]{:S(2)}, u32[]{:S(2)}) collective-permute-start(bf16[64,2048]{1,0:T(8,128)(2,1)S(1)} %get-tuple-element.34), channel_id=1, source_target_pairs={{0,1},{1,0},{2,3},{3,2},{4,5},{5,4},{6,7},{7,6},{8,9},{9,8},{10,11... | collective-permute-start | bytes 786440 | tf_op jit(solution)/shard_map/ppermute | solution.py:361
  28.8 8.7 %collective-permute-start.11 = (bf16[64,2048]{1,0:T(8,128)(2,1)S(1)}, bf16[64,2048]{1,0:T(8,128)(2,1)S(1)}, u32[]{:S(2)}, u32[]{:S(2)}) collective-permute-start(bf16[64,2048]{1,0:T(8,128)(2,1)S(1)} %add_convert_fusion.1), channel_id=1, source_target_pairs={{0,2},{1,3},{2,0},{3,1},{4,6},{5,7},{6,4},{7,5},{8,10},{9,11},{10,... | collective-permute-start | bytes 786440 | tf_op jit(solution)/shard_map/ppermute | solution.py:361
  37.5 1.6 %collective-permute-start.12 = (bf16[64,2048]{1,0:T(8,128)(2,1)S(1)}, bf16[64,2048]{1,0:T(8,128)(2,1)S(1)}, u32[]{:S(2)}, u32[]{:S(2)}) collective-permute-start(bf16[64,2048]{1,0:T(8,128)(2,1)S(1)} %add_convert_fusion.half_ref), channel_id=1, source_target_pairs={{0,1},{1,0},{2,3},{3,2},{4,5},{5,4},{6,7},{7,6},{8,9},{9,8},{10,11... | collective-permute-start | bytes 786440 | tf_op jit(solution)/shard_map/ppermute | solution.py:361

commit v7 on v6

--- a/solution.py
+++ b/solution.py
@@ -71,6 +71,16 @@
     out = refs[-1]
     for i, ref in enumerate(refs[:-1]):
         out[i * ref.shape[0] : (i + 1) * ref.shape[0], :] = ref[...]
+
+
+def gate_kernel(*refs):
+    refs[-1][...] = jnp.zeros_like(refs[-1])
+
+
+def last_join_kernel(_, far_ref, ask_ref, out):
+    step = far_ref.shape[0]
+    out[0:step, :] = far_ref[...]
+    out[step : 2 * step, :] = ask_ref[ask_ref.shape[0] - step :, :]
 
 
 def query_kernel(per, *refs):
@@ -195,11 +205,11 @@
 
 
 def first_kernel(rows, per, *refs):
-    asks, early, (state_ref, sum_ref) = refs[:2], refs[2:-2], refs[-2:]
+    asks, early, (state_ref, sum_ref) = refs[1::-1], refs[2:-2], refs[-2:]
     queries, group = questions(asks, rows, per)
     tokens = group.shape[1]
     step = 2 * HD * per + NOTE_ROWS
-    found = [block_scores(asks[1], per * rows, queries, group)]
+    found = [] if early[2:] else [block_scores(asks[1], per * rows, queries, group)]
     for ref in early:
         found += [block_scores(ref, at, queries, group) for at in range(0, ref.shape[0], step)]
     for i in range(per):
@@ -216,7 +226,7 @@
 
 
 def second_kernel(rows, per, *refs):
-    asks, (state_ref, sum_ref), blocks, outs = refs[:2], refs[2:4], refs[4:-2], refs[-2:]
+    asks, (state_ref, sum_ref), blocks, outs = refs[1::-1], refs[2:4], refs[4:-2], refs[-2:]
     queries, group = questions(asks, rows, per)
     tokens = group.shape[1]
     step = 2 * HD * per + NOTE_ROWS
@@ -349,8 +359,8 @@
             square, pair, lane = i // 4, i // 2 % 2, i % 2
             for m in range(n_mp):
                 other, core = m // 2, m % 2
-                blk = (square ^ far) * 4 + (pair ^ bits) * 2 + core
-                link = (i * n_mp + m, blk * n_mp + other * 2 + 1 - lane)
+                blk = (square ^ far) * 4 + (pair ^ bits) * 2 + 1 - core
+                link = (i * n_mp + m, blk * n_mp + other * 2 + lane)
                 pairs.append(link[::-1] if back else link)
         return lax.ppermute(x, ("blk", "mp"), pairs)
 
@@ -396,7 +406,8 @@
         segment,
         request_group,
     )
-    asks = [exchange(packs[k], k) for k in ORDER]
+    asks = {k: exchange(packs[k], k) for k in ORDER[::-1]}
+    asks = [asks[k] for k in ORDER]
     suffix_sum, suffix_log = call(
         functools.partial(suffix_kernel, heads),
         [((local_width, rows), f32), ((max(heads, 8), rows), f32)],
@@ -414,10 +425,11 @@
         join = call(join_kernel, [((2 * step, HD), bf16)], (VMEM,) * 3, cost=JOIN1)
         first = join(suffix_log, fars[0], near)[0]
         first_other = across_mp(first, 1)
-        wait = call(join_kernel, [((step, HD), bf16)], (VMEM,) * 2, cost=JOIN)
-        second = wait(first, fars[1])[0]
+        wait = call(gate_kernel, [((8, HD), f32)], (VMEM,) * 2, cost=JOIN)
+        gate = wait(first, fars[1])[0]
+        second = call(last_join_kernel, [((2 * step, HD), bf16)], (VMEM,) * 3)(gate, fars[1], asks[1])[0]
         blocks = [first, first_other, second]
-        others = [across_mp(x, 1) for x in (second, last)]
+        others = [across_mp(second, 1)]
     else:
         blocks = [near, across_mp(near, 1)]
         others, bit = [across_mp(last, 1)], 4
@@ -429,12 +441,12 @@
         [((8, heads * rows), f32), ((HD, heads * rows), f32)],
         (VMEM,) * (2 + len(blocks)),
         cost=30,
-    )(*asks, *blocks)
+    )(*asks[::-1], *blocks)
     backs = call(
         functools.partial(second_kernel, rows, per),
         [((per * HD + NOTE_ROWS, rows), bf16)] * 2,
         (VMEM,) * (4 + len(others)),
-    )(*asks, state, summed, *others)
+    )(*asks[::-1], state, summed, *others)
     backs = dict(zip(ORDER, backs))
     backs = [exchange(backs[k], k, back=True) for k in BACK]
 

time: 40.1 us -> 39.9 us (level)
  waiting for transfers between devices: 15.1 us -> 12.5 us
  starting transfers between devices: 13 us -> 15.4 us
    ppermute x7, waiting for transfers between devices: 5.82 us -> 3.62 us  [exchange(): return lax.ppermute(x, ('blk', 'mp'), pairs)]
    ppermute x7, starting transfers between devices: 9.12 us -> 11 us  [exchange(): return lax.ppermute(x, ('blk', 'mp'), pairs)]
    ppermute x6 -> x5, starting transfers between devices: 3.87 us -> 4.4 us  [across_mp(): return lax.ppermute(x, 'mp', [(i, i ^ bit) for i in range(n_mp)])]
    ppermute x6 -> x5, waiting for transfers between devices: 9.28 us -> 8.93 us  [across_mp(): return lax.ppermute(x, 'mp', [(i, i ^ bit) for i in range(n_mp)])]
    pallas_call x10 -> x11, Pallas kernels: 10.1 us -> 10.1 us  [run(): return inner(*pinned)]
  transfers between devices with their start and end apart: 13 -> 12, of which waited for: 8 -> 6; matrix products, arithmetic and copies ran while one was open for 0% -> 0% of each run, Pallas kernels for 18% -> 18%
where the time goes in v7:
time: 39.9 us; the launch traced here: 39.7 us
  starting transfers between devices  15.4 us (39%)
  waiting for transfers between devices  12.5 us (31%)
  Pallas kernels  10.1 us (25%)
  between operations  1.5 us (4%)
    ppermute x7, starting transfers between devices, exchange(): return lax.ppermute(x, ('blk', 'mp'), pairs)  11 us
    pallas_call x11, Pallas kernels, run(): return inner(*pinned)  10.1 us
    ppermute x5, waiting for transfers between devices, across_mp(): return lax.ppermute(x, 'mp', [(i, i ^ bit) for i in range(n_mp)])  8.93 us
    ppermute x5, starting transfers between devices, across_mp(): return lax.ppermute(x, 'mp', [(i, i ^ bit) for i in range(n_mp)])  4.4 us
    ppermute x7, waiting for transfers between devices, exchange(): return lax.ppermute(x, ('blk', 'mp'), pairs)  3.62 us
  transfers between devices with their start and end apart: 12, of which 6 were waited for; matrix products, arithmetic and copies ran while one was open for 0% of the time, Pallas kernels for 18%

profile of v7, /device:TPU:0, one launch (start us, length us, event | category | flops | bytes accessed | tf_op | source)
XLA Modules:
  0.0 39.7 jit_solution(11253529263571968440)
XLA Ops:
  1.3 1.1 %shard_map.129 = (bf16[528,128]{1,0:T(8,128)(2,1)S(1)}, bf16[528,128]{1,0:T(8,128)(2,1)S(1)}, bf16[528,128]{1,0:T(8,128)(2,1)S(1)}) custom-call(bf16[1,128,512]{2,1,0:T(8,128)(2,1)} %keys_ref.1, bf16[1,128,512]{2,1,0:T(8,128)(2,1)} %values_ref.1, bf16[16,128]{1,0:T(8,128)(2,1)S(1)} %broadcast_in_dim.4.refs_2_.tag_ref), custom_call_target="tpu_custom_call" | custom-call | flops 1000000 | bytes 1 | tf_op jit(solution)/shard_map/pallas_call | solution.py:316
  2.4 5.0 %collective-permute-start.2 = (bf16[528,128]{1,0:T(8,128)(2,1)S(1)}, bf16[528,128]{1,0:T(8,128)(2,1)S(1)}, u32[]{:S(2)}, u32[]{:S(2)}) collective-permute-start(bf16[528,128]{1,0:T(8,128)(2,1)S(1)} %get-tuple-element.26), channel_id=1, source_target_pairs={{0,20},{1,16},{2,22},{3,18},{4,21},{5,17},{6,23},{7,19},{8,28},{9,... | collective-permute-start | bytes 405512 | tf_op jit(solution)/shard_map/ppermute | solution.py:365
  7.4 1.0 %collective-permute-start.3 = (bf16[528,128]{1,0:T(8,128)(2,1)S(1)}, bf16[528,128]{1,0:T(8,128)(2,1)S(1)}, u32[]{:S(2)}, u32[]{:S(2)}) collective-permute-start(bf16[528,128]{1,0:T(8,128)(2,1)S(1)} %get-tuple-element.27), channel_id=1, source_target_pairs={{0,12},{1,8},{2,14},{3,10},{4,13},{5,9},{6,15},{7,11},{8,4},{9,0},... | collective-permute-start | bytes 405512 | tf_op jit(solution)/shard_map/ppermute | solution.py:365
  8.5 0.1 collective-permute-start.5
  8.6 2.3 %shard_map.127 = (bf16[128,2048]{1,0:T(8,128)(2,1)S(1)}, bf16[128,512]{1,0:T(8,128)(2,1)S(1)}, bf16[784,128]{1,0:T(8,128)(2,1)S(1)}, bf16[272,128]{1,0:T(8,128)(2,1)S(1)}) custom-call(bf16[1,128,512]{2,1,0:T(8,128)(2,1)} %keys_ref.1, bf16[1,128,512]{2,1,0:T(8,128)(2,1)} %values_ref.1, bf16[16,128]{1,0:T(8,128)(2,1)S(1)} %broadcast_in_dim.4.refs_2_.tag_ref, ...), custom_call_target="tpu_custom_call" | custom-call | flops 1000000 | bytes 1 | tf_op jit(solution)/shard_map/pallas_call | solution.py:316
  10.9 0.1 collective-permute-start
  11.0 1.9 %collective-permute-start.1 = (bf16[272,128]{1,0:T(8,128)(2,1)S(1)}, bf16[272,128]{1,0:T(8,128)(2,1)S(1)}, u32[]{:S(2)}, u32[]{:S(2)}) collective-permute-start(bf16[272,128]{1,0:T(8,128)(2,1)S(1)} %get-tuple-element.25), channel_id=1, source_target_pairs={{0,12},{1,8},{2,14},{3,10},{4,13},{5,9},{6,15},{7,11},{8,4},{9,0},... | collective-permute-start | bytes 208904 | tf_op jit(solution)/shard_map/ppermute | solution.py:365
  13.0 3.2 %shard_map.128 = (f32[512,128]{1,0:T(8,128)S(1)}, f32[8,128]{1,0:T(8,128)S(1)}) custom-call(bf16[128,2048]{1,0:T(8,128)(2,1)S(1)} %get-tuple-element.20.normed_ref, bf16[128,512]{1,0:T(8,128)(2,1)S(1)} %get-tuple-element.21.query_ref, s32[1,128]{1,0:T(1,128)} %refs_0_.3, bf16[2048,512]{1,0:T(8,128)(2,1)} %refs_1_.3, bf16[2048,512]{1,0:T(8,128)(2,1)} %refs_2_.1), custom_call_target="tpu_custom_call" | custom-call | flops 1000000 | bytes 1 | tf_op jit(solution)/shard_map/pallas_call | solution.py:316
  16.2 0.0 collective-permute-done.2.refs_0_
  16.2 0.0 collective-permute-done.3.refs_1_
  16.3 0.1 collective-permute-start.4
  16.4 0.0 collective-permute-done.5.refs_1_.far_ref
  16.4 0.0 collective-permute-done.ask_ref.refs_0_
  16.4 2.2 %collective-permute-start.6 = (bf16[1056,128]{1,0:T(8,128)(2,1)S(1)}, bf16[1056,128]{1,0:T(8,128)(2,1)S(1)}, u32[]{:S(2)}, u32[]{:S(2)}) collective-permute-start(bf16[1056,128]{1,0:T(8,128)(2,1)S(1)} %shard_map.132.refs_4_), channel_id=1, source_target_pairs={{0,1},{1,0},{2,3},{3,2},{4,5},{5,4},{6,7},{7,6},{8,9},{9,8},{10,11... | collective-permute-start | bytes 811016 | tf_op jit(solution)/shard_map/ppermute | solution.py:371
  18.6 0.4 collective-permute-done.1.refs_1_
  19.0 0.0 collective-permute-done.4.refs_3_
  19.0 0.0 copy-start
  19.0 0.8 %shard_map.133 = (f32[8,512]{1,0:T(8,128)S(1)}, f32[128,512]{1,0:T(8,128)S(1)}) custom-call(bf16[784,128]{1,0:T(8,128)(2,1)S(1)} %collective-permute-done.ask_ref.refs_0_, bf16[272,128]{1,0:T(8,128)(2,1)S(1)} %collective-permute-done.1.refs_1_, bf16[1056,128]{1,0:T(8,128)(2,1)S(1)} %shard_map.130.refs_0_.refs_2_, ...), custom_call_target="tpu_custom_call" | custom-call | flops 30000001024 | bytes 1 | tf_op jit(solution)/shard_map/pallas_call | solution.py:316
  19.8 0.0 collective-permute-done.6.refs_4_
  19.8 0.0 copy-start.1
  19.8 0.5 %shard_map.134 = (bf16[272,128]{1,0:T(8,128)(2,1)S(1)}, bf16[272,128]{1,0:T(8,128)(2,1)S(1)}) custom-call(bf16[784,128]{1,0:T(8,128)(2,1)S(1)} %collective-permute-done.ask_ref.refs_0_, bf16[272,128]{1,0:T(8,128)(2,1)S(1)} %collective-permute-done.1.refs_1_, f32[8,512]{1,0:T(8,128)S(1)} %get-tuple-element.29.refs_2_, ...), custom_call_target="tpu_custom_call" | custom-call | flops 1000000 | bytes 1 | tf_op jit(solution)/shard_map/pallas_call | solution.py:316
  20.4 0.3 collective-permute-start.7
  20.7 2.4 %collective-permute-start.8 = (bf16[272,128]{1,0:T(8,128)(2,1)S(1)}, bf16[272,128]{1,0:T(8,128)(2,1)S(1)}, u32[]{:S(2)}, u32[]{:S(2)}) collective-permute-start(bf16[272,128]{1,0:T(8,128)(2,1)S(1)} %get-tuple-element.32), channel_id=1, source_target_pairs={{12,0},{8,1},{14,2},{10,3},{13,4},{9,5},{15,6},{11,7},{4,8},{0,9},... | collective-permute-start | bytes 208904 | tf_op jit(solution)/shard_map/ppermute | solution.py:365
  23.1 1.6 %collective-permute-done.7.refs_0_ = bf16[272,128]{1,0:T(8,128)(2,1)S(1)} collective-permute-done((bf16[272,128]{1,0:T(8,128)(2,1)S(1)}, bf16[272,128]{1,0:T(8,128)(2,1)S(1)}, u32[]{:S(2)}, u32[]{:S(2)}) %collective-permute-start.7) | collective-permute-done | bytes 69664 | tf_op jit(solution)/shard_map/ppermute | solution.py:365
  24.7 1.6 %collective-permute-done.8.refs_1_ = bf16[272,128]{1,0:T(8,128)(2,1)S(1)} collective-permute-done((bf16[272,128]{1,0:T(8,128)(2,1)S(1)}, bf16[272,128]{1,0:T(8,128)(2,1)S(1)}, u32[]{:S(2)}, u32[]{:S(2)}) %collective-permute-start.8) | collective-permute-done | bytes 69664 | tf_op jit(solution)/shard_map/ppermute | solution.py:365
  26.3 0.0 copy-done
  26.3 0.7 %shard_map.135 = (f32[64,2048]{1,0:T(8,128)S(1)}, bf16[64,2048]{1,0:T(8,128)(2,1)S(1)}) custom-call(f32[512,128]{1,0:T(8,128)S(1)} %get-tuple-element.22.sum_ref, f32[8,128]{1,0:T(8,128)S(1)} %get-tuple-element.23._.log_ref, bf16[512,2048]{1,0:T(8,128)(2,1)S(1)} %copy-done, bf16[272,128]{1,0:T(8,128)(2,1)S(1)} %collective-permute-done.7.refs_0_, ...), custom_call_target="tpu_custom_call" | custom-call | flops 1000000 | bytes 1 | tf_op jit(solution)/shard_map/pallas_call | solution.py:316
  27.0 0.1 collective-permute-start.9
  27.1 1.5 %collective-permute-done.9 = bf16[64,2048]{1,0:T(8,128)(2,1)S(1)} collective-permute-done((bf16[64,2048]{1,0:T(8,128)(2,1)S(1)}, bf16[64,2048]{1,0:T(8,128)(2,1)S(1)}, u32[]{:S(2)}, u32[]{:S(2)}) %collective-permute-start.9) | collective-permute-done | bytes 262176 | tf_op jit(solution)/shard_map/ppermute | solution.py:371
  28.7 2.0 %collective-permute-start.10 = (bf16[64,2048]{1,0:T(8,128)(2,1)S(1)}, bf16[64,2048]{1,0:T(8,128)(2,1)S(1)}, u32[]{:S(2)}, u32[]{:S(2)}) collective-permute-start(bf16[64,2048]{1,0:T(8,128)(2,1)S(1)} %add_convert_fusion.1), channel_id=1, source_target_pairs={{0,2},{1,3},{2,0},{3,1},{4,6},{5,7},{6,4},{7,5},{8,10},{9,11},{10,... | collective-permute-start | bytes 786440 | tf_op jit(solution)/shard_map/ppermute | solution.py:371
  30.7 6.6 %collective-permute-done.10 = bf16[64,2048]{1,0:T(8,128)(2,1)S(1)} collective-permute-done((bf16[64,2048]{1,0:T(8,128)(2,1)S(1)}, bf16[64,2048]{1,0:T(8,128)(2,1)S(1)}, u32[]{:S(2)}, u32[]{:S(2)}) %collective-permute-start.10) | collective-permute-done | bytes 262176 | tf_op jit(solution)/shard_map/ppermute | solution.py:371
  37.3 0.0 copy-done.1
  37.3 0.1 add_convert_fusion.half_ref
  37.4 0.1 collective-permute-start.11
  37.5 0.7 %shard_map.136._ = bf16[128,2048]{1,0:T(8,128)(2,1)} custom-call(bf16[64,2048]{1,0:T(8,128)(2,1)S(1)} %add_convert_fusion.half_ref), custom_call_target="tpu_custom_call" | custom-call | flops 1000000 | bytes 1 | tf_op jit(solution)/shard_map/pallas_call | solution.py:316
  38.2 0.8 %collective-permute-done.11.half_ref = bf16[64,2048]{1,0:T(8,128)(2,1)S(1)} collective-permute-done((bf16[64,2048]{1,0:T(8,128)(2,1)S(1)}, bf16[64,2048]{1,0:T(8,128)(2,1)S(1)}, u32[]{:S(2)}, u32[]{:S(2)}) %collective-permute-start.11) | collective-permute-done | bytes 262176 | tf_op jit(solution)/shard_map/ppermute | solution.py:371
  39.0 0.7 %shard_map.137 = bf16[128,2048]{1,0:T(8,128)(2,1)} custom-call(bf16[64,2048]{1,0:T(8,128)(2,1)S(1)} %collective-permute-done.11.half_ref, bf16[128,2048]{1,0:T(8,128)(2,1)} %shard_map.136._), custom_call_target="tpu_custom_call", output_to_operand_aliasing={{}: (1, {})} | custom-call | flops 1000000 | bytes 1 | tf_op jit(solution)/shard_map/pallas_call | solution.py:316
  (5 shorter events, 0.1 us)
Async XLA Ops:
  2.4 13.8 %collective-permute-start.2 = (bf16[528,128]{1,0:T(8,128)(2,1)S(1)}, bf16[528,128]{1,0:T(8,128)(2,1)S(1)}, u32[]{:S(2)}, u32[]{:S(2)}) collective-permute-start(bf16[528,128]{1,0:T(8,128)(2,1)S(1)} %get-tuple-element.26), channel_id=1, source_target_pairs={{0,20},{1,16},{2,22},{3,18},{4,21},{5,17},{6,23},{7,19},{8,28},{9,... | collective-permute-start | bytes 405512 | tf_op jit(solution)/shard_map/ppermute | solution.py:365
  7.4 8.8 %collective-permute-start.3 = (bf16[528,128]{1,0:T(8,128)(2,1)S(1)}, bf16[528,128]{1,0:T(8,128)(2,1)S(1)}, u32[]{:S(2)}, u32[]{:S(2)}) collective-permute-start(bf16[528,128]{1,0:T(8,128)(2,1)S(1)} %get-tuple-element.27), channel_id=1, source_target_pairs={{0,12},{1,8},{2,14},{3,10},{4,13},{5,9},{6,15},{7,11},{8,4},{9,0},... | collective-permute-start | bytes 405512 | tf_op jit(solution)/shard_map/ppermute | solution.py:365
  8.5 7.9 %collective-permute-start.5 = (bf16[528,128]{1,0:T(8,128)(2,1)S(1)}, bf16[528,128]{1,0:T(8,128)(2,1)S(1)}, u32[]{:S(2)}, u32[]{:S(2)}) collective-permute-start(bf16[528,128]{1,0:T(8,128)(2,1)S(1)} %get-tuple-element.28), channel_id=1, source_target_pairs={{0,28},{1,24},{2,30},{3,26},{4,29},{5,25},{6,31},{7,27},{8,20},{9,... | collective-permute-start | bytes 405512 | tf_op jit(solution)/shard_map/ppermute | solution.py:365
  10.9 5.5 %collective-permute-start = (bf16[784,128]{1,0:T(8,128)(2,1)S(1)}, bf16[784,128]{1,0:T(8,128)(2,1)S(1)}, u32[]{:S(2)}, u32[]{:S(2)}) collective-permute-start(bf16[784,128]{1,0:T(8,128)(2,1)S(1)} %get-tuple-element.24), channel_id=1, source_target_pairs={{0,4},{1,0},{2,6},{3,2},{4,5},{5,1},{6,7},{7,3},{8,12},{9,8},{10,1... | collective-permute-start | bytes 602120 | tf_op jit(solution)/shard_map/ppermute | solution.py:365
  11.0 7.9 %collective-permute-start.1 = (bf16[272,128]{1,0:T(8,128)(2,1)S(1)}, bf16[272,128]{1,0:T(8,128)(2,1)S(1)}, u32[]{:S(2)}, u32[]{:S(2)}) collective-permute-start(bf16[272,128]{1,0:T(8,128)(2,1)S(1)} %get-tuple-element.25), channel_id=1, source_target_pairs={{0,12},{1,8},{2,14},{3,10},{4,13},{5,9},{6,15},{7,11},{8,4},{9,0},... | collective-permute-start | bytes 208904 | tf_op jit(solution)/shard_map/ppermute | solution.py:365
  16.3 2.7 %collective-permute-start.4 = (bf16[1056,128]{1,0:T(8,128)(2,1)S(1)}, bf16[1056,128]{1,0:T(8,128)(2,1)S(1)}, u32[]{:S(2)}, u32[]{:S(2)}) collective-permute-start(bf16[1056,128]{1,0:T(8,128)(2,1)S(1)} %shard_map.130.refs_0_.refs_2_), channel_id=1, source_target_pairs={{0,1},{1,0},{2,3},{3,2},{4,5},{5,4},{6,7},{7,6},{8,9},{9,8},{10,11... | collective-permute-start | bytes 811016 | tf_op jit(solution)/shard_map/ppermute | solution.py:371
  16.4 3.4 %collective-permute-start.6 = (bf16[1056,128]{1,0:T(8,128)(2,1)S(1)}, bf16[1056,128]{1,0:T(8,128)(2,1)S(1)}, u32[]{:S(2)}, u32[]{:S(2)}) collective-permute-start(bf16[1056,128]{1,0:T(8,128)(2,1)S(1)} %shard_map.132.refs_4_), channel_id=1, source_target_pairs={{0,1},{1,0},{2,3},{3,2},{4,5},{5,4},{6,7},{7,6},{8,9},{9,8},{10,11... | collective-permute-start | bytes 811016 | tf_op jit(solution)/shard_map/ppermute | solution.py:371
  19.0 7.4 %copy-start = (bf16[512,2048]{1,0:T(8,128)(2,1)S(1)}, bf16[512,2048]{1,0:T(8,128)(2,1)}, u32[]{:S(2)}) copy-start(bf16[512,2048]{1,0:T(8,128)(2,1)} %w_out_ref.1) | copy-start | bytes 6291460
  19.8 17.5 %copy-start.1 = (bf16[128,2048]{1,0:T(8,128)(2,1)S(1)}, bf16[128,2048]{1,0:T(8,128)(2,1)}, u32[]{:S(2)}) copy-start(bf16[128,2048]{1,0:T(8,128)(2,1)} %refs_3_.1) | copy-start | bytes 1572868
  20.4 4.3 %collective-permute-start.7 = (bf16[272,128]{1,0:T(8,128)(2,1)S(1)}, bf16[272,128]{1,0:T(8,128)(2,1)S(1)}, u32[]{:S(2)}, u32[]{:S(2)}) collective-permute-start(bf16[272,128]{1,0:T(8,128)(2,1)S(1)} %get-tuple-element.31), channel_id=1, source_target_pairs={{4,0},{0,1},{6,2},{2,3},{5,4},{1,5},{7,6},{3,7},{12,8},{8,9},{14,1... | collective-permute-start | bytes 208904 | tf_op jit(solution)/shard_map/ppermute | solution.py:365
  20.7 5.6 %collective-permute-start.8 = (bf16[272,128]{1,0:T(8,128)(2,1)S(1)}, bf16[272,128]{1,0:T(8,128)(2,1)S(1)}, u32[]{:S(2)}, u32[]{:S(2)}) collective-permute-start(bf16[272,128]{1,0:T(8,128)(2,1)S(1)} %get-tuple-element.32), channel_id=1, source_target_pairs={{12,0},{8,1},{14,2},{10,3},{13,4},{9,5},{15,6},{11,7},{4,8},{0,9},... | collective-permute-start | bytes 208904 | tf_op jit(solution)/shard_map/ppermute | solution.py:365
  27.0 1.6 %collective-permute-start.9 = (bf16[64,2048]{1,0:T(8,128)(2,1)S(1)}, bf16[64,2048]{1,0:T(8,128)(2,1)S(1)}, u32[]{:S(2)}, u32[]{:S(2)}) collective-permute-start(bf16[64,2048]{1,0:T(8,128)(2,1)S(1)} %get-tuple-element.34), channel_id=1, source_target_pairs={{0,1},{1,0},{2,3},{3,2},{4,5},{5,4},{6,7},{7,6},{8,9},{9,8},{10,11... | collective-permute-start | bytes 786440 | tf_op jit(solution)/shard_map/ppermute | solution.py:371
  28.7 8.6 %collective-permute-start.10 = (bf16[64,2048]{1,0:T(8,128)(2,1)S(1)}, bf16[64,2048]{1,0:T(8,128)(2,1)S(1)}, u32[]{:S(2)}, u32[]{:S(2)}) collective-permute-start(bf16[64,2048]{1,0:T(8,128)(2,1)S(1)} %add_convert_fusion.1), channel_id=1, source_target_pairs={{0,2},{1,3},{2,0},{3,1},{4,6},{5,7},{6,4},{7,5},{8,10},{9,11},{10,... | collective-permute-start | bytes 786440 | tf_op jit(solution)/shard_map/ppermute | solution.py:371
  37.4 1.6 %collective-permute-start.11 = (bf16[64,2048]{1,0:T(8,128)(2,1)S(1)}, bf16[64,2048]{1,0:T(8,128)(2,1)S(1)}, u32[]{:S(2)}, u32[]{:S(2)}) collective-permute-start(bf16[64,2048]{1,0:T(8,128)(2,1)S(1)} %add_convert_fusion.half_ref), channel_id=1, source_target_pairs={{0,1},{1,0},{2,3},{3,2},{4,5},{5,4},{6,7},{7,6},{8,9},{9,8},{10,11... | collective-permute-start | bytes 786440 | tf_op jit(solution)/shard_map/ppermute | solution.py:371

commit v8 on v7

--- a/solution.py
+++ b/solution.py
@@ -11,8 +11,8 @@
 GROUPS = 4
 NOTE_ROWS = 16
 ASK_ROWS = NOTE_ROWS + 128
-W_CUTS = 4
-ROW_CUTS = 2
+W_CUTS = 2
+ROW_CUTS = 1
 
 ORDER = (1, 0)
 BACK = (0, 1)

time: 39.9 us -> 39.9 us (level)
  transfers between devices with their start and end apart: 12 -> 12, of which waited for: 6 -> 6; matrix products, arithmetic and copies ran while one was open for 0% -> 0% of each run, Pallas kernels for 18% -> 19%
where the time goes in v8:
time: 39.9 us; the launch traced here: 39.7 us
  starting transfers between devices  15.1 us (38%)
  waiting for transfers between devices  12.5 us (31%)
  Pallas kernels  10.4 us (26%)
  between operations  1.5 us (4%)
    ppermute x7, starting transfers between devices, exchange(): return lax.ppermute(x, ('blk', 'mp'), pairs)  11 us
    pallas_call x11, Pallas kernels, run(): return inner(*pinned)  10.4 us
    ppermute x5, waiting for transfers between devices, across_mp(): return lax.ppermute(x, 'mp', [(i, i ^ bit) for i in range(n_mp)])  8.93 us
    ppermute x5, starting transfers between devices, across_mp(): return lax.ppermute(x, 'mp', [(i, i ^ bit) for i in range(n_mp)])  4.15 us
    ppermute x7, waiting for transfers between devices, exchange(): return lax.ppermute(x, ('blk', 'mp'), pairs)  3.6 us
  transfers between devices with their start and end apart: 12, of which 6 were waited for; matrix products, arithmetic and copies ran while one was open for 0% of the time, Pallas kernels for 19%

profile of v8, /device:TPU:0, one launch (start us, length us, event | category | flops | bytes accessed | tf_op | source)
XLA Modules:
  0.0 39.7 jit_solution(12361107501879769304)
XLA Ops:
  1.3 1.1 %shard_map.129 = (bf16[528,128]{1,0:T(8,128)(2,1)S(1)}, bf16[528,128]{1,0:T(8,128)(2,1)S(1)}, bf16[528,128]{1,0:T(8,128)(2,1)S(1)}) custom-call(bf16[1,128,512]{2,1,0:T(8,128)(2,1)} %keys_ref.1, bf16[1,128,512]{2,1,0:T(8,128)(2,1)} %values_ref.1, bf16[16,128]{1,0:T(8,128)(2,1)S(1)} %broadcast_in_dim.4.refs_2_.tag_ref), custom_call_target="tpu_custom_call" | custom-call | flops 1000000 | bytes 1 | tf_op jit(solution)/shard_map/pallas_call | solution.py:316
  2.4 5.0 %collective-permute-start.2 = (bf16[528,128]{1,0:T(8,128)(2,1)S(1)}, bf16[528,128]{1,0:T(8,128)(2,1)S(1)}, u32[]{:S(2)}, u32[]{:S(2)}) collective-permute-start(bf16[528,128]{1,0:T(8,128)(2,1)S(1)} %get-tuple-element.26), channel_id=1, source_target_pairs={{0,20},{1,16},{2,22},{3,18},{4,21},{5,17},{6,23},{7,19},{8,28},{9,... | collective-permute-start | bytes 405512 | tf_op jit(solution)/shard_map/ppermute | solution.py:365
  7.4 1.0 %collective-permute-start.3 = (bf16[528,128]{1,0:T(8,128)(2,1)S(1)}, bf16[528,128]{1,0:T(8,128)(2,1)S(1)}, u32[]{:S(2)}, u32[]{:S(2)}) collective-permute-start(bf16[528,128]{1,0:T(8,128)(2,1)S(1)} %get-tuple-element.27), channel_id=1, source_target_pairs={{0,12},{1,8},{2,14},{3,10},{4,13},{5,9},{6,15},{7,11},{8,4},{9,0},... | collective-permute-start | bytes 405512 | tf_op jit(solution)/shard_map/ppermute | solution.py:365
  8.5 0.1 collective-permute-start.5
  8.6 2.3 %shard_map.127 = (bf16[128,2048]{1,0:T(8,128)(2,1)S(1)}, bf16[128,512]{1,0:T(8,128)(2,1)S(1)}, bf16[784,128]{1,0:T(8,128)(2,1)S(1)}, bf16[272,128]{1,0:T(8,128)(2,1)S(1)}) custom-call(bf16[1,128,512]{2,1,0:T(8,128)(2,1)} %keys_ref.1, bf16[1,128,512]{2,1,0:T(8,128)(2,1)} %values_ref.1, bf16[16,128]{1,0:T(8,128)(2,1)S(1)} %broadcast_in_dim.4.refs_2_.tag_ref, ...), custom_call_target="tpu_custom_call" | custom-call | flops 1000000 | bytes 1 | tf_op jit(solution)/shard_map/pallas_call | solution.py:316
  11.0 0.1 collective-permute-start
  11.1 1.9 %collective-permute-start.1 = (bf16[272,128]{1,0:T(8,128)(2,1)S(1)}, bf16[272,128]{1,0:T(8,128)(2,1)S(1)}, u32[]{:S(2)}, u32[]{:S(2)}) collective-permute-start(bf16[272,128]{1,0:T(8,128)(2,1)S(1)} %get-tuple-element.25), channel_id=1, source_target_pairs={{0,12},{1,8},{2,14},{3,10},{4,13},{5,9},{6,15},{7,11},{8,4},{9,0},... | collective-permute-start | bytes 208904 | tf_op jit(solution)/shard_map/ppermute | solution.py:365
  13.0 3.5 %shard_map.128 = (f32[512,128]{1,0:T(8,128)S(1)}, f32[8,128]{1,0:T(8,128)S(1)}) custom-call(bf16[128,2048]{1,0:T(8,128)(2,1)S(1)} %get-tuple-element.20.normed_ref, bf16[128,512]{1,0:T(8,128)(2,1)S(1)} %get-tuple-element.21.query_ref, s32[1,128]{1,0:T(1,128)} %refs_0_.3, bf16[2048,512]{1,0:T(8,128)(2,1)} %refs_1_.3, bf16[2048,512]{1,0:T(8,128)(2,1)} %refs_2_.1), custom_call_target="tpu_custom_call" | custom-call | flops 1000000 | bytes 1 | tf_op jit(solution)/shard_map/pallas_call | solution.py:316
  16.5 0.0 collective-permute-done.2.refs_0_
  16.5 0.0 collective-permute-done.3.refs_1_
  16.5 0.1 collective-permute-start.4
  16.6 0.0 collective-permute-done.5.refs_1_.far_ref
  16.6 0.0 collective-permute-done.ask_ref.refs_0_
  16.7 1.9 %collective-permute-start.6 = (bf16[1056,128]{1,0:T(8,128)(2,1)S(1)}, bf16[1056,128]{1,0:T(8,128)(2,1)S(1)}, u32[]{:S(2)}, u32[]{:S(2)}) collective-permute-start(bf16[1056,128]{1,0:T(8,128)(2,1)S(1)} %shard_map.132.refs_4_), channel_id=1, source_target_pairs={{0,1},{1,0},{2,3},{3,2},{4,5},{5,4},{6,7},{7,6},{8,9},{9,8},{10,11... | collective-permute-start | bytes 811016 | tf_op jit(solution)/shard_map/ppermute | solution.py:371
  18.6 0.4 collective-permute-done.1.refs_1_
  19.0 0.0 collective-permute-done.4.refs_3_
  19.0 0.0 copy-start
  19.0 0.8 %shard_map.133 = (f32[8,512]{1,0:T(8,128)S(1)}, f32[128,512]{1,0:T(8,128)S(1)}) custom-call(bf16[784,128]{1,0:T(8,128)(2,1)S(1)} %collective-permute-done.ask_ref.refs_0_, bf16[272,128]{1,0:T(8,128)(2,1)S(1)} %collective-permute-done.1.refs_1_, bf16[1056,128]{1,0:T(8,128)(2,1)S(1)} %shard_map.130.refs_0_.refs_2_, ...), custom_call_target="tpu_custom_call" | custom-call | flops 30000001024 | bytes 1 | tf_op jit(solution)/shard_map/pallas_call | solution.py:316
  19.8 0.0 collective-permute-done.6.refs_4_
  19.8 0.0 copy-start.1
  19.8 0.5 %shard_map.134 = (bf16[272,128]{1,0:T(8,128)(2,1)S(1)}, bf16[272,128]{1,0:T(8,128)(2,1)S(1)}) custom-call(bf16[784,128]{1,0:T(8,128)(2,1)S(1)} %collective-permute-done.ask_ref.refs_0_, bf16[272,128]{1,0:T(8,128)(2,1)S(1)} %collective-permute-done.1.refs_1_, f32[8,512]{1,0:T(8,128)S(1)} %get-tuple-element.29.refs_2_, ...), custom_call_target="tpu_custom_call" | custom-call | flops 1000000 | bytes 1 | tf_op jit(solution)/shard_map/pallas_call | solution.py:316
  20.4 0.3 collective-permute-start.7
  20.7 2.4 %collective-permute-start.8 = (bf16[272,128]{1,0:T(8,128)(2,1)S(1)}, bf16[272,128]{1,0:T(8,128)(2,1)S(1)}, u32[]{:S(2)}, u32[]{:S(2)}) collective-permute-start(bf16[272,128]{1,0:T(8,128)(2,1)S(1)} %get-tuple-element.32), channel_id=1, source_target_pairs={{12,0},{8,1},{14,2},{10,3},{13,4},{9,5},{15,6},{11,7},{4,8},{0,9},... | collective-permute-start | bytes 208904 | tf_op jit(solution)/shard_map/ppermute | solution.py:365
  23.1 1.6 %collective-permute-done.7.refs_0_ = bf16[272,128]{1,0:T(8,128)(2,1)S(1)} collective-permute-done((bf16[272,128]{1,0:T(8,128)(2,1)S(1)}, bf16[272,128]{1,0:T(8,128)(2,1)S(1)}, u32[]{:S(2)}, u32[]{:S(2)}) %collective-permute-start.7) | collective-permute-done | bytes 69664 | tf_op jit(solution)/shard_map/ppermute | solution.py:365
  24.7 1.6 %collective-permute-done.8.refs_1_ = bf16[272,128]{1,0:T(8,128)(2,1)S(1)} collective-permute-done((bf16[272,128]{1,0:T(8,128)(2,1)S(1)}, bf16[272,128]{1,0:T(8,128)(2,1)S(1)}, u32[]{:S(2)}, u32[]{:S(2)}) %collective-permute-start.8) | collective-permute-done | bytes 69664 | tf_op jit(solution)/shard_map/ppermute | solution.py:365
  26.3 0.0 copy-done
  26.3 0.7 %shard_map.135 = (f32[64,2048]{1,0:T(8,128)S(1)}, bf16[64,2048]{1,0:T(8,128)(2,1)S(1)}) custom-call(f32[512,128]{1,0:T(8,128)S(1)} %get-tuple-element.22.sum_ref, f32[8,128]{1,0:T(8,128)S(1)} %get-tuple-element.23._.log_ref, bf16[512,2048]{1,0:T(8,128)(2,1)S(1)} %copy-done, bf16[272,128]{1,0:T(8,128)(2,1)S(1)} %collective-permute-done.7.refs_0_, ...), custom_call_target="tpu_custom_call" | custom-call | flops 1000000 | bytes 1 | tf_op jit(solution)/shard_map/pallas_call | solution.py:316
  27.0 0.1 collective-permute-start.9
  27.1 1.5 %collective-permute-done.9 = bf16[64,2048]{1,0:T(8,128)(2,1)S(1)} collective-permute-done((bf16[64,2048]{1,0:T(8,128)(2,1)S(1)}, bf16[64,2048]{1,0:T(8,128)(2,1)S(1)}, u32[]{:S(2)}, u32[]{:S(2)}) %collective-permute-start.9) | collective-permute-done | bytes 262176 | tf_op jit(solution)/shard_map/ppermute | solution.py:371
  28.7 2.0 %collective-permute-start.10 = (bf16[64,2048]{1,0:T(8,128)(2,1)S(1)}, bf16[64,2048]{1,0:T(8,128)(2,1)S(1)}, u32[]{:S(2)}, u32[]{:S(2)}) collective-permute-start(bf16[64,2048]{1,0:T(8,128)(2,1)S(1)} %add_convert_fusion.1), channel_id=1, source_target_pairs={{0,2},{1,3},{2,0},{3,1},{4,6},{5,7},{6,4},{7,5},{8,10},{9,11},{10,... | collective-permute-start | bytes 786440 | tf_op jit(solution)/shard_map/ppermute | solution.py:371
  30.7 6.6 %collective-permute-done.10 = bf16[64,2048]{1,0:T(8,128)(2,1)S(1)} collective-permute-done((bf16[64,2048]{1,0:T(8,128)(2,1)S(1)}, bf16[64,2048]{1,0:T(8,128)(2,1)S(1)}, u32[]{:S(2)}, u32[]{:S(2)}) %collective-permute-start.10) | collective-permute-done | bytes 262176 | tf_op jit(solution)/shard_map/ppermute | solution.py:371
  37.3 0.0 copy-done.1
  37.3 0.1 add_convert_fusion.half_ref
  37.4 0.1 collective-permute-start.11
  37.5 0.7 %shard_map.136._ = bf16[128,2048]{1,0:T(8,128)(2,1)} custom-call(bf16[64,2048]{1,0:T(8,128)(2,1)S(1)} %add_convert_fusion.half_ref), custom_call_target="tpu_custom_call" | custom-call | flops 1000000 | bytes 1 | tf_op jit(solution)/shard_map/pallas_call | solution.py:316
  38.2 0.8 %collective-permute-done.11.half_ref = bf16[64,2048]{1,0:T(8,128)(2,1)S(1)} collective-permute-done((bf16[64,2048]{1,0:T(8,128)(2,1)S(1)}, bf16[64,2048]{1,0:T(8,128)(2,1)S(1)}, u32[]{:S(2)}, u32[]{:S(2)}) %collective-permute-start.11) | collective-permute-done | bytes 262176 | tf_op jit(solution)/shard_map/ppermute | solution.py:371
  39.0 0.7 %shard_map.137 = bf16[128,2048]{1,0:T(8,128)(2,1)} custom-call(bf16[64,2048]{1,0:T(8,128)(2,1)S(1)} %collective-permute-done.11.half_ref, bf16[128,2048]{1,0:T(8,128)(2,1)} %shard_map.136._), custom_call_target="tpu_custom_call", output_to_operand_aliasing={{}: (1, {})} | custom-call | flops 1000000 | bytes 1 | tf_op jit(solution)/shard_map/pallas_call | solution.py:316
  (5 shorter events, 0.1 us)
Async XLA Ops:
  2.4 14.1 %collective-permute-start.2 = (bf16[528,128]{1,0:T(8,128)(2,1)S(1)}, bf16[528,128]{1,0:T(8,128)(2,1)S(1)}, u32[]{:S(2)}, u32[]{:S(2)}) collective-permute-start(bf16[528,128]{1,0:T(8,128)(2,1)S(1)} %get-tuple-element.26), channel_id=1, source_target_pairs={{0,20},{1,16},{2,22},{3,18},{4,21},{5,17},{6,23},{7,19},{8,28},{9,... | collective-permute-start | bytes 405512 | tf_op jit(solution)/shard_map/ppermute | solution.py:365
  7.4 9.1 %collective-permute-start.3 = (bf16[528,128]{1,0:T(8,128)(2,1)S(1)}, bf16[528,128]{1,0:T(8,128)(2,1)S(1)}, u32[]{:S(2)}, u32[]{:S(2)}) collective-permute-start(bf16[528,128]{1,0:T(8,128)(2,1)S(1)} %get-tuple-element.27), channel_id=1, source_target_pairs={{0,12},{1,8},{2,14},{3,10},{4,13},{5,9},{6,15},{7,11},{8,4},{9,0},... | collective-permute-start | bytes 405512 | tf_op jit(solution)/shard_map/ppermute | solution.py:365
  8.5 8.2 %collective-permute-start.5 = (bf16[528,128]{1,0:T(8,128)(2,1)S(1)}, bf16[528,128]{1,0:T(8,128)(2,1)S(1)}, u32[]{:S(2)}, u32[]{:S(2)}) collective-permute-start(bf16[528,128]{1,0:T(8,128)(2,1)S(1)} %get-tuple-element.28), channel_id=1, source_target_pairs={{0,28},{1,24},{2,30},{3,26},{4,29},{5,25},{6,31},{7,27},{8,20},{9,... | collective-permute-start | bytes 405512 | tf_op jit(solution)/shard_map/ppermute | solution.py:365
  11.0 5.7 %collective-permute-start = (bf16[784,128]{1,0:T(8,128)(2,1)S(1)}, bf16[784,128]{1,0:T(8,128)(2,1)S(1)}, u32[]{:S(2)}, u32[]{:S(2)}) collective-permute-start(bf16[784,128]{1,0:T(8,128)(2,1)S(1)} %get-tuple-element.24), channel_id=1, source_target_pairs={{0,4},{1,0},{2,6},{3,2},{4,5},{5,1},{6,7},{7,3},{8,12},{9,8},{10,1... | collective-permute-start | bytes 602120 | tf_op jit(solution)/shard_map/ppermute | solution.py:365
  11.1 7.9 %collective-permute-start.1 = (bf16[272,128]{1,0:T(8,128)(2,1)S(1)}, bf16[272,128]{1,0:T(8,128)(2,1)S(1)}, u32[]{:S(2)}, u32[]{:S(2)}) collective-permute-start(bf16[272,128]{1,0:T(8,128)(2,1)S(1)} %get-tuple-element.25), channel_id=1, source_target_pairs={{0,12},{1,8},{2,14},{3,10},{4,13},{5,9},{6,15},{7,11},{8,4},{9,0},... | collective-permute-start | bytes 208904 | tf_op jit(solution)/shard_map/ppermute | solution.py:365
  16.5 2.4 %collective-permute-start.4 = (bf16[1056,128]{1,0:T(8,128)(2,1)S(1)}, bf16[1056,128]{1,0:T(8,128)(2,1)S(1)}, u32[]{:S(2)}, u32[]{:S(2)}) collective-permute-start(bf16[1056,128]{1,0:T(8,128)(2,1)S(1)} %shard_map.130.refs_0_.refs_2_), channel_id=1, source_target_pairs={{0,1},{1,0},{2,3},{3,2},{4,5},{5,4},{6,7},{7,6},{8,9},{9,8},{10,11... | collective-permute-start | bytes 811016 | tf_op jit(solution)/shard_map/ppermute | solution.py:371
  16.7 3.1 %collective-permute-start.6 = (bf16[1056,128]{1,0:T(8,128)(2,1)S(1)}, bf16[1056,128]{1,0:T(8,128)(2,1)S(1)}, u32[]{:S(2)}, u32[]{:S(2)}) collective-permute-start(bf16[1056,128]{1,0:T(8,128)(2,1)S(1)} %shard_map.132.refs_4_), channel_id=1, source_target_pairs={{0,1},{1,0},{2,3},{3,2},{4,5},{5,4},{6,7},{7,6},{8,9},{9,8},{10,11... | collective-permute-start | bytes 811016 | tf_op jit(solution)/shard_map/ppermute | solution.py:371
  19.0 7.4 %copy-start = (bf16[512,2048]{1,0:T(8,128)(2,1)S(1)}, bf16[512,2048]{1,0:T(8,128)(2,1)}, u32[]{:S(2)}) copy-start(bf16[512,2048]{1,0:T(8,128)(2,1)} %w_out_ref.1) | copy-start | bytes 6291460
  19.8 17.5 %copy-start.1 = (bf16[128,2048]{1,0:T(8,128)(2,1)S(1)}, bf16[128,2048]{1,0:T(8,128)(2,1)}, u32[]{:S(2)}) copy-start(bf16[128,2048]{1,0:T(8,128)(2,1)} %refs_3_.1) | copy-start | bytes 1572868
  20.4 4.3 %collective-permute-start.7 = (bf16[272,128]{1,0:T(8,128)(2,1)S(1)}, bf16[272,128]{1,0:T(8,128)(2,1)S(1)}, u32[]{:S(2)}, u32[]{:S(2)}) collective-permute-start(bf16[272,128]{1,0:T(8,128)(2,1)S(1)} %get-tuple-element.31), channel_id=1, source_target_pairs={{4,0},{0,1},{6,2},{2,3},{5,4},{1,5},{7,6},{3,7},{12,8},{8,9},{14,1... | collective-permute-start | bytes 208904 | tf_op jit(solution)/shard_map/ppermute | solution.py:365
  20.7 5.6 %collective-permute-start.8 = (bf16[272,128]{1,0:T(8,128)(2,1)S(1)}, bf16[272,128]{1,0:T(8,128)(2,1)S(1)}, u32[]{:S(2)}, u32[]{:S(2)}) collective-permute-start(bf16[272,128]{1,0:T(8,128)(2,1)S(1)} %get-tuple-element.32), channel_id=1, source_target_pairs={{12,0},{8,1},{14,2},{10,3},{13,4},{9,5},{15,6},{11,7},{4,8},{0,9},... | collective-permute-start | bytes 208904 | tf_op jit(solution)/shard_map/ppermute | solution.py:365
  27.0 1.6 %collective-permute-start.9 = (bf16[64,2048]{1,0:T(8,128)(2,1)S(1)}, bf16[64,2048]{1,0:T(8,128)(2,1)S(1)}, u32[]{:S(2)}, u32[]{:S(2)}) collective-permute-start(bf16[64,2048]{1,0:T(8,128)(2,1)S(1)} %get-tuple-element.34), channel_id=1, source_target_pairs={{0,1},{1,0},{2,3},{3,2},{4,5},{5,4},{6,7},{7,6},{8,9},{9,8},{10,11... | collective-permute-start | bytes 786440 | tf_op jit(solution)/shard_map/ppermute | solution.py:371
  28.7 8.6 %collective-permute-start.10 = (bf16[64,2048]{1,0:T(8,128)(2,1)S(1)}, bf16[64,2048]{1,0:T(8,128)(2,1)S(1)}, u32[]{:S(2)}, u32[]{:S(2)}) collective-permute-start(bf16[64,2048]{1,0:T(8,128)(2,1)S(1)} %add_convert_fusion.1), channel_id=1, source_target_pairs={{0,2},{1,3},{2,0},{3,1},{4,6},{5,7},{6,4},{7,5},{8,10},{9,11},{10,... | collective-permute-start | bytes 786440 | tf_op jit(solution)/shard_map/ppermute | solution.py:371
  37.4 1.6 %collective-permute-start.11 = (bf16[64,2048]{1,0:T(8,128)(2,1)S(1)}, bf16[64,2048]{1,0:T(8,128)(2,1)S(1)}, u32[]{:S(2)}, u32[]{:S(2)}) collective-permute-start(bf16[64,2048]{1,0:T(8,128)(2,1)S(1)} %add_convert_fusion.half_ref), channel_id=1, source_target_pairs={{0,1},{1,0},{2,3},{3,2},{4,5},{5,4},{6,7},{7,6},{8,9},{9,8},{10,11... | collective-permute-start | bytes 786440 | tf_op jit(solution)/shard_map/ppermute | solution.py:371
